TPU v7x, 32 devices: a whole 2x2x4 slice. The times are simulated.
32 devices in a mesh: kv: 4 (over y, x), wide: 8 (over z, core).
Axes of the slice: x: 2, y: 2, z: 4, core: 2. Of those that a mesh axis runs over, the one named last changes fastest.
Arguments:
- stream_in: bfloat16 [16, 4, 2560], P('wide', None, 'kv'), may hold values from -8 to 8
- queries: bfloat16 [16, 4, 2560], P('wide', None, 'kv'), may hold values from -2.5 to 2.5
- new_kv: bfloat16 [16, 4, 2, 512], P('wide', None, None, 'kv'), may hold values from -2.5 to 2.5
- cache_keys: bfloat16 [4, 128, 128, 128], P('kv', 'wide'), may hold values from -2.5 to 2.5
- cache_values: bfloat16 [4, 128, 128, 128], P('kv', 'wide'), may hold values from -2.5 to 2.5
- lengths: int32 [2], replicated, may hold values from 1 to 4096, as said below
- page_table: int32 [2, 32], replicated, may hold values from -1 to 127, as said below
- parents: int32 [16, 3], replicated, may hold values from 0 to 7
- routes: int32 [16, 4, 6], P('wide'), may hold values from 0 to 63, all different within a row; in each aligned block of 8 rows (0 to 7, 8 to 15, ..., all dimensions but the last counted through in order) at most 2 rows name the same one
- norm_gain: float32 [2560], replicated, may hold values from 0.5 to 1.5
- router: bfloat16 [2560, 64], replicated, may hold values from -0.01965332 to 0.01965332
- gate_w: bfloat16 [128, 2560, 768], P('wide', None, 'kv'), may hold values from -0.125 to 0.125
- up_w: bfloat16 [128, 2560, 768], P('wide', None, 'kv'), may hold values from -0.125 to 0.125
- down_w: bfloat16 [128, 768, 2560], P('wide', 'kv'), may hold values from -0.15625 to 0.15625
Outputs:
- stream_out: bfloat16 [16, 4, 2560], P('wide', None, 'kv')
Inputs may be any that keep to these rules, and one draw needn't show every extreme that they name: `lengths`: one group has exactly 4096 positions. `page_table`: entry [g, b] is the slot (index of wide times 16 plus the local slot) holding positions b * 128 to b * 128 + 127 of group g when b * 128 < lengths[g], and -1 otherwise; no slot is named twice; every slot of some index of wide is named. `parents`: entry [t, j] is a beam of t's own group. `routes`: within the rows of one index of wide (2 beams times 4 steps) no expert is named by more than 2 rows.
All inputs are finite; a program needn't handle non-finite values.
Results may differ from a plain program's by a relative error of at most 0.012.
Values may be sent and summed in bfloat16 or wider, within the bound.
No kernel may reach another device: no remote copies, remote signals or barrier semaphores. Data moves between devices by JAX's collectives and lax.ppermute only.
A program may use at most 128 MiB of HBM per device.

v0:
```python
import math

import jax
import jax.numpy as jnp
from jax import lax
from jax.sharding import PartitionSpec as P

D = 2560
HD = 128
E = 64
TOP = 6
BEAMS = 8
BLK = 128
MOST = 2


def chain_tokens(parents, token_count, steps):
    tokens = jnp.arange(token_count, dtype=jnp.int32)
    group_base = tokens // BEAMS * BEAMS
    chain_table = []
    for step_now in range(steps):
        columns = [tokens] * steps
        current = tokens
        for earlier in range(step_now, 0, -1):
            current = group_base + parents[current, earlier - 1]
            columns[earlier - 1] = current
        chain_table.append(jnp.stack(columns, axis=1))
    return jnp.stack(chain_table, axis=1)


def local(
    stream_in,
    queries,
    new_kv,
    cache_keys,
    cache_values,
    lengths,
    page_table,
    parents,
    routes,
    norm_gain,
    router,
    gate_w,
    up_w,
    down_w,
):
    wide_index = lax.axis_index("wide")
    wide_count = lax.axis_size("wide")
    step_tok = stream_in.shape[0]
    steps = stream_in.shape[1]
    kv_local = new_kv.shape[3] // HD
    q_local = queries.shape[2] // HD
    head_ratio = q_local // kv_local
    groups = lengths.shape[0]
    token_count = groups * BEAMS
    slots_local = cache_keys.shape[1]
    score_scale = 1.0 / math.sqrt(HD)
    all_queries, all_kv = (
        lax.all_gather(queries, "wide", axis=0, tiled=True),
        lax.all_gather(new_kv, "wide", axis=0, tiled=True),
    )
    slot_ids = wide_index * slots_local + jnp.arange(slots_local, dtype=jnp.int32)
    slot_hits = page_table[None, :, :] == slot_ids[:, None, None]
    group_ids = jnp.arange(groups, dtype=jnp.int32)
    block_starts = jnp.arange(page_table.shape[1], dtype=jnp.int32) * BLK
    owner_group = jnp.sum(jnp.where(slot_hits, group_ids[None, :, None], 0), axis=(1, 2))
    slot_live = jnp.any(slot_hits, axis=(1, 2))
    block_limit = jnp.sum(
        jnp.where(slot_hits, lengths[None, :, None] - block_starts[None, None, :], 0), axis=(1, 2)
    )
    key_ok = (jnp.arange(BLK, dtype=jnp.int32)[None, :] < block_limit[:, None]).astype(jnp.float32)
    grouped = all_queries.reshape(groups, BEAMS, steps, kv_local, head_ratio, HD)
    picked = grouped[owner_group]
    scores = jnp.einsum(
        "nbskrd,knpd->nbskrp", picked, cache_keys, preferred_element_type=jnp.float32
    )
    weights = jnp.exp(scores * score_scale) * key_ok[:, None, None, None, None, :]
    rounded = weights.astype(jnp.bfloat16)
    numerator = jnp.einsum(
        "nbskrp,knpd->nbskrd", rounded, cache_values, preferred_element_type=jnp.float32
    )
    denominator = jnp.sum(rounded.astype(jnp.float32), axis=-1)
    onehot = ((owner_group[None, :] == group_ids[:, None]) & slot_live[None, :]).astype(jnp.float32)
    part_num = jnp.einsum("gn,nbskrd->gbskrd", onehot, numerator, precision=lax.Precision.HIGHEST)
    part_den = jnp.einsum("gn,nbskr->gbskr", onehot, denominator, precision=lax.Precision.HIGHEST)
    part_num = part_num.reshape(token_count, steps, q_local * HD)
    part_den = part_den.reshape(token_count, steps, q_local)
    first_token = wide_index * step_tok
    full_num, full_den = lax.psum((part_num, part_den), "wide")
    mine_num = lax.dynamic_slice_in_dim(full_num, first_token, step_tok, 0)
    mine_den = lax.dynamic_slice_in_dim(full_den, first_token, step_tok, 0)
    chains = chain_tokens(parents, token_count, steps)
    my_chain = lax.dynamic_slice_in_dim(chains, first_token, step_tok, 0)
    group_first = first_token // BEAMS * BEAMS
    local_chain = my_chain - group_first
    group_kv = lax.dynamic_slice_in_dim(all_kv, group_first, BEAMS, 0)
    history = group_kv[local_chain, jnp.arange(steps, dtype=jnp.int32)[None, None, :]]
    tail_keys = history[:, :, :, 0].reshape(step_tok, steps, steps, kv_local, HD)
    tail_values = history[:, :, :, 1].reshape(step_tok, steps, steps, kv_local, HD)
    own_queries = queries.reshape(step_tok, steps, kv_local, head_ratio, HD)
    tail_scores = jnp.einsum(
        "iskrd,isjkd->iskrj", own_queries, tail_keys, preferred_element_type=jnp.float32
    )
    causal = (jnp.arange(steps)[None, :] <= jnp.arange(steps)[:, None]).astype(jnp.float32)
    tail_weights = (jnp.exp(tail_scores * score_scale) * causal[None, :, None, None, :]).astype(
        jnp.bfloat16
    )
    tail_num = jnp.einsum(
        "iskrj,isjkd->iskrd", tail_weights, tail_values, preferred_element_type=jnp.float32
    )
    tail_den = jnp.sum(tail_weights.astype(jnp.float32), axis=-1)
    numer_all = mine_num.reshape(step_tok, steps, kv_local, head_ratio, HD) + tail_num
    denom_all = mine_den.reshape(step_tok, steps, kv_local, head_ratio) + tail_den
    attended = (
        (numer_all / denom_all[..., None])
        .astype(jnp.bfloat16)
        .reshape(step_tok, steps, q_local * HD)
    )
    residual = (stream_in.astype(jnp.float32) + attended.astype(jnp.float32)).astype(jnp.bfloat16)
    row_count = step_tok * steps
    full_rows = lax.all_gather(residual, "kv", axis=2, tiled=True)
    token_rows = full_rows.reshape(row_count, D).astype(jnp.float32)
    mean_square = jnp.mean(token_rows * token_rows, axis=1, keepdims=True)
    normed = (token_rows * lax.rsqrt(mean_square + 1e-06) * norm_gain[None, :]).astype(jnp.bfloat16)
    logits = jnp.dot(normed, router, preferred_element_type=jnp.float32)
    routed = routes.reshape(row_count, TOP)
    expert_ids = jnp.arange(E, dtype=jnp.int32)
    chosen = jnp.sum(
        jnp.where(routed[:, :, None] == expert_ids[None, None, :], logits[:, None, :], 0.0), axis=2
    )
    raised = jnp.exp(chosen)
    gate_share = raised / jnp.sum(raised, axis=1, keepdims=True)
    flat_routes = routed.reshape(-1)
    expert_hot = (flat_routes[:, None] == expert_ids[None, :]).astype(jnp.int32)
    before = jnp.cumsum(expert_hot, axis=0) - expert_hot
    place_in = jnp.sum(before * expert_hot, axis=1)
    row_of = jnp.arange(row_count * TOP, dtype=jnp.int32) // TOP
    slot_match = (expert_hot[:, :, None] == 1) & (
        place_in[:, None, None] == jnp.arange(MOST, dtype=jnp.int32)[None, None, :]
    )
    source_row = jnp.sum(jnp.where(slot_match, row_of[:, None, None] + 1, 0), axis=0) - 1
    source_row = jnp.where(source_row < 0, row_count, source_row)
    half_rows = jnp.repeat(source_row, 2, axis=0)
    row_width = normed.shape[1]
    padded = jnp.concatenate([normed, jnp.zeros((1, row_width), jnp.bfloat16)], axis=0)
    halves_local = gate_w.shape[0]
    outgoing = padded[half_rows].reshape(wide_count, halves_local, MOST, row_width)
    arrived_rows = lax.all_to_all(outgoing, "wide", split_axis=0, concat_axis=0, tiled=True)
    gate_out = jnp.einsum(
        "slmd,ldf->slmf", arrived_rows, gate_w, preferred_element_type=jnp.float32
    )
    up_out = jnp.einsum("slmd,ldf->slmf", arrived_rows, up_w, preferred_element_type=jnp.float32)
    hidden = (jax.nn.silu(gate_out) * up_out).astype(jnp.bfloat16)
    partial_value = jnp.einsum("slmf,lfd->slmd", hidden, down_w, preferred_element_type=jnp.float32)
    returned = lax.all_to_all(
        partial_value.astype(jnp.bfloat16), "wide", split_axis=0, concat_axis=0, tiled=True
    ).astype(partial_value.dtype)
    out_width = returned.shape[-1]
    per_expert = returned.reshape(E, 2, MOST, out_width).sum(axis=1).reshape(E * MOST, out_width)
    per_route = per_expert[flat_routes * MOST + place_in] * gate_share.reshape(-1)[:, None]
    combined = (
        per_route.reshape(row_count, TOP, out_width).sum(axis=1).reshape(step_tok, steps, out_width)
    )
    moe_part = lax.psum_scatter(
        combined.astype(jnp.bfloat16), "kv", scatter_dimension=2, tiled=True
    ).astype(jnp.float32)
    return (residual.astype(jnp.float32) + moe_part).astype(jnp.bfloat16)


def solution(mesh):
    return jax.shard_map(
        local,
        mesh=mesh,
        in_specs=(
            P("wide", None, "kv"),
            P("wide", None, "kv"),
            P("wide", None, None, "kv"),
            P("kv", "wide", None, None),
            P("kv", "wide", None, None),
            P(),
            P(),
            P(),
            P("wide", None, None),
            P(),
            P(),
            P("wide", None, "kv"),
            P("wide", None, "kv"),
            P("wide", "kv", None),
        ),
        out_specs=P("wide", None, "kv"),
        check_vma=False,
    )
```

profile of v0, /device:TPU:0, one launch (start us, length us, event | category | flops | bytes accessed | tf_op | source)
XLA Modules:
  0.0 230.9 jit_solution(2587542454132136699)
XLA Ops:
  6.5 0.9 compare_reduce_fusion
  7.5 0.7 broadcast_subtract_fusion
  8.2 0.9 fusion.49
  9.1 15.8 %all_gather.9 = bf16[16,4,640]{2,1,0:T(4,128)(2,1)S(1)} all-gather(bf16[2,4,640]{2,1,0:T(4,128)(2,1)} %param.15), channel_id=1, replica_groups=mesh['kv'=4,'wide'=8] {'wide'}, dimensions={0}, use_global_device_ids=true | all-gather | bytes 92160 | tf_op jit(solution)/shard_map/all_gather | solution.py:59
  27.2 1.3 fusion.16
  28.5 0.7 reshape.476
  29.4 0.7 gather_fusion.2
  30.1 0.7 gather_fusion.4
  30.8 0.7 gather_fusion.1
  31.5 0.7 gather_fusion.3
  32.3 0.7 gather_fusion.5
  33.0 0.7 gather_fusion.6
  34.0 14.0 %all_gather.10 = bf16[16,4,2,128]{3,1,2,0:T(4,128)(2,1)S(1)} all-gather(bf16[2,4,2,128]{3,1,2,0:T(4,128)(2,1)S(1)} %copy.61), channel_id=1, replica_groups=mesh['kv'=4,'wide'=8] {'wide'}, dimensions={0}, use_global_device_ids=true | all-gather | bytes 36864 | tf_op jit(solution)/shard_map/all_gather | solution.py:60
  49.9 29.1 %psum.15 = f32[16,4,5]{2,1,0:T(4,128)S(1)} all-reduce(f32[16,4,5]{2,1,0:T(4,128)S(1)} %bitcast.149), channel_id=1, replica_groups=mesh['kv'=4,'wide'=8] {'wide'}, use_global_device_ids=true, to_apply=%region_5.6 | all-reduce | flops 320 | bytes 2560 | tf_op jit(solution)/shard_map/psum | solution.py:89
  79.1 3.5 %all-reduce.6.cloned.1.call-done = f32[16,4,640]{2,0,1:T(8,128)} async-done(((f32[16,4,640]{2,0,1:T(8,128)}), f32[16,4,640]{2,0,1:T(8,128)}) %all-reduce.6.cloned.1.call-update) | async-done | bytes 163856 | tf_op jit(solution)/shard_map/psum | solution.py:89
  82.7 0.9 constant_dynamic-slice_fusion.1
  83.8 8.2 %all_gather.11 = bf16[2,4,2560]{2,1,0:T(4,128)(2,1)S(1)} all-gather(bf16[2,4,640]{2,1,0:T(4,128)(2,1)S(1)} %add_convert_fusion.1), channel_id=1, replica_groups=mesh['kv'=4,'wide'=8] {'kv'}, dimensions={2}, use_global_device_ids=true | all-gather | bytes 51200 | tf_op jit(solution)/shard_map/all_gather | solution.py:121
  92.3 1.4 gather_fusion.8
  94.3 37.3 %all_to_all.10 = bf16[8,16,2,2560]{3,2,1,0:T(2,128)(2,1)S(1)} all-to-all(bf16[8,16,2,2560]{3,2,1,0:T(2,128)(2,1)S(1)} %reshape.483), channel_id=1, replica_groups=mesh['kv'=4,'wide'=8] {'wide'}, dimensions={0} | all-to-all | bytes 2621440 | tf_op jit(solution)/shard_map/all_to_all | solution.py:148
  131.6 7.6 %fusion.18 = f32[8,16,2,192]{3,0,2,1:T(8,128)S(1)} fusion(bf16[16,2560,192]{1,2,0:T(8,128)(2,1)} %param.25, bf16[8,16,2,2560]{3,2,1,0:T(2,128)(2,1)S(1)} %all_to_all.10), kind=kOutput, calls=%fused_computation.27 | convolution fusion | flops 251658240 | bytes 17235968 | tf_op jit(solution)/shard_map/slmd,ldf->slmf/dot_general | solution.py:149
  139.2 7.7 %fusion.29 = bf16[8,16,2,192]{3,0,2,1:T(8,128)(2,1)S(1)} fusion(bf16[16,2560,192]{1,2,0:T(8,128)(2,1)} %param.26, bf16[8,16,2,2560]{3,2,1,0:T(2,128)(2,1)S(1)} %all_to_all.10, f32[8,16,2,192]{3,0,2,1:T(8,128)S(1)} %fusion.18), kind=kOutput, calls=%fused_computation.32 | convolution fusion | flops 251953152 | bytes 17334272 | tf_op jit(solution)/shard_map/slmd,ldf->slmf/dot_general | solution.py:152
  146.9 7.6 %fusion.9 = bf16[8,16,2,2560]{3,0,2,1:T(8,128)(2,1)S(1)} fusion(bf16[8,16,2,192]{3,0,2,1:T(8,128)(2,1)S(1)} %fusion.29, bf16[16,192,2560]{2,1,0:T(8,128)(2,1)} %param.27), kind=kOutput, calls=%fused_computation.17 | convolution fusion | flops 252313600 | bytes 17137664 | tf_op jit(solution)/shard_map/slmf,lfd->slmd/dot_general | solution.py:154
  154.5 2.1 copy.71
  156.6 3.7 %all-to-all-start.1 = ((bf16[8,16,2,2560]{3,2,1,0:T(2,128)(2,1)}), bf16[8,16,2,2560]{3,2,1,0:T(2,128)(2,1)S(1)}, u32[]{:S(2)}, u32[]{:S(2)}) async-start(bf16[8,16,2,2560]{3,2,1,0:T(2,128)(2,1)} %copy.71), calls=%async_computation.1 | async-start | bytes 2621440 | tf_op jit(solution)/shard_map/all_to_all | solution.py:155
  161.1 31.4 %all-to-all-done.1 = bf16[8,16,2,2560]{3,2,1,0:T(2,128)(2,1)S(1)} async-done(((bf16[8,16,2,2560]{3,2,1,0:T(2,128)(2,1)}), bf16[8,16,2,2560]{3,2,1,0:T(2,128)(2,1)S(1)}, u32[]{:S(2)}, u32[]{:S(2)}) %all-to-all-start.1) | async-done | bytes 1310752 | tf_op jit(solution)/shard_map/all_to_all | solution.py:155
  192.5 1.6 convert_reduce_fusion
  194.1 0.9 reshape.486
  195.0 0.7 gather_fusion.9
  196.1 1.0 copy.86
  197.2 1.5 reshape.576
  198.7 23.5 %reduce-scatter.4.cloned.1.call-done = bf16[640,8]{1,0:T(8,128)(2,1)} async-done(((bf16[2560,8]{1,0:T(8,128)(2,1)}), bf16[640,8]{1,0:T(8,128)(2,1)}) %reduce-scatter.4.cloned.1.call-update) | async-done | bytes 10256
  222.2 1.1 reshape.577
  (102 shorter events, 7.7 us)
Async XLA Ops:
  6.5 19.2 %copy-start = (bf16[1,16,128,128]{3,2,1,0:T(8,128)(2,1)S(1)}, bf16[1,16,128,128]{3,2,1,0:T(8,128)(2,1)}, u32[]{:S(2)}) copy-start(bf16[1,16,128,128]{3,2,1,0:T(8,128)(2,1)} %param.17) | copy-start | bytes 1572868
  6.5 76.1 %all-reduce.6.cloned.1.call-start = ((), (), s32[]{:S(2)}) async-start(), calls=%async_computation.3 | async-start | bytes 327680 | tf_op jit(solution)/shard_map/psum | solution.py:89
  25.8 1.0 copy-start.3
  27.1 2.2 copy-start.7
  27.1 2.2 copy-start.8
  27.2 2.3 copy-start.2
  27.2 2.3 copy-start.6
  27.2 2.9 %copy-start.5 = (s32[16]{0:T(128)S(1)}, s32[16]{0:T(128)}, u32[]{:S(2)}) copy-start(s32[16]{0:T(128)} %constant.244) | copy-start | bytes 196
  30.1 3.9 %copy-start.11 = (bf16[2,4,2,128]{3,2,1,0:T(2,128)(2,1)S(1)}, bf16[2,4,2,128]{3,2,1,0:T(2,128)(2,1)}, u32[]{:S(2)}) copy-start(bf16[2,4,2,128]{3,2,1,0:T(2,128)(2,1)} %param.16) | copy-start | bytes 12292
  32.2 51.6 %copy-start.10 = (bf16[2,4,640]{2,1,0:T(4,128)(2,1)S(1)}, bf16[2,4,640]{2,1,0:T(4,128)(2,1)}, u32[]{:S(2)}) copy-start(bf16[2,4,640]{2,1,0:T(4,128)(2,1)} %param.14) | copy-start | bytes 30724
  32.2 60.0 %copy-start.9 = (f32[2560]{0:T(1024)S(1)}, f32[2560]{0:T(1024)}, u32[]{:S(2)}) copy-start(f32[2560]{0:T(1024)} %param.23) | copy-start | bytes 30724
  156.6 4.0 %copy-start.4 = (bf16[2560,64]{0,1:T(8,128)(2,1)S(1)}, bf16[2560,64]{0,1:T(8,128)(2,1)}, u32[]{:S(2)}) copy-start(bf16[2560,64]{0,1:T(8,128)(2,1)} %param.24) | copy-start | bytes 983044
  156.6 35.8 %all-to-all-start.1 = ((bf16[8,16,2,2560]{3,2,1,0:T(2,128)(2,1)}), bf16[8,16,2,2560]{3,2,1,0:T(2,128)(2,1)S(1)}, u32[]{:S(2)}, u32[]{:S(2)}) async-start(bf16[8,16,2,2560]{3,2,1,0:T(2,128)(2,1)} %copy.71), calls=%async_computation.1 | async-start | bytes 2621440 | tf_op jit(solution)/shard_map/all_to_all | solution.py:155
  160.3 61.8 %reduce-scatter.4.cloned.1.call-start = ((), (), s32[]{:S(2)}) async-start(), calls=%async_computation.4 | async-start | bytes 819200
  197.2 26.9 %copy-start.1 = (bf16[1,16,128,128]{3,2,1,0:T(8,128)(2,1)S(1)}, bf16[1,16,128,128]{3,2,1,0:T(8,128)(2,1)}, u32[]{:S(2)}) copy-start(bf16[1,16,128,128]{3,2,1,0:T(8,128)(2,1)} %param.17) | copy-start | bytes 1572868
Sparse Core Ops, SparseCore 0:
  29.4 53.2 all-reduce.5
  198.8 23.3 reduce-scatter.3
where the time goes:
time: 231 us
  blocking collectives  104 us (45%)
  waiting for transfers between devices  58.5 us (25%)
  matrix products  26 us (11%)
  local copies, waits for them, and re-layouts  18.3 us (8%)
  between operations  13.9 us (6%)
  other arithmetic  6.19 us (3%)
  starting transfers between devices  3.74 us (2%)
    all_to_all x1, blocking collectives, local(): lax.all_to_all(outgoing, 'wide', split_axis=0, concat_axis=0, tiled=True)  37.3 us
    all_to_all x1, waiting for transfers between devices, local(): lax.all_to_all(partial_value.astype(jnp.bfloat16), 'wide', split_axis=0,...  31.4 us
    psum x1, blocking collectives, local(): full_num, full_den = lax.psum((part_num, part_den), 'wide')  29.1 us
    unnamed x3, waiting for transfers between devices  23.5 us
    all_gather x1, blocking collectives, local(): lax.all_gather(queries, 'wide', axis=0, tiled=True)  15.8 us
    all_gather x1, blocking collectives, local(): lax.all_gather(new_kv, 'wide', axis=0, tiled=True)  14 us
    all_gather x1, blocking collectives, local(): full_rows = lax.all_gather(residual, 'kv', axis=2, tiled=True)  8.18 us
    dot_general x1, matrix products, local(): jnp.einsum('slmd,ldf->slmf', arrived_rows, up_w, preferred_element_type=j...  7.74 us
  transfers between devices with their start and end apart: 3, of which 3 were waited for; matrix products, arithmetic and copies ran while one was open for 3% of the time, Pallas kernels for 0%

commit v1 on v0

v1 whole, which is shorter than its diff:
```python
import math

import jax
import jax.numpy as jnp
from jax import lax
from jax.sharding import PartitionSpec as P

HD = 128
E = 64
BEAMS = 8
BLK = 128
LANES = 128


def spread(block, axes, count):
    copies = jnp.broadcast_to(block[None], (count,) + block.shape)
    return lax.all_to_all(copies, axes, split_axis=0, concat_axis=0, tiled=True)


def chain_mask(parents, own_tokens, steps):
    tokens = jnp.arange(parents.shape[0], dtype=jnp.int32)
    base = tokens // BEAMS * BEAMS
    hops = [
        ((base + parents[:, j])[:, None] == tokens[None, :]).astype(jnp.float32)
        for j in range(steps - 1)
    ]
    same = (own_tokens[:, None] == tokens[None, :]).astype(jnp.float32)
    zero = jnp.zeros_like(same)
    rows = []
    for step_now in range(steps):
        cells = [zero] * steps
        cells[step_now] = same
        for earlier in range(step_now, 0, -1):
            cells[earlier - 1] = jnp.dot(cells[earlier], hops[earlier - 1])
        rows.append(jnp.stack(cells, axis=1))
    return jnp.stack(rows, axis=1)


def local(
    stream_in,
    queries,
    new_kv,
    cache_keys,
    cache_values,
    lengths,
    page_table,
    parents,
    routes,
    norm_gain,
    router,
    gate_w,
    up_w,
    down_w,
):
    wide_index = lax.axis_index("wide")
    wide_count = lax.axis_size("wide")
    kv_count = lax.axis_size("kv")
    step_tok, steps, feats = stream_in.shape
    rows = step_tok * steps
    heads = feats // HD
    groups = lengths.shape[0]
    token_count = groups * BEAMS
    all_rows = token_count * steps
    slots_local = cache_keys.shape[1]
    top = routes.shape[2]
    halves = gate_w.shape[0]
    score_scale = 1.0 / math.sqrt(HD)

    packed = jnp.concatenate(
        [
            queries.reshape(rows, feats),
            new_kv.reshape(rows, 2 * HD),
            jnp.pad(routes.reshape(rows, top).astype(jnp.bfloat16), ((0, 0), (0, LANES - top))),
        ],
        axis=1,
    )
    gathered = spread(packed, "wide", wide_count).reshape(all_rows, feats + 2 * HD + LANES)
    all_queries = gathered[:, :feats]
    all_keys = gathered[:, feats : feats + HD]
    all_values = gathered[:, feats + HD : feats + 2 * HD]
    all_routes = gathered[:, feats + 2 * HD : feats + 2 * HD + top].astype(jnp.int32)

    slot_ids = wide_index * slots_local + jnp.arange(slots_local, dtype=jnp.int32)
    slot_hits = page_table[None, :, :] == slot_ids[:, None, None]
    group_ids = jnp.arange(groups, dtype=jnp.int32)
    block_starts = jnp.arange(page_table.shape[1], dtype=jnp.int32) * BLK
    owner_group = jnp.sum(jnp.where(slot_hits, group_ids[None, :, None], 0), axis=(1, 2))
    block_limit = jnp.sum(
        jnp.where(slot_hits, lengths[None, :, None] - block_starts[None, None, :], 0), axis=(1, 2)
    )
    key_ok = (jnp.arange(BLK, dtype=jnp.int32)[None, :] < block_limit[:, None]).astype(jnp.float32)
    grouped = all_queries.reshape(groups, BEAMS * steps * heads, HD)
    picked = grouped[owner_group]
    scores = jnp.einsum("nrd,npd->nrp", picked, cache_keys[0], preferred_element_type=jnp.float32)
    weights = (jnp.exp(scores * score_scale) * key_ok[:, None, :]).astype(jnp.bfloat16)
    numerator = jnp.einsum(
        "nrp,npd->nrd", weights, cache_values[0], preferred_element_type=jnp.float32
    )
    denominator = jnp.sum(weights.astype(jnp.float32), axis=-1)
    member = (owner_group[None, :] == group_ids[:, None]).astype(jnp.float32)
    part_num = jnp.sum(member[:, :, None, None] * numerator[None], axis=1)
    part_den = jnp.sum(member[:, :, None] * denominator[None], axis=1)
    part_den = part_den.reshape(all_rows, heads)
    den_high = part_den.astype(jnp.bfloat16)
    den_low = (part_den - den_high.astype(jnp.float32)).astype(jnp.bfloat16)
    sums = jnp.concatenate(
        [
            part_num.reshape(all_rows, feats).astype(jnp.bfloat16),
            jnp.pad(
                jnp.concatenate([den_high, den_low], axis=1), ((0, 0), (0, LANES - 2 * heads))
            ),
        ],
        axis=1,
    )
    arrived = lax.all_to_all(
        sums.reshape(wide_count, rows, feats + LANES), "wide", split_axis=0, concat_axis=0, tiled=True
    )
    total = jnp.sum(arrived.astype(jnp.float32), axis=0)
    mine_num = total[:, :feats].reshape(rows, heads, HD)
    mine_den = total[:, feats : feats + heads] + total[:, feats + heads : feats + 2 * heads]

    own_tokens = wide_index * step_tok + jnp.arange(step_tok, dtype=jnp.int32)
    mask = chain_mask(parents, own_tokens, steps).reshape(rows, 1, steps, token_count)
    own_queries = queries.reshape(rows, heads, HD)
    tail_keys = all_keys.reshape(token_count, steps, HD)
    tail_values = all_values.reshape(token_count, steps, HD)
    tail_scores = jnp.einsum(
        "rhd,tjd->rhjt", own_queries, tail_keys, preferred_element_type=jnp.float32
    )
    tail_weights = jnp.where(mask > 0, jnp.exp(tail_scores * score_scale), 0.0)
    tail_weights = tail_weights.astype(jnp.bfloat16)
    tail_num = jnp.einsum(
        "rhjt,tjd->rhd", tail_weights, tail_values, preferred_element_type=jnp.float32
    )
    tail_den = jnp.sum(tail_weights.astype(jnp.float32), axis=(2, 3))
    attended = ((mine_num + tail_num) / (mine_den + tail_den)[..., None]).astype(jnp.bfloat16)
    residual = (
        stream_in.reshape(rows, feats).astype(jnp.float32)
        + attended.reshape(rows, feats).astype(jnp.float32)
    ).astype(jnp.bfloat16)

    spread_rows = spread(residual, ("kv", "wide"), kv_count * wide_count)
    spread_rows = spread_rows.reshape(kv_count, all_rows, feats)
    token_rows = jnp.swapaxes(spread_rows, 0, 1).reshape(all_rows, kv_count * feats)
    token_rows = token_rows.astype(jnp.float32)
    mean_square = jnp.mean(token_rows * token_rows, axis=1, keepdims=True)
    normed = (token_rows * lax.rsqrt(mean_square + 1e-06) * norm_gain[None, :]).astype(jnp.bfloat16)
    logits = jnp.dot(normed, router, preferred_element_type=jnp.float32)
    expert_ids = jnp.arange(E, dtype=jnp.int32)
    chosen = jnp.any(all_routes[:, :, None] == expert_ids[None, None, :], axis=1)
    raised = jnp.where(chosen, jnp.exp(logits), 0.0)
    share = raised / jnp.sum(raised, axis=1, keepdims=True)
    half_expert = (wide_index * halves + jnp.arange(halves, dtype=jnp.int32)) // 2
    pick = (expert_ids[:, None] == half_expert[None, :]).astype(jnp.float32)
    half_share = jnp.dot(share, pick, precision=lax.Precision.HIGHEST)

    gate_out = jnp.einsum("td,ldf->tlf", normed, gate_w, preferred_element_type=jnp.float32)
    up_out = jnp.einsum("td,ldf->tlf", normed, up_w, preferred_element_type=jnp.float32)
    hidden = (jax.nn.silu(gate_out) * up_out * half_share[:, :, None]).astype(jnp.bfloat16)
    partial = jnp.einsum("tlf,lfd->td", hidden, down_w, preferred_element_type=jnp.float32)
    outgoing = partial.astype(jnp.bfloat16).reshape(wide_count, rows, kv_count, feats)
    outgoing = jnp.transpose(outgoing, (2, 0, 1, 3)).reshape(kv_count * wide_count, rows, feats)
    returned = lax.all_to_all(
        outgoing, ("kv", "wide"), split_axis=0, concat_axis=0, tiled=True
    )
    moe_part = jnp.sum(returned.astype(jnp.float32), axis=0)
    out = (residual.astype(jnp.float32) + moe_part).astype(jnp.bfloat16)
    return out.reshape(step_tok, steps, feats)


def solution(mesh):
    return jax.shard_map(
        local,
        mesh=mesh,
        in_specs=(
            P("wide", None, "kv"),
            P("wide", None, "kv"),
            P("wide", None, None, "kv"),
            P("kv", "wide", None, None),
            P("kv", "wide", None, None),
            P(),
            P(),
            P(),
            P("wide", None, None),
            P(),
            P(),
            P("wide", None, "kv"),
            P("wide", None, "kv"),
            P("wide", "kv", None),
        ),
        out_specs=P("wide", None, "kv"),
        check_vma=False,
    )
```

time: 231 us -> 88.5 us (0.38)
  blocking collectives: 104 us -> 0 us
  waiting for transfers between devices: 58.5 us -> 31.3 us
  between operations: 13.9 us -> 0.25 us
  starting transfers between devices: 3.74 us -> 16 us
  local copies, waits for them, and re-layouts: 18.3 us -> 6.71 us
    all_gather x3 -> x0, blocking collectives: 38 us -> none  [the longest x1 15.8 us: local(): lax.all_gather(queries, 'wide', axis=0, tiled=True)]
    all_to_all x1 -> x0, blocking collectives: 37.3 us -> none  [local(): lax.all_to_all(outgoing, 'wide', split_axis=0, concat_axis=0, tiled=True)]
    psum x1 -> x0, blocking collectives: 29.1 us -> none  [local(): full_num, full_den = lax.psum((part_num, part_den), 'wide')]
    unnamed x3 -> x0, waiting for transfers between devices: 23.5 us -> none
    all_to_all x1 -> x4, starting transfers between devices: 3.7 us -> 16 us  [the longest x2 9.71 us: spread(): return lax.all_to_all(copies, axes, split_axis=0, concat_axis=0, tiled=True)]
    gather x11 -> x0, local copies, waits for them, and re-layouts: 7.03 us -> none  [the longest x6 4.13 us: chain_tokens(): current = group_base + parents[current, earlier - 1]]
    psum x1 -> x0, waiting for transfers between devices: 3.55 us -> none  [local(): full_num, full_den = lax.psum((part_num, part_den), 'wide')]
    unnamed x30 -> x9, local copies, waits for them, and re-layouts: 4.26 us -> 0.9 us
  transfers between devices with their start and end apart: 3 -> 4, of which waited for: 3 -> 4; matrix products, arithmetic and copies ran while one was open for 3% -> 7% of each run, Pallas kernels for 0% -> 0%
where the time goes in v1:
time: 88.5 us; the launch traced here: 87.5 us
  waiting for transfers between devices  31.3 us (35%)
  matrix products  26.9 us (30%)
  starting transfers between devices  16 us (18%)
  local copies, waits for them, and re-layouts  6.71 us (8%)
  other arithmetic  6.35 us (7%)
    dot_general x1, matrix products, local(): jnp.einsum('tlf,lfd->td', hidden, down_w, preferred_element_type=jnp.floa...  14 us
    all_to_all x2, waiting for transfers between devices, spread(): return lax.all_to_all(copies, axes, split_axis=0, concat_axis=0, tiled=True)  13.2 us
    all_to_all x1, waiting for transfers between devices, local(): lax.all_to_all(outgoing, ('kv', 'wide'), split_axis=0, concat_axis=0, til...  12.1 us
    all_to_all x2, starting transfers between devices, spread(): return lax.all_to_all(copies, axes, split_axis=0, concat_axis=0, tiled=True)  9.71 us
    dot_general x1, matrix products, local(): jnp.einsum('td,ldf->tlf', normed, gate_w, preferred_element_type=jnp.floa...  8.42 us
    all_to_all x1, waiting for transfers between devices, local(): lax.all_to_all(sums.reshape(wide_count, rows, feats + LANES), 'wide', spl...  6.01 us
    all_to_all x1, starting transfers between devices, local(): lax.all_to_all(sums.reshape(wide_count, rows, feats + LANES), 'wide', spl...  3.69 us
    all_to_all x1, starting transfers between devices, local(): lax.all_to_all(outgoing, ('kv', 'wide'), split_axis=0, concat_axis=0, til...  2.59 us
  transfers between devices with their start and end apart: 4, of which 4 were waited for; matrix products, arithmetic and copies ran while one was open for 7% of the time, Pallas kernels for 0%

profile of v1, /device:TPU:0, one launch (start us, length us, event | category | flops | bytes accessed | tf_op | source)
XLA Modules:
  0.0 87.5 jit_solution(10962168053775155918)
XLA Ops:
  0.0 0.8 convert_element_type.156
  0.8 0.7 copy.157
  1.5 0.7 reshape.297
  2.2 0.6 broadcast_in_dim.39
  2.8 6.3 %all-to-all-start = ((bf16[8,8,1024]{2,1,0:T(8,128)(2,1)}), bf16[8,8,1024]{2,1,0:T(8,128)(2,1)S(1)}, u32[]{:S(2)}, u32[]{:S(2)}) async-start(bf16[8,8,1024]{2,1,0:T(8,128)(2,1)} %broadcast_in_dim.39), calls=%async_computation | async-start | bytes 262144 | tf_op jit(solution)/shard_map/all_to_all | solution.py:17
  9.2 0.7 broadcast_subtract_fusion
  9.9 0.9 fusion.33
  10.9 0.8 add_bitcast_fusion.2
  13.0 0.7 reshape.305
  13.8 0.7 reshape.310
  14.5 1.4 %all-to-all-done = bf16[8,8,1024]{2,1,0:T(8,128)(2,1)S(1)} async-done(((bf16[8,8,1024]{2,1,0:T(8,128)(2,1)}), bf16[8,8,1024]{2,1,0:T(8,128)(2,1)S(1)}, u32[]{:S(2)}, u32[]{:S(2)}) %all-to-all-start) | async-done | bytes 131104 | tf_op jit(solution)/shard_map/all_to_all | solution.py:17
  16.0 0.7 gather_fusion
  16.7 0.8 convert_reduce_fusion
  18.0 1.4 %fusion.15 = f32[16,160,128]{2,1,0:T(8,128)S(1)} fusion(bf16[16,160,128]{2,1,0:T(8,128)(2,1)S(1)} %get-tuple-element.19, bf16[1,16,128,128]{3,2,1,0:T(8,128)(2,1)} %param.18), kind=kOutput, calls=%fused_computation.29 | convolution fusion | flops 83886080 | bytes 2490368 | tf_op jit(solution)/shard_map/nrp,npd->nrd/dot_general | solution.py:96
  19.3 0.3 multiply_reduce_fusion
  19.7 0.6 fusion.27
  20.3 3.7 %all-to-all-start.1 = ((bf16[8,8,768]{2,1,0:T(8,128)(2,1)}), bf16[8,8,768]{2,1,0:T(8,128)(2,1)S(1)}, u32[]{:S(2)}, u32[]{:S(2)}) async-start(bf16[8,8,768]{2,1,0:T(8,128)(2,1)} %fusion.27), calls=%async_computation.1 | async-start | bytes 196608 | tf_op jit(solution)/shard_map/all_to_all | solution.py:115
  24.0 0.2 convert_reduce_fusion.3
  24.4 6.0 %all-to-all-done.1 = bf16[8,8,768]{2,1,0:T(8,128)(2,1)S(1)} async-done(((bf16[8,8,768]{2,1,0:T(8,128)(2,1)}), bf16[8,8,768]{2,1,0:T(8,128)(2,1)S(1)}, u32[]{:S(2)}, u32[]{:S(2)}) %all-to-all-start.1) | async-done | bytes 98336 | tf_op jit(solution)/shard_map/all_to_all | solution.py:115
  30.5 0.5 fusion.31
  31.1 0.7 broadcast_in_dim.43
  31.8 3.4 %all-to-all-start.2 = ((bf16[32,8,640]{2,1,0:T(8,128)(2,1)}), bf16[32,8,640]{2,1,0:T(8,128)(2,1)S(1)}, u32[]{:S(2)}, u32[]{:S(2)}) async-start(bf16[32,8,640]{2,1,0:T(8,128)(2,1)} %broadcast_in_dim.43), calls=%async_computation.2 | async-start | bytes 655360 | tf_op jit(solution)/shard_map/all_to_all | solution.py:17
  35.5 11.8 %all-to-all-done.2 = bf16[32,8,640]{2,1,0:T(8,128)(2,1)S(1)} async-done(((bf16[32,8,640]{2,1,0:T(8,128)(2,1)}), bf16[32,8,640]{2,1,0:T(8,128)(2,1)S(1)}, u32[]{:S(2)}, u32[]{:S(2)}) %all-to-all-start.2) | async-done | bytes 327712 | tf_op jit(solution)/shard_map/all_to_all | solution.py:17
  47.6 0.8 multiply_convert_fusion
  48.5 8.4 %fusion.22 = f32[64,16,192]{2,0,1:T(8,128)S(1)} fusion(bf16[16,2560,192]{1,2,0:T(8,128)(2,1)} %param.25, bf16[64,2560]{1,0:T(8,128)(2,1)S(1)} %multiply_convert_fusion), kind=kOutput, calls=%fused_computation.35 | convolution fusion | flops 1006632960 | bytes 16842752 | tf_op jit(solution)/shard_map/td,ldf->tlf/dot_general | solution.py:157
  56.9 0.3 fusion.60
  57.2 0.2 fusion.28
  57.4 14.0 %fusion = bf16[64,2560]{1,0:T(8,128)(2,1)S(1)} fusion(bf16[16,192,2560]{2,1,0:T(8,128)(2,1)} %param.27, bf16[16,2560,192]{1,2,0:T(8,128)(2,1)} %param.26, f32[64,16,192]{2,0,1:T(8,128)S(1)} %fusion.22, f32[64,16]{0,1:T(8,128)S(1)} %fusion.28, bf16[64,2560]{1,0:T(8,128)(2,1)S(1)} %multiply_convert_fusion), kind=kOutput, calls=%fused_computation.2 | convolution fusion | flops 2014806016 | bytes 32903168 | tf_op jit(solution)/shard_map/tlf,lfd->td/dot_general | solution.py:160
  71.4 0.7 copy.129
  72.1 2.6 %all-to-all-start.3 = ((bf16[32,8,640]{2,1,0:T(8,128)(2,1)}), bf16[32,8,640]{2,1,0:T(8,128)(2,1)S(1)}, u32[]{:S(2)}, u32[]{:S(2)}) async-start(bf16[32,8,640]{2,1,0:T(8,128)(2,1)} %bitcast.40), calls=%async_computation.3 | async-start | bytes 655360 | tf_op jit(solution)/shard_map/all_to_all | solution.py:163
  74.8 12.1 %all-to-all-done.3 = bf16[32,8,640]{2,1,0:T(8,128)(2,1)S(1)} async-done(((bf16[32,8,640]{2,1,0:T(8,128)(2,1)}), bf16[32,8,640]{2,1,0:T(8,128)(2,1)S(1)}, u32[]{:S(2)}, u32[]{:S(2)}) %all-to-all-start.3) | async-done | bytes 327712 | tf_op jit(solution)/shard_map/all_to_all | solution.py:163
  86.9 0.6 add_convert_fusion
  (57 shorter events, 3.1 us)
Async XLA Ops:
  0.0 16.7 %copy-start = (bf16[1,16,128,128]{3,2,1,0:T(8,128)(2,1)S(1)}, bf16[1,16,128,128]{3,2,1,0:T(8,128)(2,1)}, u32[]{:S(2)}) copy-start(bf16[1,16,128,128]{3,2,1,0:T(8,128)(2,1)} %param.17) | copy-start | bytes 1572868
  0.0 56.9 %copy-start.1 = (bf16[2560,64]{0,1:T(8,128)(2,1)S(1)}, bf16[2560,64]{0,1:T(8,128)(2,1)}, u32[]{:S(2)}) copy-start(bf16[2560,64]{0,1:T(8,128)(2,1)} %param.24) | copy-start | bytes 983044
  2.8 13.1 %all-to-all-start = ((bf16[8,8,1024]{2,1,0:T(8,128)(2,1)}), bf16[8,8,1024]{2,1,0:T(8,128)(2,1)S(1)}, u32[]{:S(2)}, u32[]{:S(2)}) async-start(bf16[8,8,1024]{2,1,0:T(8,128)(2,1)} %broadcast_in_dim.39), calls=%async_computation | async-start | bytes 262144 | tf_op jit(solution)/shard_map/all_to_all | solution.py:17
  20.3 10.0 %all-to-all-start.1 = ((bf16[8,8,768]{2,1,0:T(8,128)(2,1)}), bf16[8,8,768]{2,1,0:T(8,128)(2,1)S(1)}, u32[]{:S(2)}, u32[]{:S(2)}) async-start(bf16[8,8,768]{2,1,0:T(8,128)(2,1)} %fusion.27), calls=%async_computation.1 | async-start | bytes 196608 | tf_op jit(solution)/shard_map/all_to_all | solution.py:115
  31.8 15.5 %all-to-all-start.2 = ((bf16[32,8,640]{2,1,0:T(8,128)(2,1)}), bf16[32,8,640]{2,1,0:T(8,128)(2,1)S(1)}, u32[]{:S(2)}, u32[]{:S(2)}) async-start(bf16[32,8,640]{2,1,0:T(8,128)(2,1)} %broadcast_in_dim.43), calls=%async_computation.2 | async-start | bytes 655360 | tf_op jit(solution)/shard_map/all_to_all | solution.py:17
  57.4 29.5 %copy-start.2 = (bf16[2,4,640]{2,1,0:T(4,128)(2,1)S(1)}, bf16[2,4,640]{2,1,0:T(4,128)(2,1)}, u32[]{:S(2)}) copy-start(bf16[2,4,640]{2,1,0:T(4,128)(2,1)} %param.14) | copy-start | bytes 30724
  72.1 14.7 %all-to-all-start.3 = ((bf16[32,8,640]{2,1,0:T(8,128)(2,1)}), bf16[32,8,640]{2,1,0:T(8,128)(2,1)S(1)}, u32[]{:S(2)}, u32[]{:S(2)}) async-start(bf16[32,8,640]{2,1,0:T(8,128)(2,1)} %bitcast.40), calls=%async_computation.3 | async-start | bytes 655360 | tf_op jit(solution)/shard_map/all_to_all | solution.py:163

commit v2 on v1

v2 whole, which is shorter than its diff:
```python
import functools
import math

import jax
import jax.numpy as jnp
from jax import lax
from jax.experimental import pallas as pl
from jax.experimental.pallas import tpu as pltpu
from jax.sharding import PartitionSpec as P

HD = 128
E = 64
BEAMS = 8
BLK = 128
LANES = 128
MIB = 2**20
AHEAD = 6
F32 = jnp.float32
BF16 = jnp.bfloat16
NT = (((1,), (1,)), ((), ()))
TN = (((0,), (0,)), ((), ()))
VMEM = pl.BlockSpec(memory_space=pltpu.VMEM)
SMEM = pl.BlockSpec(memory_space=pltpu.SMEM)
HBM = pl.BlockSpec(memory_space=pltpu.HBM)


def sent(block, axes):
    return lax.all_to_all(block, axes, split_axis=0, concat_axis=0, tiled=True)


def pack_kernel(query_ref, new_ref, route_ref, out_ref):
    step_tok, steps, feats = query_ref.shape
    lanes = lax.broadcasted_iota(jnp.int32, (steps, LANES), 1)
    parts = []
    for t in range(step_tok):
        named = route_ref[t]
        chosen = jnp.zeros((steps, LANES), F32)
        for i in range(named.shape[1]):
            chosen = jnp.where(named[:, i : i + 1] == lanes, 1.0, chosen)
        parts.append(
            jnp.concatenate(
                [
                    query_ref[t].astype(F32),
                    new_ref[t, :, 0, :].astype(F32),
                    new_ref[t, :, 1, :].astype(F32),
                    chosen,
                ],
                axis=1,
            )
        )
    block = jnp.concatenate(parts, axis=0).astype(BF16)
    for w in range(out_ref.shape[0]):
        out_ref[w] = block


def attend_kernel(owner_ref, limit_ref, rows_ref, key_ref, value_ref, out_ref, query_ref, sum_ref):
    slots = key_ref.shape[0]
    groups, stacked, _ = query_ref.shape
    feats = out_ref.shape[1] - LANES
    heads = feats // HD
    span = stacked // heads
    scale = 1.0 / math.sqrt(HD)
    for g in range(groups):
        for h in range(heads):
            query_ref[g, h * span : (h + 1) * span, :] = rows_ref[
                g * span : (g + 1) * span, h * HD : (h + 1) * HD
            ]
    sum_ref[...] = jnp.zeros_like(sum_ref)
    ones = jnp.ones((BLK, HD), BF16)
    place = lax.broadcasted_iota(jnp.int32, (stacked, BLK), 1)
    for n in range(slots):
        group = owner_ref[n]
        scores = lax.dot_general(query_ref[group], key_ref[n], NT, preferred_element_type=F32)
        weights = jnp.where(place < limit_ref[n], jnp.exp(scores * scale), 0.0).astype(BF16)
        extended = jnp.concatenate([value_ref[n], ones], axis=1)
        sum_ref[group] += jnp.dot(weights, extended, preferred_element_type=F32)
    lanes = lax.broadcasted_iota(jnp.int32, (span, LANES), 1)
    for g in range(groups):
        tail = jnp.zeros((span, LANES), F32)
        for h in range(heads):
            piece = sum_ref[g, h * span : (h + 1) * span, :]
            out_ref[g * span : (g + 1) * span, h * HD : (h + 1) * HD] = piece[:, :HD].astype(BF16)
            high = piece[:, HD:].astype(BF16).astype(F32)
            tail = jnp.where(lanes == h, high, tail)
            tail = jnp.where(lanes == heads + h, piece[:, HD:] - high, tail)
        out_ref[g * span : (g + 1) * span, feats:] = tail.astype(BF16)


def suffix_kernel(query_ref, rows_ref, mask_ref, num_ref, den_ref):
    step_tok, steps, feats = query_ref.shape
    rows = step_tok * steps
    heads = feats // HD
    scale = 1.0 / math.sqrt(HD)
    own = jnp.concatenate([query_ref[t].astype(F32) for t in range(step_tok)], axis=0)
    stacked = jnp.concatenate([own[:, h * HD : (h + 1) * HD] for h in range(heads)], axis=0)
    keys = rows_ref[:, feats : feats + HD]
    values = rows_ref[:, feats + HD : feats + 2 * HD]
    scores = lax.dot_general(stacked.astype(BF16), keys, NT, preferred_element_type=F32)
    mask = jnp.concatenate([mask_ref[...]] * heads, axis=0)
    weights = jnp.where(mask > 0, jnp.exp(scores * scale), 0.0).astype(BF16)
    extended = jnp.concatenate([values, jnp.ones_like(values)], axis=1)
    sums = jnp.dot(weights, extended, preferred_element_type=F32)
    for h in range(heads):
        num_ref[:, h * HD : (h + 1) * HD] = sums[h * rows : (h + 1) * rows, :HD]
        den_ref[:, h * HD : (h + 1) * HD] = sums[h * rows : (h + 1) * rows, HD:]


def residual_kernel(sums_ref, num_ref, den_ref, stream_ref, out_ref, spread_ref):
    rows, feats = out_ref.shape
    heads = feats // HD
    total = sums_ref[0].astype(F32)
    for w in range(1, sums_ref.shape[0]):
        total = total + sums_ref[w].astype(F32)
    stream = jnp.concatenate(
        [stream_ref[t].astype(F32) for t in range(stream_ref.shape[0])], axis=0
    )
    dens = total[:, feats : feats + heads] + total[:, feats + heads : feats + 2 * heads]
    parts = []
    for h in range(heads):
        at = slice(h * HD, (h + 1) * HD)
        attended = (total[:, at] + num_ref[:, at]) / (dens[:, h : h + 1] + den_ref[:, at])
        parts.append(stream[:, at] + attended.astype(BF16).astype(F32))
    residual = jnp.concatenate(parts, axis=1).astype(BF16)
    out_ref[...] = residual
    for d in range(spread_ref.shape[0]):
        spread_ref[d] = residual


def expert_kernel(
    per_unit, first_ref, rows_ref, chosen_ref, gain_ref, router_ref, gate_hbm, up_hbm, down_hbm,
    out_ref, slot_ref, norm_ref, share_ref, hidden_ref, total_ref, sems,
):
    kv_count, count, feats = rows_ref.shape
    units, width, _ = gate_hbm.shape
    sources = [ref.at[l] for l in range(units) for ref in (gate_hbm, up_hbm)]
    sources += [down_hbm.at[l] for l in range(units)]
    copies = [
        pltpu.make_async_copy(source, slot_ref.at[i], sems.at[i])
        for i, source in enumerate(sources)
    ]
    for copy in copies[:AHEAD]:
        copy.start()

    def arrive(i):
        copies[i].wait()
        if i + AHEAD < len(copies):
            copies[i + AHEAD].start()

    block = 64
    offset = chosen_ref.shape[1] - LANES
    for b in range(count // block):
        at = slice(b * block, (b + 1) * block)
        squares = jnp.zeros((block, 1), F32)
        for k in range(kv_count):
            part = rows_ref[k, at, :].astype(F32)
            squares += jnp.sum(part * part, axis=1, keepdims=True)
        root = lax.rsqrt(squares / (kv_count * feats) + 1e-06)
        for k in range(kv_count):
            columns = slice(k * feats, (k + 1) * feats)
            part = rows_ref[k, at, :].astype(F32)
            norm_ref[at, columns] = (part * root * gain_ref[:, columns]).astype(BF16)
        logits = lax.dot_general(norm_ref[at, :], router_ref[...], NT, preferred_element_type=F32)
        chosen = chosen_ref[at, offset:].astype(F32)
        raised = jnp.where(chosen[:, :E] > 0, jnp.exp(logits), 0.0)
        share = raised / jnp.sum(raised, axis=1, keepdims=True)
        share = jnp.concatenate([share, jnp.zeros((block, LANES - E), F32)], axis=1)
        share_ref[:, at] = share.T
    normed = norm_ref[...]
    for l in range(units):
        arrive(2 * l)
        arrive(2 * l + 1)
        gate = lax.dot_general(slot_ref[2 * l], normed, NT, preferred_element_type=F32)
        up = lax.dot_general(slot_ref[2 * l + 1], normed, NT, preferred_element_type=F32)
        weight = share_ref[pl.ds((first_ref[0] + l * per_unit) // 2, 1), :]
        hidden_ref[l] = (gate / (1.0 + jnp.exp(-gate)) * up * weight).astype(BF16)
    for l in range(units):
        i = 2 * units + l
        arrive(i)
        for k in range(kv_count):
            columns = slice(k * feats, (k + 1) * feats)
            piece = lax.dot_general(
                hidden_ref[l], slot_ref[i, :, columns], TN, preferred_element_type=F32
            )
            if l > 0:
                piece = piece + total_ref[k]
            if l + 1 < units:
                total_ref[k] = piece
            else:
                out_ref[k] = piece.astype(BF16)


def chain_mask(parents, own_tokens, steps):
    tokens = jnp.arange(parents.shape[0], dtype=jnp.int32)
    base = tokens // BEAMS * BEAMS
    hops = [
        ((base + parents[:, j])[:, None] == tokens[None, :]).astype(jnp.float32)
        for j in range(steps - 1)
    ]
    same = (own_tokens[:, None] == tokens[None, :]).astype(jnp.float32)
    zero = jnp.zeros_like(same)
    rows = []
    for step_now in range(steps):
        cells = [zero] * steps
        cells[step_now] = same
        for earlier in range(step_now, 0, -1):
            cells[earlier - 1] = jnp.dot(cells[earlier], hops[earlier - 1])
        rows.append(jnp.stack(cells, axis=1))
    return jnp.stack(rows, axis=1)


def local(
    stream_in,
    queries,
    new_kv,
    cache_keys,
    cache_values,
    lengths,
    page_table,
    parents,
    routes,
    norm_gain,
    router,
    gate_w,
    up_w,
    down_w,
):
    wide_index = lax.axis_index("wide")
    wide_count = lax.axis_size("wide")
    kv_count = lax.axis_size("kv")
    step_tok, steps, feats = stream_in.shape
    rows = step_tok * steps
    heads = feats // HD
    groups = lengths.shape[0]
    token_count = groups * BEAMS
    all_rows = token_count * steps
    slots_local = cache_keys.shape[1]
    halves = gate_w.shape[0]
    half_width = gate_w.shape[2]
    width = kv_count * feats
    payload = feats + 2 * HD + LANES

    packed = pl.pallas_call(
        pack_kernel,
        out_shape=jax.ShapeDtypeStruct((wide_count, rows, payload), BF16),
        in_specs=[VMEM] * 3,
        out_specs=VMEM,
        name="pack",
    )(queries, new_kv, routes)
    gathered = sent(packed, "wide").reshape(all_rows, payload)

    slot_ids = wide_index * slots_local + jnp.arange(slots_local, dtype=jnp.int32)
    slot_hits = page_table[None, :, :] == slot_ids[:, None, None]
    group_ids = jnp.arange(groups, dtype=jnp.int32)
    block_starts = jnp.arange(page_table.shape[1], dtype=jnp.int32) * BLK
    owner_group = jnp.sum(jnp.where(slot_hits, group_ids[None, :, None], 0), axis=(1, 2))
    block_limit = jnp.sum(
        jnp.where(slot_hits, lengths[None, :, None] - block_starts[None, None, :], 0), axis=(1, 2)
    )
    own_tokens = wide_index * step_tok + jnp.arange(step_tok, dtype=jnp.int32)
    mask = chain_mask(parents, own_tokens, steps)
    mask = jnp.swapaxes(mask, 2, 3).reshape(rows, all_rows)

    sums = pl.pallas_call(
        attend_kernel,
        out_shape=jax.ShapeDtypeStruct((all_rows, feats + LANES), BF16),
        in_specs=[SMEM, SMEM, VMEM, VMEM, VMEM],
        out_specs=VMEM,
        scratch_shapes=[
            pltpu.VMEM((groups, BEAMS * steps * heads, HD), BF16),
            pltpu.VMEM((groups, BEAMS * steps * heads, 2 * HD), F32),
        ],
        compiler_params=pltpu.CompilerParams(vmem_limit_bytes=32 * MIB),
        name="attend",
    )(owner_group, block_limit, gathered, cache_keys[0], cache_values[0])
    gain = norm_gain.reshape(1, width)
    sums, gain = lax.optimization_barrier((sums, gain))
    arrived = sent(sums.reshape(wide_count, rows, feats + LANES), "wide")
    tail_num, tail_den = pl.pallas_call(
        suffix_kernel,
        out_shape=[jax.ShapeDtypeStruct((rows, feats), F32)] * 2,
        in_specs=[VMEM] * 3,
        out_specs=[VMEM] * 2,
        cost_estimate=pl.CostEstimate(flops=40_000_000, bytes_accessed=2_000_000, transcendentals=0),
        name="suffix",
    )(queries, gathered, mask)
    residual, copies = pl.pallas_call(
        residual_kernel,
        out_shape=[
            jax.ShapeDtypeStruct((rows, feats), BF16),
            jax.ShapeDtypeStruct((kv_count * wide_count, rows, feats), BF16),
        ],
        in_specs=[VMEM] * 4,
        out_specs=[VMEM] * 2,
        name="residual",
    )(arrived, tail_num, tail_den, stream_in)

    spread_rows = sent(copies, ("kv", "wide")).reshape(kv_count, all_rows, feats)
    per_unit = 2 if halves % 2 == 0 else 1
    units = halves // per_unit
    unit_width = per_unit * half_width
    gate_rows = jnp.swapaxes(gate_w, 1, 2).reshape(units, unit_width, width)
    up_rows = jnp.swapaxes(up_w, 1, 2).reshape(units, unit_width, width)
    down_rows = down_w.reshape(units, unit_width, width)
    partial = pl.pallas_call(
        functools.partial(expert_kernel, per_unit),
        out_shape=jax.ShapeDtypeStruct((kv_count, all_rows, feats), BF16),
        in_specs=[SMEM, VMEM, VMEM, VMEM, VMEM, HBM, HBM, HBM],
        out_specs=VMEM,
        scratch_shapes=[
            pltpu.VMEM((3 * units, unit_width, width), BF16),
            pltpu.VMEM((all_rows, width), BF16),
            pltpu.VMEM((LANES, all_rows), F32),
            pltpu.VMEM((units, unit_width, all_rows), BF16),
            pltpu.VMEM((kv_count, all_rows, feats), F32),
            pltpu.SemaphoreType.DMA((3 * units,)),
        ],
        compiler_params=pltpu.CompilerParams(vmem_limit_bytes=56 * MIB),
        cost_estimate=pl.CostEstimate(
            flops=6 * all_rows * halves * half_width * width,
            bytes_accessed=6 * halves * half_width * width,
            transcendentals=0,
        ),
        name="experts",
    )(
        (wide_index * halves).astype(jnp.int32).reshape(1),
        spread_rows,
        gathered,
        gain,
        router.T,
        gate_rows,
        up_rows,
        down_rows,
    )
    returned = sent(partial.reshape(kv_count * wide_count, rows, feats), ("kv", "wide"))
    moe_part = jnp.sum(returned.astype(F32), axis=0)
    out = (residual.astype(F32) + moe_part).astype(BF16)
    return out.reshape(step_tok, steps, feats)


def solution(mesh):
    return jax.shard_map(
        local,
        mesh=mesh,
        in_specs=(
            P("wide", None, "kv"),
            P("wide", None, "kv"),
            P("wide", None, None, "kv"),
            P("kv", "wide", None, None),
            P("kv", "wide", None, None),
            P(),
            P(),
            P(),
            P("wide", None, None),
            P(),
            P(),
            P("wide", None, "kv"),
            P("wide", None, "kv"),
            P("wide", "kv", None),
        ),
        out_specs=P("wide", None, "kv"),
        check_vma=False,
    )
```

time: 88.5 us -> 80.9 us (0.914)
  blocking collectives: 0 us -> 30.4 us
  waiting for transfers between devices: 31.3 us -> 5.37 us
  matrix products: 26.9 us -> 1.13 us
  Pallas kernels: 0 us -> 25.3 us
  starting transfers between devices: 16 us -> 9.69 us
  other arithmetic: 6.35 us -> 2.64 us
  local copies, waits for them, and re-layouts: 6.71 us -> 5.58 us
    all_to_all x0 -> x2, blocking collectives: none -> 30.4 us  [sent(): return lax.all_to_all(block, axes, split_axis=0, concat_axis=0, tiled=True)]
    all_to_all x4 -> x2, waiting for transfers between devices: 31.3 us -> 5.37 us  [sent(): return lax.all_to_all(block, axes, split_axis=0, concat_axis=0, tiled=True)]
    dot_general x8 -> x0, matrix products: 25.8 us -> none  [the longest x1 14 us: local(): jnp.einsum('tlf,lfd->td', hidden, down_w, preferred_element_type=jnp.floa...]
    pallas_call x0 -> x5, Pallas kernels: none -> 25.3 us  [the longest x1 17.4 us: local(): pl.pallas_call(functools.partial(expert_kernel, per_unit), out_shape=jax....]
    all_to_all x4 -> x2, starting transfers between devices: 16 us -> 9.69 us  [sent(): return lax.all_to_all(block, axes, split_axis=0, concat_axis=0, tiled=True)]
    convert_element_type x7 -> x1, other arithmetic: 2.3 us -> 0.01 us  [local(): out = (residual.astype(F32) + moe_part).astype(BF16)]
    unnamed x9 -> x10, local copies, waits for them, and re-layouts: 0.9 us -> 2.77 us
    broadcast_in_dim x2 -> x0, local copies, waits for them, and re-layouts: 1.39 us -> none  [spread(): copies = jnp.broadcast_to(block[None], (count,) + block.shape)]
  transfers between devices with their start and end apart: 4 -> 2, of which waited for: 4 -> 2; matrix products, arithmetic and copies ran while one was open for 7% -> 7% of each run, Pallas kernels for 0% -> 2%
where the time goes in v2:
time: 80.9 us; the launch traced here: 80.1 us
  blocking collectives  30.4 us (38%)
  Pallas kernels  25.3 us (31%)
  starting transfers between devices  9.69 us (12%)
  local copies, waits for them, and re-layouts  5.58 us (7%)
  waiting for transfers between devices  5.37 us (7%)
  other arithmetic  2.64 us (3%)
  matrix products  1.13 us (1%)
    all_to_all x2, blocking collectives, sent(): return lax.all_to_all(block, axes, split_axis=0, concat_axis=0, tiled=True)  30.4 us
    pallas_call x1, Pallas kernels, local(): pl.pallas_call(functools.partial(expert_kernel, per_unit), out_shape=jax....  17.4 us
    all_to_all x2, starting transfers between devices, sent(): return lax.all_to_all(block, axes, split_axis=0, concat_axis=0, tiled=True)  9.69 us
    all_to_all x2, waiting for transfers between devices, sent(): return lax.all_to_all(block, axes, split_axis=0, concat_axis=0, tiled=True)  5.37 us
    pallas_call x1, Pallas kernels, local(): pl.pallas_call(attend_kernel, out_shape=jax.ShapeDtypeStruct((all_rows, f...  2.77 us
    unnamed x10, local copies, waits for them, and re-layouts  2.77 us
    pallas_call x1, Pallas kernels, local(): pl.pallas_call(residual_kernel, out_shape=[jax.ShapeDtypeStruct((rows, fe...  1.83 us
    pallas_call x1, Pallas kernels, local(): pl.pallas_call(suffix_kernel, out_shape=[jax.ShapeDtypeStruct((rows, feat...  1.79 us
  transfers between devices with their start and end apart: 2, of which 2 were waited for; matrix products, arithmetic and copies ran while one was open for 7% of the time, Pallas kernels for 2%

profile of v2, /device:TPU:0, one launch (start us, length us, event | category | flops | bytes accessed | tf_op | source)
XLA Modules:
  0.0 80.1 jit_solution(3713274852783382632)
XLA Ops:
  0.0 1.5 %pack.1 = bf16[8,8,1024]{2,1,0:T(8,128)(2,1)} custom-call(bf16[2,4,640]{2,1,0:T(4,128)(2,1)} %query_ref.3, bf16[2,4,2,128]{3,2,1,0:T(2,128)(2,1)} %new_ref.1, s32[2,4,6]{2,1,0:T(4,128)} %route_ref.1), custom_call_target="tpu_custom_call" | custom-call | tf_op jit(solution)/shard_map/pack/pallas_call | solution.py:242
  1.5 6.3 %all-to-all-start = ((bf16[8,8,1024]{2,1,0:T(8,128)(2,1)}), bf16[8,8,1024]{2,1,0:T(8,128)(2,1)S(1)}, u32[]{:S(2)}, u32[]{:S(2)}) async-start(bf16[8,8,1024]{2,1,0:T(8,128)(2,1)} %pack.1), calls=%async_computation | async-start | bytes 262144 | tf_op jit(solution)/shard_map/all_to_all | solution.py:28
  7.8 0.1 compare_convert_fusion
  7.9 0.8 %add_bitcast_fusion.2 = (s32[16]{0:T(128)S(1)}, s32[16]{0:T(128)S(1)}, s32[16]{0:T(128)S(1)}) fusion(s32[16,3]{0,1:T(4,128)} %param.21), kind=kLoop, calls=%fused_computation.37 | loop fusion | flops 192 | bytes 384 | tf_op jit(solution)/shard_map/eq | solution.py:196
  8.7 0.2 fusion.5
  8.9 0.2 fusion.3
  9.1 0.2 fusion.2
  9.3 0.2 fusion.4
  9.4 0.2 convolution_bitcast_fusion.1
  9.6 0.2 convolution_bitcast_fusion
  9.8 0.7 broadcast_subtract_fusion
  10.6 0.9 %fusion.1 = (s32[16]{0:T(128)S(1)}, s32[16]{0:T(128)S(1)}) fusion(s32[2,32]{1,0:T(2,128)S(1)} %broadcast_subtract_fusion, s32[2,32]{1,0:T(2,128)} %param.20, s32[16]{0:T(128)S(1)} %iota_add_fusion.1), kind=kLoop, calls=%fused_computation.7 | loop fusion | flops 5088 | bytes 704 | tf_op jit(solution)/shard_map/reduce_sum | solution.py:256
  11.4 1.3 %reshape.147.gain_ref = f32[1,2560]{1,0:T(1,128)} reshape(f32[2560]{0:T(1024)} %param.23) | data formatting | bytes 20480 | tf_op jit(solution)/shard_map/reshape | solution.py:275
  12.8 0.1 pad.17.clone
  12.8 1.7 %all-to-all-done = bf16[8,8,1024]{2,1,0:T(8,128)(2,1)S(1)} async-done(((bf16[8,8,1024]{2,1,0:T(8,128)(2,1)}), bf16[8,8,1024]{2,1,0:T(8,128)(2,1)S(1)}, u32[]{:S(2)}, u32[]{:S(2)}) %all-to-all-start) | async-done | bytes 131104 | tf_op jit(solution)/shard_map/all_to_all | solution.py:28
  14.6 1.1 %copy-done.1 = bf16[1,16,128,128]{3,2,1,0:T(8,128)(2,1)S(1)} copy-done((bf16[1,16,128,128]{3,2,1,0:T(8,128)(2,1)S(1)}, bf16[1,16,128,128]{3,2,1,0:T(8,128)(2,1)}, u32[]{:S(2)}) %copy-start.1) | copy-done | bytes 524312
  15.7 1.0 %copy-done.2 = bf16[1,16,128,128]{3,2,1,0:T(8,128)(2,1)S(1)} copy-done((bf16[1,16,128,128]{3,2,1,0:T(8,128)(2,1)S(1)}, bf16[1,16,128,128]{3,2,1,0:T(8,128)(2,1)}, u32[]{:S(2)}) %copy-start.2) | copy-done | bytes 524312
  16.7 2.8 %attend.1 = bf16[64,768]{1,0:T(8,128)(2,1)} custom-call(s32[16]{0:T(128)S(1)} %get-tuple-element.18.owner_ref, s32[16]{0:T(128)S(1)} %get-tuple-element.17.limit_ref, bf16[64,1024]{1,0:T(8,128)(2,1)S(1)} %bitcast.49, bf16[16,128,128]{2,1,0:T(8,128)(2,1)S(1)} %bitcast.52, bf16[16,128,128]{2,1,0:T(8,128)(2,1)S(1)} %bitcast.53), custom_call_target="tpu_custom_call" | custom-call | tf_op jit(solution)/shard_map/attend/pallas_call | solution.py:263
  19.5 3.4 %all-to-all-start.1 = ((bf16[8,8,768]{2,1,0:T(8,128)(2,1)}), bf16[8,8,768]{2,1,0:T(8,128)(2,1)S(1)}, u32[]{:S(2)}, u32[]{:S(2)}) async-start(bf16[8,8,768]{2,1,0:T(8,128)(2,1)} %bitcast.3), calls=%async_computation.1 | async-start | bytes 196608 | tf_op jit(solution)/shard_map/all_to_all | solution.py:28
  22.8 0.1 maximum_bitcast_fusion.1
  22.9 0.1 copy.35
  23.1 0.7 reshape.149.mask_ref
  23.7 0.0 copy-done
  23.7 1.8 %suffix.1 = (f32[8,640]{1,0:T(8,128)}, f32[8,640]{1,0:T(8,128)}) custom-call(bf16[2,4,640]{2,1,0:T(4,128)(2,1)} %query_ref.3, bf16[64,1024]{1,0:T(8,128)(2,1)} %bitcast.50, f32[8,64]{1,0:T(8,128)} %reshape.149.mask_ref), custom_call_target="tpu_custom_call" | custom-call | flops 40000000 | bytes 2000000 | tf_op jit(solution)/shard_map/suffix/pallas_call | solution.py:278
  25.5 3.6 %all-to-all-done.1.sums_ref = bf16[8,8,768]{2,1,0:T(8,128)(2,1)S(1)} async-done(((bf16[8,8,768]{2,1,0:T(8,128)(2,1)}), bf16[8,8,768]{2,1,0:T(8,128)(2,1)S(1)}, u32[]{:S(2)}, u32[]{:S(2)}) %all-to-all-start.1) | async-done | bytes 98336 | tf_op jit(solution)/shard_map/all_to_all | solution.py:28
  29.2 0.6 copy-done.3
  29.8 1.8 %residual.1 = (bf16[8,640]{1,0:T(8,128)(2,1)}, bf16[32,8,640]{2,1,0:T(8,128)(2,1)}) custom-call(bf16[8,8,768]{2,1,0:T(8,128)(2,1)} %copy-done.3, f32[8,640]{1,0:T(8,128)} %get-tuple-element.12.num_ref, f32[8,640]{1,0:T(8,128)} %get-tuple-element.13.den_ref, bf16[2,4,640]{2,1,0:T(4,128)(2,1)} %stream_ref.1), custom_call_target="tpu_custom_call" | custom-call | tf_op jit(solution)/shard_map/residual/pallas_call | solution.py:286
  31.6 15.6 %all_to_all.20 = bf16[32,8,640]{2,1,0:T(8,128)(2,1)} all-to-all(bf16[32,8,640]{2,1,0:T(8,128)(2,1)} %get-tuple-element.15), channel_id=1, replica_groups=mesh['kv'=4,'wide'=8] {'kv','wide'}, dimensions={0} | all-to-all | bytes 655360 | tf_op jit(solution)/shard_map/all_to_all | solution.py:28
  47.3 17.4 %experts.1 = bf16[4,64,640]{2,1,0:T(8,128)(2,1)} custom-call(s32[1]{0:T(128)} %bitcast.22.first_ref, bf16[4,64,640]{2,1,0:T(8,128)(2,1)} %bitcast.57, bf16[64,1024]{1,0:T(8,128)(2,1)} %bitcast.51, f32[1,2560]{1,0:T(1,128)} %reshape.147.gain_ref, bf16[64,2560]{1,0:T(8,128)(2,1)} %bitcast.59, bf16[8,384,2560]{2,1,0:T(8,128)(2,1)} %bitcast.54, ...), custom_call_target="tpu_custom_call" | custom-call | flops 3019898880 | bytes 47185920 | tf_op jit(solution)/shard_map/experts/pallas_call | solution.py:304
  64.7 14.7 %all_to_all.21 = bf16[32,8,640]{2,1,0:T(8,128)(2,1)S(1)} all-to-all(bf16[32,8,640]{2,1,0:T(8,128)(2,1)} %bitcast.58), channel_id=1, replica_groups=mesh['kv'=4,'wide'=8] {'kv','wide'}, dimensions={0} | all-to-all | bytes 655360 | tf_op jit(solution)/shard_map/all_to_all | solution.py:28
  79.4 0.1 convert_reduce_fusion
  79.5 0.6 reshape.156
  (15 shorter events, 0.1 us)
Async XLA Ops:
  1.5 13.1 %all-to-all-start = ((bf16[8,8,1024]{2,1,0:T(8,128)(2,1)}), bf16[8,8,1024]{2,1,0:T(8,128)(2,1)S(1)}, u32[]{:S(2)}, u32[]{:S(2)}) async-start(bf16[8,8,1024]{2,1,0:T(8,128)(2,1)} %pack.1), calls=%async_computation | async-start | bytes 262144 | tf_op jit(solution)/shard_map/all_to_all | solution.py:28
  14.6 9.2 %copy-start = (bf16[8,8,1024]{2,1,0:T(8,128)(2,1)}, bf16[8,8,1024]{2,1,0:T(8,128)(2,1)S(1)}, u32[]{:S(2)}) copy-start(bf16[8,8,1024]{2,1,0:T(8,128)(2,1)S(1)} %all-to-all-done) | copy-start | bytes 393220
  14.6 1.1 %copy-start.1 = (bf16[1,16,128,128]{3,2,1,0:T(8,128)(2,1)S(1)}, bf16[1,16,128,128]{3,2,1,0:T(8,128)(2,1)}, u32[]{:S(2)}) copy-start(bf16[1,16,128,128]{3,2,1,0:T(8,128)(2,1)} %param.17) | copy-start | bytes 1572868
  15.7 1.0 %copy-start.2 = (bf16[1,16,128,128]{3,2,1,0:T(8,128)(2,1)S(1)}, bf16[1,16,128,128]{3,2,1,0:T(8,128)(2,1)}, u32[]{:S(2)}) copy-start(bf16[1,16,128,128]{3,2,1,0:T(8,128)(2,1)} %param.18) | copy-start | bytes 1572868
  19.5 9.7 %all-to-all-start.1 = ((bf16[8,8,768]{2,1,0:T(8,128)(2,1)}), bf16[8,8,768]{2,1,0:T(8,128)(2,1)S(1)}, u32[]{:S(2)}, u32[]{:S(2)}) async-start(bf16[8,8,768]{2,1,0:T(8,128)(2,1)} %bitcast.3), calls=%async_computation.1 | async-start | bytes 196608 | tf_op jit(solution)/shard_map/all_to_all | solution.py:28
  29.2 0.6 copy-start.3
  47.3 32.2 %copy-start.4 = (bf16[8,640]{1,0:T(8,128)(2,1)S(1)}, bf16[8,640]{1,0:T(8,128)(2,1)}, u32[]{:S(2)}) copy-start(bf16[8,640]{1,0:T(8,128)(2,1)} %get-tuple-element.14) | copy-start | bytes 30724

commit v3 on v2

v3 whole, which is shorter than its diff:
```python
import functools
import math

import jax
import jax.numpy as jnp
from jax import lax
from jax.experimental import pallas as pl
from jax.experimental.pallas import tpu as pltpu
from jax.sharding import Mesh
from jax.sharding import PartitionSpec as P

HD = 128
E = 64
BEAMS = 8
BLK = 128
LANES = 128
MIB = 2**20
AHEAD = 6
F32 = jnp.float32
BF16 = jnp.bfloat16
NT = (((1,), (1,)), ((), ()))
TN = (((0,), (0,)), ((), ()))
VMEM = pl.BlockSpec(memory_space=pltpu.VMEM)
SMEM = pl.BlockSpec(memory_space=pltpu.SMEM)
HBM = pl.BlockSpec(memory_space=pltpu.HBM)
ANY = pl.BlockSpec(memory_space=pl.ANY)
WIDE = ("z", "core")


def small(shape, dtype):
    return math.prod(shape) * jnp.dtype(dtype).itemsize <= MIB


def near(array):
    if small(array.shape, array.dtype):
        return pltpu.with_memory_space_constraint(array, pltpu.VMEM)
    return array


def far(array):
    return pltpu.with_memory_space_constraint(array, pltpu.HBM)


def result(shape, dtype):
    if small(shape, dtype):
        return pltpu.VMEM(shape, dtype)
    return jax.ShapeDtypeStruct(shape, dtype)


def sent(block, axes):
    return lax.all_to_all(block, axes, split_axis=0, concat_axis=0, tiled=True)


def pack_kernel(query_ref, new_ref, route_ref, out_ref):
    step_tok, steps, feats = query_ref.shape
    lanes = lax.broadcasted_iota(jnp.int32, (steps, LANES), 1)
    parts = []
    for t in range(step_tok):
        named = route_ref[t]
        chosen = jnp.zeros((steps, LANES), F32)
        for i in range(named.shape[1]):
            chosen = jnp.where(named[:, i : i + 1] == lanes, 1.0, chosen)
        parts.append(
            jnp.concatenate(
                [
                    query_ref[t].astype(F32),
                    new_ref[t, :, 0, :].astype(F32),
                    new_ref[t, :, 1, :].astype(F32),
                    chosen,
                ],
                axis=1,
            )
        )
    block = jnp.concatenate(parts, axis=0).astype(BF16)
    for w in range(out_ref.shape[0]):
        out_ref[w] = block


def stage_kernel(
    table_ref, length_ref, key_hbm, value_hbm, router_hbm, gain_hbm, after_ref,
    key_ref, extended_ref, router_ref, gain_ref, valid_ref, sems,
):
    del after_ref
    slots = key_ref.shape[0]
    groups, blocks = table_ref.shape
    copies = [
        pltpu.make_async_copy(key_hbm, key_ref, sems.at[0]),
        pltpu.make_async_copy(value_hbm, extended_ref.at[:, :, pl.ds(0, HD)], sems.at[1]),
        pltpu.make_async_copy(router_hbm, router_ref, sems.at[2]),
        pltpu.make_async_copy(gain_hbm, gain_ref, sems.at[3]),
    ]
    for copy in copies:
        copy.start()
    extended_ref[:, :, HD:] = jnp.ones((slots, BLK, HD), BF16)
    valid_ref[...] = jnp.zeros_like(valid_ref)
    first_slot = lax.axis_index(WIDE) * slots
    place = lax.broadcasted_iota(jnp.int32, (1, BLK), 1)

    def look(i, carry):
        group, block = i // blocks, i % blocks
        slot = table_ref[group, block] - first_slot

        @pl.when((slot >= 0) & (slot < slots))
        def _():
            limit = length_ref[group] - block * BLK
            valid_ref[group, pl.ds(slot, 1), :] = jnp.where(place < limit, 1.0, 0.0)

        return carry

    lax.fori_loop(0, groups * blocks, look, 0)
    for copy in copies:
        copy.wait()


def attend_kernel(rows_ref, key_ref, extended_ref, valid_ref, out_ref, query_ref, weight_ref):
    slots = key_ref.shape[0]
    groups = valid_ref.shape[0]
    stacked = query_ref.shape[0]
    feats = out_ref.shape[1] - LANES
    heads = feats // HD
    span = stacked // heads
    scale = 1.0 / math.sqrt(HD)
    lanes = lax.broadcasted_iota(jnp.int32, (span, LANES), 1)

    def one_group(g, carry):
        rows = pl.ds(pl.multiple_of(g * span, span), span)
        for h in range(heads):
            query_ref[h * span : (h + 1) * span, :] = rows_ref[rows, h * HD : (h + 1) * HD]
        query = query_ref[...]
        for n in range(slots):
            scores = lax.dot_general(query, key_ref[n], NT, preferred_element_type=F32)
            weights = jnp.where(valid_ref[g, n : n + 1, :] > 0, jnp.exp(scores * scale), 0.0)
            weight_ref[:, n * BLK : (n + 1) * BLK] = weights.astype(BF16)
        sums = jnp.dot(
            weight_ref[...],
            extended_ref[...].reshape(slots * BLK, 2 * HD),
            preferred_element_type=F32,
        )
        tail = jnp.zeros((span, LANES), F32)
        for h in range(heads):
            piece = sums[h * span : (h + 1) * span, :]
            out_ref[rows, h * HD : (h + 1) * HD] = piece[:, :HD].astype(BF16)
            high = piece[:, HD:].astype(BF16).astype(F32)
            tail = jnp.where(lanes == h, high, tail)
            tail = jnp.where(lanes == heads + h, piece[:, HD:] - high, tail)
        out_ref[rows, feats:] = tail.astype(BF16)
        return carry

    lax.fori_loop(0, groups, one_group, 0, unroll=groups <= 2)


def suffix_kernel(parent_ref, query_ref, rows_ref, stream_ref, num_ref, den_ref, own_ref):
    step_tok, steps, feats = query_ref.shape
    rows = step_tok * steps
    heads = feats // HD
    scale = 1.0 / math.sqrt(HD)
    own = jnp.concatenate([query_ref[t].astype(F32) for t in range(step_tok)], axis=0)
    own_ref[...] = jnp.concatenate([stream_ref[t].astype(F32) for t in range(step_tok)], axis=0)
    stacked = jnp.concatenate([own[:, h * HD : (h + 1) * HD] for h in range(heads)], axis=0)
    keys = rows_ref[:, feats : feats + HD]
    values = rows_ref[:, feats + HD : feats + 2 * HD]
    scores = lax.dot_general(stacked.astype(BF16), keys, NT, preferred_element_type=F32)
    first_token = lax.axis_index(WIDE) * step_tok
    shape = (heads * rows, rows_ref.shape[0])
    row = lax.broadcasted_iota(jnp.int32, shape, 0) % rows
    column = lax.broadcasted_iota(jnp.int32, shape, 1)
    mask = jnp.zeros(shape, F32)
    for t in range(step_tok):
        token = first_token + t
        base = token // BEAMS * BEAMS
        for s in range(steps):
            ancestor = token
            for j in range(s, -1, -1):
                hit = (row == t * steps + s) & (column == ancestor * steps + j)
                mask = jnp.where(hit, 1.0, mask)
                if j > 0:
                    ancestor = base + parent_ref[j - 1, ancestor]
    weights = jnp.where(mask > 0, jnp.exp(scores * scale), 0.0).astype(BF16)
    extended = jnp.concatenate([values, jnp.ones_like(values)], axis=1)
    sums = jnp.dot(weights, extended, preferred_element_type=F32)
    for h in range(heads):
        num_ref[:, h * HD : (h + 1) * HD] = sums[h * rows : (h + 1) * rows, :HD]
        den_ref[:, h * HD : (h + 1) * HD] = sums[h * rows : (h + 1) * rows, HD:]


def residual_kernel(sums_ref, num_ref, den_ref, stream_ref, out_ref, spread_ref):
    rows, feats = out_ref.shape
    heads = feats // HD
    total = sums_ref[0].astype(F32)
    for w in range(1, sums_ref.shape[0]):
        total = total + sums_ref[w].astype(F32)
    dens = total[:, feats : feats + heads] + total[:, feats + heads : feats + 2 * heads]
    parts = []
    for h in range(heads):
        at = slice(h * HD, (h + 1) * HD)
        attended = (total[:, at] + num_ref[:, at]) / (dens[:, h : h + 1] + den_ref[:, at])
        parts.append(stream_ref[:, at] + attended.astype(BF16).astype(F32))
    residual = jnp.concatenate(parts, axis=1).astype(BF16)
    out_ref[...] = residual
    for d in range(spread_ref.shape[0]):
        spread_ref[d] = residual


def expert_kernel(
    per_unit, own_ref, other_ref, chosen_ref, gain_ref, router_ref, gate_hbm, up_hbm, down_hbm,
    mine_ref, theirs_ref, slot_ref, norm_ref, share_ref, hidden_ref, total_ref, sems,
):
    kv_count, count, feats = total_ref.shape
    pieces, rows, _ = own_ref.shape
    chips = pieces // kv_count
    core = lax.axis_index("core")
    units, width, _ = gate_hbm.shape
    sources = [ref.at[l] for l in range(units) for ref in (gate_hbm, up_hbm)]
    sources += [down_hbm.at[l] for l in range(units)]
    copies = [
        pltpu.make_async_copy(source, slot_ref.at[i], sems.at[i])
        for i, source in enumerate(sources)
    ]
    for copy in copies[:AHEAD]:
        copy.start()

    def arrive(i):
        copies[i].wait()
        if i + AHEAD < len(copies):
            copies[i + AHEAD].start()

    def place(z, carry):
        for ref, side in ((own_ref, core), (other_ref, 1 - core)):
            at = pl.ds(pl.multiple_of((z * 2 + side) * rows, rows), rows)
            for k in range(kv_count):
                total_ref[k, at, :] = ref[k * chips + z].astype(F32)
        return carry

    lax.fori_loop(0, chips, place, 0, unroll=chips <= 8)
    block = 64
    offset = chosen_ref.shape[1] - LANES
    for b in range(count // block):
        at = slice(b * block, (b + 1) * block)
        squares = jnp.zeros((block, 1), F32)
        for k in range(kv_count):
            part = total_ref[k, at, :]
            squares += jnp.sum(part * part, axis=1, keepdims=True)
        root = lax.rsqrt(squares / (kv_count * feats) + 1e-06)
        for k in range(kv_count):
            columns = slice(k * feats, (k + 1) * feats)
            part = total_ref[k, at, :]
            norm_ref[at, columns] = (part * root * gain_ref[columns].reshape(1, feats)).astype(BF16)
        logits = lax.dot_general(norm_ref[at, :], router_ref[...], NT, preferred_element_type=F32)
        chosen = chosen_ref[at, offset:].astype(F32)
        raised = jnp.where(chosen[:, :E] > 0, jnp.exp(logits), 0.0)
        share = raised / jnp.sum(raised, axis=1, keepdims=True)
        share = jnp.concatenate([share, jnp.zeros((block, LANES - E), F32)], axis=1)
        share_ref[:, at] = share.T
    normed = norm_ref[...]
    first_half = lax.axis_index(WIDE) * units * per_unit
    for l in range(units):
        arrive(2 * l)
        arrive(2 * l + 1)
        gate = lax.dot_general(slot_ref[2 * l], normed, NT, preferred_element_type=F32)
        up = lax.dot_general(slot_ref[2 * l + 1], normed, NT, preferred_element_type=F32)
        weight = share_ref[pl.ds((first_half + l * per_unit) // 2, 1), :]
        hidden_ref[l] = (gate / (1.0 + jnp.exp(-gate)) * up * weight).astype(BF16)
    for l in range(units):
        i = 2 * units + l
        arrive(i)
        for k in range(kv_count):
            columns = slice(k * feats, (k + 1) * feats)
            piece = lax.dot_general(
                hidden_ref[l], slot_ref[i, :, columns], TN, preferred_element_type=F32
            )
            total_ref[k] = piece if l == 0 else piece + total_ref[k]

    def hand_out(z, carry):
        for ref, side in ((mine_ref, core), (theirs_ref, 1 - core)):
            at = pl.ds(pl.multiple_of((z * 2 + side) * rows, rows), rows)
            for k in range(kv_count):
                ref[k * chips + z] = total_ref[k, at, :].astype(BF16)
        return carry

    lax.fori_loop(0, chips, hand_out, 0, unroll=chips <= 8)


def add_kernel(left_ref, right_ref, out_ref):
    for i in range(out_ref.shape[0]):
        out_ref[i] = (left_ref[i].astype(F32) + right_ref[i].astype(F32)).astype(BF16)


def finish_kernel(parts_ref, residual_ref, out_ref):
    total = parts_ref[0].astype(F32)
    for i in range(1, parts_ref.shape[0]):
        total = total + parts_ref[i].astype(F32)
    total = (residual_ref[...].astype(F32) + total).astype(BF16)
    step_tok, steps, _ = out_ref.shape
    for t in range(step_tok):
        out_ref[t] = total[t * steps : (t + 1) * steps]


def local(
    stream_in,
    queries,
    new_kv,
    cache_keys,
    cache_values,
    lengths,
    page_table,
    parents,
    routes,
    norm_gain,
    router,
    gate_w,
    up_w,
    down_w,
):
    kv_count = lax.axis_size("kv")
    chips = lax.axis_size("z")
    wide_count = lax.axis_size(WIDE)
    step_tok, steps, feats = stream_in.shape
    rows = step_tok * steps
    heads = feats // HD
    groups = lengths.shape[0]
    all_rows = groups * BEAMS * steps
    slots = cache_keys.shape[1]
    halves = gate_w.shape[0]
    half_width = gate_w.shape[2]
    width = kv_count * feats
    payload = feats + 2 * HD + LANES

    packed = pl.pallas_call(
        pack_kernel,
        out_shape=result((wide_count, rows, payload), BF16),
        in_specs=[VMEM] * 3,
        out_specs=VMEM,
        name="pack",
    )(queries, new_kv, routes)
    gathered = near(sent(packed, WIDE).reshape(all_rows, payload))
    keys, extended, router_rows, gain, valid = pl.pallas_call(
        stage_kernel,
        out_shape=[
            result((slots, BLK, HD), BF16),
            result((slots, BLK, 2 * HD), BF16),
            result((E, width), BF16),
            result((width,), F32),
            result((groups, slots, BLK), F32),
        ],
        in_specs=[SMEM, SMEM, HBM, HBM, HBM, HBM, ANY],
        out_specs=[VMEM] * 5,
        scratch_shapes=[pltpu.SemaphoreType.DMA((4,))],
        compiler_params=pltpu.CompilerParams(vmem_limit_bytes=16 * MIB),
        name="stage",
    )(
        far(page_table),
        far(lengths),
        far(cache_keys[0]),
        far(cache_values[0]),
        far(router.T),
        far(norm_gain),
        packed,
    )
    sums = pl.pallas_call(
        attend_kernel,
        out_shape=result((all_rows, feats + LANES), BF16),
        in_specs=[VMEM] * 4,
        out_specs=VMEM,
        scratch_shapes=[
            pltpu.VMEM((BEAMS * steps * heads, HD), BF16),
            pltpu.VMEM((BEAMS * steps * heads, slots * BLK), BF16),
        ],
        compiler_params=pltpu.CompilerParams(vmem_limit_bytes=32 * MIB),
        name="attend",
    )(gathered, near(keys), near(extended), near(valid))
    arrived = sent(sums.reshape(wide_count, rows, feats + LANES), WIDE)
    tail_num, tail_den, stream = pl.pallas_call(
        suffix_kernel,
        out_shape=[result((rows, feats), F32)] * 3,
        in_specs=[SMEM, VMEM, VMEM, VMEM],
        out_specs=[VMEM] * 3,
        cost_estimate=pl.CostEstimate(flops=40_000_000, bytes_accessed=2_000_000, transcendentals=0),
        name="suffix",
    )(far(parents.T), far(queries), gathered, far(stream_in))
    residual, copies = pl.pallas_call(
        residual_kernel,
        out_shape=[
            result((rows, feats), BF16),
            result((kv_count * chips, rows, feats), BF16),
        ],
        in_specs=[VMEM] * 4,
        out_specs=[VMEM] * 2,
        compiler_params=pltpu.CompilerParams(vmem_limit_bytes=16 * MIB),
        name="residual",
    )(near(arrived), near(tail_num), near(tail_den), near(stream))

    own = sent(copies, ("kv", "z"))
    other = lax.ppermute(own, "core", ((0, 1), (1, 0)))
    per_unit = 2 if halves % 2 == 0 else 1
    units = halves // per_unit
    unit_width = per_unit * half_width
    mine, theirs = pl.pallas_call(
        functools.partial(expert_kernel, per_unit),
        out_shape=[result((kv_count * chips, rows, feats), BF16)] * 2,
        in_specs=[VMEM] * 5 + [HBM] * 3,
        out_specs=[VMEM] * 2,
        scratch_shapes=[
            pltpu.VMEM((3 * units, unit_width, width), BF16),
            pltpu.VMEM((all_rows, width), BF16),
            pltpu.VMEM((LANES, all_rows), F32),
            pltpu.VMEM((units, unit_width, all_rows), BF16),
            pltpu.VMEM((kv_count, all_rows, feats), F32),
            pltpu.SemaphoreType.DMA((3 * units,)),
        ],
        compiler_params=pltpu.CompilerParams(vmem_limit_bytes=56 * MIB),
        cost_estimate=pl.CostEstimate(
            flops=6 * all_rows * halves * half_width * width,
            bytes_accessed=6 * halves * half_width * width,
            transcendentals=0,
        ),
        name="experts",
    )(
        near(own),
        near(other),
        gathered,
        near(gain),
        near(router_rows),
        jnp.swapaxes(gate_w, 1, 2).reshape(units, unit_width, width),
        jnp.swapaxes(up_w, 1, 2).reshape(units, unit_width, width),
        down_w.reshape(units, unit_width, width),
    )
    swapped = lax.ppermute(theirs, "core", ((0, 1), (1, 0)))
    both = pl.pallas_call(
        add_kernel,
        out_shape=result(mine.shape, BF16),
        in_specs=[VMEM] * 2,
        out_specs=VMEM,
        name="add",
    )(near(mine), near(swapped))
    returned = sent(both, ("kv", "z"))
    return pl.pallas_call(
        finish_kernel,
        out_shape=jax.ShapeDtypeStruct(stream_in.shape, BF16),
        in_specs=[VMEM] * 2,
        out_specs=VMEM,
        name="finish",
    )(near(returned), near(residual))


def solution(mesh):
    kv_count, wide_count = mesh.devices.shape
    split = Mesh(mesh.devices.reshape(kv_count, wide_count // 2, 2), ("kv",) + WIDE)
    return jax.shard_map(
        local,
        mesh=split,
        in_specs=(
            P(WIDE, None, "kv"),
            P(WIDE, None, "kv"),
            P(WIDE, None, None, "kv"),
            P("kv", WIDE, None, None),
            P("kv", WIDE, None, None),
            P(),
            P(),
            P(),
            P(WIDE, None, None),
            P(),
            P(),
            P(WIDE, None, "kv"),
            P(WIDE, None, "kv"),
            P(WIDE, "kv", None),
        ),
        out_specs=P(WIDE, None, "kv"),
        check_vma=False,
    )
```

time: 80.9 us -> 70.7 us (0.87)
  waiting for transfers between devices: 5.37 us -> 12.4 us
  blocking collectives: 30.4 us -> 24 us
  local copies, waits for them, and re-layouts: 5.58 us -> 0 us
  other arithmetic: 2.64 us -> 0 us
  Pallas kernels: 25.3 us -> 23.8 us
  matrix products: 1.13 us -> 0 us
    all_to_all x2, blocking collectives: 30.4 us -> 24 us  [sent(): return lax.all_to_all(block, axes, split_axis=0, concat_axis=0, tiled=True)]
    all_to_all x2, waiting for transfers between devices: 5.37 us -> 9.79 us  [sent(): return lax.all_to_all(block, axes, split_axis=0, concat_axis=0, tiled=True)]
    unnamed x10 -> x0, local copies, waits for them, and re-layouts: 2.77 us -> none
    ppermute x0 -> x2, waiting for transfers between devices: none -> 2.62 us  [the longest x1 1.39 us: local(): other = lax.ppermute(own, 'core', ((0, 1), (1, 0)))]
    reshape x3 -> x0, local copies, waits for them, and re-layouts: 2.6 us -> none  [the longest x1 1.31 us: local(): gain = norm_gain.reshape(1, width)]
    pallas_call x5 -> x8, Pallas kernels: 25.3 us -> 23.8 us  [the longest x1 16.2 us: local(): pl.pallas_call(functools.partial(expert_kernel, per_unit), out_shape=[res...]
    dot_general x6 -> x0, matrix products: 1.13 us -> none  [chain_mask(): cells[earlier - 1] = jnp.dot(cells[earlier], hops[earlier - 1])]
    reduce_sum x2 -> x0, other arithmetic: 0.92 us -> none  [the longest x1 0.86 us: local(): jnp.sum(jnp.where(slot_hits, lengths[None, :, None] - block_starts[None,...]
  transfers between devices with their start and end apart: 2 -> 4, of which waited for: 2 -> 4; matrix products, arithmetic and copies ran while one was open for 7% -> 0% of each run, Pallas kernels for 2% -> 5%
where the time goes in v3:
time: 70.7 us; the launch traced here: 70.2 us
  blocking collectives  24 us (34%)
  Pallas kernels  23.8 us (34%)
  waiting for transfers between devices  12.4 us (18%)
  starting transfers between devices  9.92 us (14%)
    all_to_all x2, blocking collectives, sent(): return lax.all_to_all(block, axes, split_axis=0, concat_axis=0, tiled=True)  24 us
    pallas_call x1, Pallas kernels, local(): pl.pallas_call(functools.partial(expert_kernel, per_unit), out_shape=[res...  16.2 us
    all_to_all x2, waiting for transfers between devices, sent(): return lax.all_to_all(block, axes, split_axis=0, concat_axis=0, tiled=True)  9.79 us
    all_to_all x2, starting transfers between devices, sent(): return lax.all_to_all(block, axes, split_axis=0, concat_axis=0, tiled=True)  9.69 us
    pallas_call x1, Pallas kernels, local(): pl.pallas_call(stage_kernel, out_shape=[result((slots, BLK, HD), BF16), r...  2.25 us
    pallas_call x1, Pallas kernels, local(): pl.pallas_call(attend_kernel, out_shape=result((all_rows, feats + LANES),...  2.09 us
    pallas_call x1, Pallas kernels, local(): pl.pallas_call(pack_kernel, out_shape=result((wide_count, rows, payload),...  1.45 us
  transfers between devices with their start and end apart: 4, of which 4 were waited for; matrix products, arithmetic and copies ran while one was open for 0% of the time, Pallas kernels for 5%

profile of v3, /device:TPU:0, one launch (start us, length us, event | category | flops | bytes accessed | tf_op | source)
XLA Modules:
  0.0 70.2 jit_solution(3365965292007042523)
XLA Ops:
  0.0 1.5 %pack.1.after_ref = bf16[8,8,1024]{2,1,0:T(8,128)(2,1)} custom-call(bf16[2,4,640]{2,1,0:T(4,128)(2,1)} %query_ref.3, bf16[2,4,2,128]{3,2,1,0:T(2,128)(2,1)} %new_ref.1, s32[2,4,6]{2,1,0:T(4,128)} %route_ref.1), custom_call_target="tpu_custom_call" | custom-call | tf_op jit(solution)/shard_map/pack/pallas_call | solution.py:328
  1.5 6.3 %all-to-all-start = ((bf16[8,8,1024]{2,1,0:T(8,128)(2,1)}), bf16[8,8,1024]{2,1,0:T(8,128)(2,1)S(1)}, u32[]{:S(2)}, u32[]{:S(2)}) async-start(bf16[8,8,1024]{2,1,0:T(8,128)(2,1)} %pack.1.after_ref), calls=%async_computation | async-start | bytes 262144 | tf_op jit(solution)/shard_map/all_to_all | solution.py:51
  7.8 2.3 %stage.1 = (bf16[16,128,128]{2,1,0:T(8,128)(2,1)S(1)}, bf16[16,128,256]{2,1,0:T(8,128)(2,1)S(1)}, bf16[64,2560]{1,0:T(8,128)(2,1)S(1)}, f32[2560]{0:T(1024)S(1)}, f32[2,16,128]{2,1,0:T(8,128)S(1)}) custom-call(s32[2,32]{1,0:T(2,128)} %table_ref.1, s32[2]{0:T(128)} %length_ref.1, bf16[16,128,128]{2,1,0:T(8,128)(2,1)} %bitcast.19, ...), custom_call_target="tpu_custom_call" | custom-call | tf_op jit(solution)/shard_map/stage/pallas_call | solution.py:336
  10.0 4.5 %all-to-all-done = bf16[8,8,1024]{2,1,0:T(8,128)(2,1)S(1)} async-done(((bf16[8,8,1024]{2,1,0:T(8,128)(2,1)}), bf16[8,8,1024]{2,1,0:T(8,128)(2,1)S(1)}, u32[]{:S(2)}, u32[]{:S(2)}) %all-to-all-start) | async-done | bytes 131104 | tf_op jit(solution)/shard_map/all_to_all | solution.py:51
  14.6 2.1 %attend.1 = bf16[64,768]{1,0:T(8,128)(2,1)} custom-call(bf16[64,1024]{1,0:T(8,128)(2,1)S(1)} %bitcast.13, bf16[16,128,128]{2,1,0:T(8,128)(2,1)S(1)} %get-tuple-element.17.key_ref, bf16[16,128,256]{2,1,0:T(8,128)(2,1)S(1)} %get-tuple-element.18.extended_ref, f32[2,16,128]{2,1,0:T(8,128)S(1)} %get-tuple-element.19.valid_ref), custom_call_target="tpu_custom_call" | custom-call | tf_op jit(solution)/shard_map/attend/pallas_call | solution.py:359
  16.6 3.4 %all-to-all-start.1 = ((bf16[8,8,768]{2,1,0:T(8,128)(2,1)}), bf16[8,8,768]{2,1,0:T(8,128)(2,1)S(1)}, u32[]{:S(2)}, u32[]{:S(2)}) async-start(bf16[8,8,768]{2,1,0:T(8,128)(2,1)} %bitcast.4), calls=%async_computation.1 | async-start | bytes 196608 | tf_op jit(solution)/shard_map/all_to_all | solution.py:51
  20.0 1.0 %suffix.1 = (f32[8,640]{1,0:T(8,128)S(1)}, f32[8,640]{1,0:T(8,128)S(1)}, f32[8,640]{1,0:T(8,128)S(1)}) custom-call(s32[3,16]{1,0:T(4,128)} %bitcast.22, bf16[2,4,640]{2,1,0:T(4,128)(2,1)} %query_ref.3, bf16[64,1024]{1,0:T(8,128)(2,1)S(1)} %bitcast.14, bf16[2,4,640]{2,1,0:T(4,128)(2,1)} %stream_ref.1), custom_call_target="tpu_custom_call" | custom-call | flops 40000000 | bytes 2000000 | tf_op jit(solution)/shard_map/suffix/pallas_call | solution.py:372
  21.0 5.3 %all-to-all-done.1.sums_ref = bf16[8,8,768]{2,1,0:T(8,128)(2,1)S(1)} async-done(((bf16[8,8,768]{2,1,0:T(8,128)(2,1)}), bf16[8,8,768]{2,1,0:T(8,128)(2,1)S(1)}, u32[]{:S(2)}, u32[]{:S(2)}) %all-to-all-start.1) | async-done | bytes 98336 | tf_op jit(solution)/shard_map/all_to_all | solution.py:51
  26.3 0.2 residual.1
  26.5 12.4 %all_to_all.20.own_ref = bf16[16,8,640]{2,1,0:T(8,128)(2,1)S(1)} all-to-all(bf16[16,8,640]{2,1,0:T(8,128)(2,1)S(1)} %get-tuple-element.23), channel_id=1, replica_groups=mesh['kv'=4,'z'=4,'core'=2] {'kv','z'}, dimensions={0} | all-to-all | bytes 327680 | tf_op jit(solution)/shard_map/all_to_all | solution.py:51
  38.9 0.0 collective-permute-start
  38.9 1.4 %collective-permute-done.other_ref = bf16[16,8,640]{2,1,0:T(8,128)(2,1)S(1)} collective-permute-done((bf16[16,8,640]{2,1,0:T(8,128)(2,1)S(1)}, bf16[16,8,640]{2,1,0:T(8,128)(2,1)S(1)}, u32[]{:S(2)}, u32[]{:S(2)}) %collective-permute-start) | collective-permute-done | bytes 163872 | tf_op jit(solution)/shard_map/ppermute | solution.py:393
  40.3 16.2 %experts.1 = (bf16[16,8,640]{2,1,0:T(8,128)(2,1)S(1)}, bf16[16,8,640]{2,1,0:T(8,128)(2,1)S(1)}) custom-call(bf16[16,8,640]{2,1,0:T(8,128)(2,1)S(1)} %all_to_all.20.own_ref, bf16[16,8,640]{2,1,0:T(8,128)(2,1)S(1)} %collective-permute-done.other_ref, bf16[64,1024]{1,0:T(8,128)(2,1)S(1)} %bitcast.15, f32[2560]{0:T(1024)S(1)} %get-tuple-element.24.gain_ref, ...), custom_call_target="tpu_custom_call" | custom-call | flops 3019898880 | bytes 47185920 | tf_op jit(solution)/shard_map/experts/pallas_call | solution.py:397
  56.5 0.2 collective-permute-start.1
  56.7 1.2 %collective-permute-done.1.right_ref = bf16[16,8,640]{2,1,0:T(8,128)(2,1)S(1)} collective-permute-done((bf16[16,8,640]{2,1,0:T(8,128)(2,1)S(1)}, bf16[16,8,640]{2,1,0:T(8,128)(2,1)S(1)}, u32[]{:S(2)}, u32[]{:S(2)}) %collective-permute-start.1) | collective-permute-done | bytes 163872 | tf_op jit(solution)/shard_map/ppermute | solution.py:427
  58.0 11.6 %all_to_all.21.parts_ref = bf16[16,8,640]{2,1,0:T(8,128)(2,1)S(1)} all-to-all(bf16[16,8,640]{2,1,0:T(8,128)(2,1)S(1)} %add.1), channel_id=1, replica_groups=mesh['kv'=4,'z'=4,'core'=2] {'kv','z'}, dimensions={0} | all-to-all | bytes 327680 | tf_op jit(solution)/shard_map/all_to_all | solution.py:51
  69.5 0.6 finish.1
  (1 shorter events, 0.0 us)
Async XLA Ops:
  1.5 13.1 %all-to-all-start = ((bf16[8,8,1024]{2,1,0:T(8,128)(2,1)}), bf16[8,8,1024]{2,1,0:T(8,128)(2,1)S(1)}, u32[]{:S(2)}, u32[]{:S(2)}) async-start(bf16[8,8,1024]{2,1,0:T(8,128)(2,1)} %pack.1.after_ref), calls=%async_computation | async-start | bytes 262144 | tf_op jit(solution)/shard_map/all_to_all | solution.py:51
  16.6 9.6 %all-to-all-start.1 = ((bf16[8,8,768]{2,1,0:T(8,128)(2,1)}), bf16[8,8,768]{2,1,0:T(8,128)(2,1)S(1)}, u32[]{:S(2)}, u32[]{:S(2)}) async-start(bf16[8,8,768]{2,1,0:T(8,128)(2,1)} %bitcast.4), calls=%async_computation.1 | async-start | bytes 196608 | tf_op jit(solution)/shard_map/all_to_all | solution.py:51
  38.9 1.4 %collective-permute-start = (bf16[16,8,640]{2,1,0:T(8,128)(2,1)S(1)}, bf16[16,8,640]{2,1,0:T(8,128)(2,1)S(1)}, u32[]{:S(2)}, u32[]{:S(2)}) collective-permute-start(bf16[16,8,640]{2,1,0:T(8,128)(2,1)S(1)} %all_to_all.20.own_ref), channel_id=1, source_target_pairs={{0,1},{1,0},{2,3},{3,2},{4,5},{5,4},{6,7},{7,6},{8,9},{9,8},{10,11... | collective-permute-start | bytes 491528 | tf_op jit(solution)/shard_map/ppermute | solution.py:393
  56.5 1.5 %collective-permute-start.1 = (bf16[16,8,640]{2,1,0:T(8,128)(2,1)S(1)}, bf16[16,8,640]{2,1,0:T(8,128)(2,1)S(1)}, u32[]{:S(2)}, u32[]{:S(2)}) collective-permute-start(bf16[16,8,640]{2,1,0:T(8,128)(2,1)S(1)} %get-tuple-element.27), channel_id=1, source_target_pairs={{0,1},{1,0},{2,3},{3,2},{4,5},{5,4},{6,7},{7,6},{8,9},{9,8},{10,11... | collective-permute-start | bytes 491528 | tf_op jit(solution)/shard_map/ppermute | solution.py:427

commit v4 on v3

v4 whole, which is shorter than its diff:
```python
import functools
import math

import jax
import jax.numpy as jnp
from jax import lax
from jax.experimental import pallas as pl
from jax.experimental.pallas import tpu as pltpu
from jax.sharding import Mesh
from jax.sharding import PartitionSpec as P

HD = 128
E = 64
BEAMS = 8
BLK = 128
LANES = 128
MIB = 2**20
AHEAD = 6
EARLY = (2, 2)
SHIFTS = (3, 1, 2)
F32 = jnp.float32
BF16 = jnp.bfloat16
NT = (((1,), (1,)), ((), ()))
TN = (((0,), (0,)), ((), ()))
VMEM = pl.BlockSpec(memory_space=pltpu.VMEM)
SMEM = pl.BlockSpec(memory_space=pltpu.SMEM)
HBM = pl.BlockSpec(memory_space=pltpu.HBM)
ANY = pl.BlockSpec(memory_space=pl.ANY)
WIDE = ("z", "core")


def small(shape, dtype):
    return math.prod(shape) * jnp.dtype(dtype).itemsize <= MIB


def near(array):
    if small(array.shape, array.dtype):
        return pltpu.with_memory_space_constraint(array, pltpu.VMEM)
    return array


def far(array):
    return pltpu.with_memory_space_constraint(array, pltpu.HBM)


def result(shape, dtype):
    if small(shape, dtype):
        return pltpu.VMEM(shape, dtype)
    return jax.ShapeDtypeStruct(shape, dtype)


def sent(block, axes):
    return lax.all_to_all(block, axes, split_axis=0, concat_axis=0, tiled=True)


def pack_kernel(query_ref, new_ref, route_ref, out_ref):
    step_tok, steps, feats = query_ref.shape
    lanes = lax.broadcasted_iota(jnp.int32, (steps, LANES), 1)
    parts = []
    for t in range(step_tok):
        named = route_ref[t]
        chosen = jnp.zeros((steps, LANES), F32)
        for i in range(named.shape[1]):
            chosen = jnp.where(named[:, i : i + 1] == lanes, 1.0, chosen)
        parts.append(
            jnp.concatenate(
                [
                    query_ref[t].astype(F32),
                    new_ref[t, :, 0, :].astype(F32),
                    new_ref[t, :, 1, :].astype(F32),
                    chosen,
                ],
                axis=1,
            )
        )
    block = jnp.concatenate(parts, axis=0).astype(BF16)
    if len(out_ref.shape) == 2:
        out_ref[...] = block
    else:
        for w in range(out_ref.shape[0]):
            out_ref[w] = block


def stage_kernel(
    table_ref, length_ref, parent_ref, key_hbm, value_hbm, router_hbm, gain_hbm, query_ref,
    stream_ref, after_ref,
    key_ref, extended_ref, router_ref, gain_ref, valid_ref, own_ref, own_stream_ref, mask_ref, sems,
):
    del after_ref
    slots = key_ref.shape[0]
    groups, blocks = table_ref.shape
    copies = [
        pltpu.make_async_copy(key_hbm, key_ref, sems.at[0]),
        pltpu.make_async_copy(value_hbm, extended_ref.at[:, :, pl.ds(0, HD)], sems.at[1]),
        pltpu.make_async_copy(router_hbm, router_ref, sems.at[2]),
        pltpu.make_async_copy(gain_hbm, gain_ref, sems.at[3]),
    ]
    for copy in copies:
        copy.start()
    extended_ref[:, :, HD:] = jnp.ones((slots, BLK, HD), BF16)
    valid_ref[...] = jnp.zeros_like(valid_ref)
    first_slot = lax.axis_index(WIDE) * slots
    place = lax.broadcasted_iota(jnp.int32, (1, BLK), 1)

    def look(i, carry):
        group, block = i // blocks, i % blocks
        slot = table_ref[group, block] - first_slot

        @pl.when((slot >= 0) & (slot < slots))
        def _():
            limit = length_ref[group] - block * BLK
            valid_ref[group, pl.ds(slot, 1), :] = jnp.where(place < limit, 1.0, 0.0)

        return carry

    lax.fori_loop(0, groups * blocks, look, 0)
    step_tok, steps, feats = query_ref.shape
    rows = step_tok * steps
    heads = feats // HD
    own = jnp.concatenate([query_ref[t].astype(F32) for t in range(step_tok)], axis=0)
    stacked = jnp.concatenate([own[:, h * HD : (h + 1) * HD] for h in range(heads)], axis=0)
    own_ref[...] = stacked.astype(BF16)
    own_stream_ref[...] = jnp.concatenate(
        [stream_ref[t].astype(F32) for t in range(step_tok)], axis=0
    )
    first_token = lax.axis_index(WIDE) * step_tok
    row = lax.broadcasted_iota(jnp.int32, mask_ref.shape, 0) % rows
    column = lax.broadcasted_iota(jnp.int32, mask_ref.shape, 1)
    mask = jnp.zeros(mask_ref.shape, F32)
    for t in range(step_tok):
        token = first_token + t
        base = token // BEAMS * BEAMS
        for s in range(steps):
            ancestor = token
            for j in range(s, -1, -1):
                hit = (row == t * steps + s) & (column == ancestor * steps + j)
                mask = jnp.where(hit, 1.0, mask)
                if j > 0:
                    ancestor = base + parent_ref[j - 1, ancestor]
    mask_ref[...] = mask
    for copy in copies:
        copy.wait()


def attend_kernel(part_count, early_count, *refs):
    part_refs, refs = refs[:part_count], refs[part_count:]
    key_ref, extended_ref, valid_ref, own_ref, mask_ref, gate_hbm, up_hbm = refs[:7]
    out_ref, chosen_ref = refs[7:9]
    refs = refs[9:]
    early_copies = []
    if early_count:
        early_ref, early_sem = refs[0], refs[-1]
        refs = refs[1:]
        early_copies = [
            pltpu.make_async_copy((gate_hbm, up_hbm)[i % 2].at[i // 2], early_ref.at[i], early_sem.at[i])
            for i in range(early_count)
        ]
    for copy in early_copies:
        copy.start()
    query_ref, weight_ref, total_ref, rows_ref = refs[:4]
    if part_count == 1:
        for w in range(part_refs[0].shape[0]):
            count = part_refs[0].shape[1]
            rows_ref[w * count : (w + 1) * count, :] = part_refs[0][w].astype(F32)
    else:
        chip, core = lax.axis_index("z"), lax.axis_index("core")
        for k, ref in enumerate(part_refs):
            count = ref.shape[1]
            source = (chip + part_count - k) % part_count
            for i in range(2):
                side = core if i == 0 else 1 - core
                at = pl.ds(pl.multiple_of((source * 2 + side) * count, count), count)
                rows_ref[at, :] = ref[i].astype(F32)
    slots = key_ref.shape[0]
    groups = valid_ref.shape[0]
    stacked = query_ref.shape[0]
    feats = out_ref.shape[1] - LANES
    heads = feats // HD
    span = stacked // heads
    scale = 1.0 / math.sqrt(HD)

    def one_group(g, carry):
        rows = pl.ds(pl.multiple_of(g * span, span), span)
        for h in range(heads):
            query_ref[h * span : (h + 1) * span, :] = rows_ref[
                rows, h * HD : (h + 1) * HD
            ].astype(BF16)
        query = query_ref[...]
        for n in range(slots):
            scores = lax.dot_general(query, key_ref[n], NT, preferred_element_type=F32)
            weights = jnp.where(valid_ref[g, n : n + 1, :] > 0, jnp.exp(scores * scale), 0.0)
            weight_ref[:, n * BLK : (n + 1) * BLK] = weights.astype(BF16)
        sums = jnp.dot(
            weight_ref[...],
            extended_ref[...].reshape(slots * BLK, 2 * HD),
            preferred_element_type=F32,
        )
        for h in range(heads):
            total_ref[h, rows, :] = sums[h * span : (h + 1) * span, :]
        return carry

    lax.fori_loop(0, groups, one_group, 0, unroll=groups <= 2)
    chosen_ref[...] = rows_ref[:, feats + 2 * HD :]
    keys = rows_ref[:, feats : feats + HD].astype(BF16)
    values = rows_ref[:, feats + HD : feats + 2 * HD].astype(BF16)
    scores = lax.dot_general(own_ref[...], keys, NT, preferred_element_type=F32)
    weights = jnp.where(mask_ref[...] > 0, jnp.exp(scores * scale), 0.0).astype(BF16)
    extended = jnp.concatenate([values, jnp.ones_like(values)], axis=1)
    tail = jnp.dot(weights, extended, preferred_element_type=F32)
    rows = own_ref.shape[0] // heads
    mine = pl.ds(pl.multiple_of(lax.axis_index(WIDE) * rows, rows), rows)
    for h in range(heads):
        total_ref[h, mine, :] += tail[h * rows : (h + 1) * rows, :]
    lanes = lax.broadcasted_iota(jnp.int32, (span, LANES), 1)

    def pack_group(g, carry):
        rows = pl.ds(pl.multiple_of(g * span, span), span)
        last = jnp.zeros((span, LANES), F32)
        for h in range(heads):
            piece = total_ref[h, rows, :]
            out_ref[rows, h * HD : (h + 1) * HD] = piece[:, :HD].astype(BF16)
            high = piece[:, HD:].astype(BF16).astype(F32)
            last = jnp.where(lanes == h, high, last)
            last = jnp.where(lanes == heads + h, piece[:, HD:] - high, last)
        out_ref[rows, feats:] = last.astype(BF16)
        return carry

    lax.fori_loop(0, groups, pack_group, 0, unroll=groups <= 2)
    for copy in early_copies:
        copy.wait()


def normalise(side, pieces_ref, chosen_ref, gain_ref, router_ref, stack_ref, pick_ref, norm_ref, share_ref):
    kv_count, count, feats = stack_ref.shape
    pieces, rows, _ = pieces_ref.shape
    chips = pieces // kv_count

    def place(z, carry):
        to = pl.ds(pl.multiple_of(z * rows, rows), rows)
        source = pl.ds(pl.multiple_of((z * 2 + side) * rows, rows), rows)
        pick_ref[to, :] = chosen_ref[source, :]
        for k in range(kv_count):
            stack_ref[k, to, :] = pieces_ref[k * chips + z].astype(F32)
        return carry

    lax.fori_loop(0, chips, place, 0, unroll=chips <= 8)
    block = min(64, count)
    for b in range(count // block):
        at = slice(b * block, (b + 1) * block)
        squares = jnp.zeros((block, 1), F32)
        for k in range(kv_count):
            part = stack_ref[k, at, :]
            squares += jnp.sum(part * part, axis=1, keepdims=True)
        root = lax.rsqrt(squares / (kv_count * feats) + 1e-06)
        for k in range(kv_count):
            columns = slice(k * feats, (k + 1) * feats)
            part = stack_ref[k, at, :]
            norm_ref[at, columns] = (part * root * gain_ref[columns].reshape(1, feats)).astype(BF16)
        logits = lax.dot_general(norm_ref[at, :], router_ref[...], NT, preferred_element_type=F32)
        raised = jnp.where(pick_ref[at, :E] > 0, jnp.exp(logits), 0.0)
        share = raised / jnp.sum(raised, axis=1, keepdims=True)
        share = jnp.concatenate([share, jnp.zeros((block, LANES - E), F32)], axis=1)
        share_ref[:, at] = share.T


def fetch_kernel(skip, count, pieces_ref, chosen_ref, gain_ref, router_ref, gate_hbm, up_hbm, *refs):
    norm_ref, share_ref = refs[:2]
    copies = [
        pltpu.make_async_copy(
            (gate_hbm, up_hbm)[(i + skip) % 2].at[(i + skip) // 2], refs[2].at[i], refs[-1].at[i]
        )
        for i in range(count)
    ]
    for copy in copies:
        copy.start()
    stack_ref, pick_ref = refs[-3:-1]
    normalise(
        lax.axis_index("core"),
        pieces_ref, chosen_ref, gain_ref, router_ref, stack_ref, pick_ref, norm_ref, share_ref,
    )
    for copy in copies:
        copy.wait()


def residual_kernel(sums_ref, stream_ref, out_ref, spread_ref):
    rows, feats = out_ref.shape
    heads = feats // HD
    total = sums_ref[0].astype(F32)
    for w in range(1, sums_ref.shape[0]):
        total = total + sums_ref[w].astype(F32)
    dens = total[:, feats : feats + heads] + total[:, feats + heads : feats + 2 * heads]
    parts = []
    for h in range(heads):
        at = slice(h * HD, (h + 1) * HD)
        attended = total[:, at] / dens[:, h : h + 1]
        parts.append(stream_ref[:, at] + attended.astype(BF16).astype(F32))
    residual = jnp.concatenate(parts, axis=1).astype(BF16)
    out_ref[...] = residual
    for d in range(spread_ref.shape[0]):
        spread_ref[d] = residual


def expert_kernel(
    per_unit, early_count, pieces_ref, norm_own_ref, share_own_ref, chosen_ref, gain_ref, router_ref,
    gate_hbm, up_hbm, down_hbm, *refs,
):
    early_refs = refs[: len(early_count)]
    mine_ref, theirs_ref, slot_ref, stack_ref, pick_ref, norm_ref, half_ref, share_ref = refs[
        len(early_count) : len(early_count) + 8
    ]
    hidden_ref, total_ref, sems = refs[len(early_count) + 8 :]
    kv_count, both, feats = total_ref.shape
    count = both // 2
    pieces, rows, _ = pieces_ref.shape
    chips = pieces // kv_count
    units, width, _ = gate_hbm.shape
    sources = [ref.at[l] for l in range(units) for ref in (gate_hbm, up_hbm)]
    sources += [down_hbm.at[l] for l in range(units)]
    blocks = [ref.at[i] for ref in early_refs for i in range(ref.shape[0])]
    early = len(blocks)
    blocks += [slot_ref.at[i] for i in range(len(sources) - early)]
    copies = [
        pltpu.make_async_copy(sources[i], blocks[i], sems.at[i - early])
        for i in range(early, len(sources))
    ]
    for copy in copies[:AHEAD]:
        copy.start()

    def arrive(i):
        if i >= early:
            copies[i - early].wait()
            if i - early + AHEAD < len(copies):
                copies[i - early + AHEAD].start()

    normalise(
        1 - lax.axis_index("core"),
        pieces_ref, chosen_ref, gain_ref, router_ref, stack_ref, pick_ref, norm_ref, half_ref,
    )
    share_ref[:, :count] = share_own_ref[...]
    share_ref[:, count:] = half_ref[...]
    normed = jnp.concatenate([norm_own_ref[...], norm_ref[...]], axis=0)
    first_half = lax.axis_index(WIDE) * units * per_unit
    for l in range(units):
        arrive(2 * l)
        arrive(2 * l + 1)
        gate = lax.dot_general(blocks[2 * l][...], normed, NT, preferred_element_type=F32)
        up = lax.dot_general(blocks[2 * l + 1][...], normed, NT, preferred_element_type=F32)
        weight = share_ref[pl.ds((first_half + l * per_unit) // 2, 1), :]
        hidden_ref[l] = (gate / (1.0 + jnp.exp(-gate)) * up * weight).astype(BF16)
    for l in range(units):
        i = 2 * units + l
        arrive(i)
        for k in range(kv_count):
            columns = slice(k * feats, (k + 1) * feats)
            piece = lax.dot_general(
                hidden_ref[l], blocks[i][:, columns], TN, preferred_element_type=F32
            )
            total_ref[k] = piece if l == 0 else piece + total_ref[k]

    def hand_out(z, carry):
        for ref, start in ((mine_ref, 0), (theirs_ref, count)):
            at = pl.ds(pl.multiple_of(start + z * rows, rows), rows)
            for k in range(kv_count):
                ref[k * chips + z] = total_ref[k, at, :].astype(BF16)
        return carry

    lax.fori_loop(0, chips, hand_out, 0, unroll=chips <= 8)


def add_kernel(left_ref, right_ref, out_ref):
    for i in range(out_ref.shape[0]):
        out_ref[i] = (left_ref[i].astype(F32) + right_ref[i].astype(F32)).astype(BF16)


def finish_kernel(parts_ref, residual_ref, out_ref):
    total = parts_ref[0].astype(F32)
    for i in range(1, parts_ref.shape[0]):
        total = total + parts_ref[i].astype(F32)
    total = (residual_ref[...].astype(F32) + total).astype(BF16)
    step_tok, steps, _ = out_ref.shape
    for t in range(step_tok):
        out_ref[t] = total[t * steps : (t + 1) * steps]


def local(
    stream_in,
    queries,
    new_kv,
    cache_keys,
    cache_values,
    lengths,
    page_table,
    parents,
    routes,
    norm_gain,
    router,
    gate_w,
    up_w,
    down_w,
):
    kv_count = lax.axis_size("kv")
    chips = lax.axis_size("z")
    wide_count = lax.axis_size(WIDE)
    step_tok, steps, feats = stream_in.shape
    rows = step_tok * steps
    heads = feats // HD
    groups = lengths.shape[0]
    all_rows = groups * BEAMS * steps
    slots = cache_keys.shape[1]
    halves = gate_w.shape[0]
    half_width = gate_w.shape[2]
    width = kv_count * feats
    payload = feats + 2 * HD + LANES

    packed = pl.pallas_call(
        pack_kernel,
        out_shape=result((rows, payload) if chips <= 4 else (wide_count, rows, payload), BF16),
        in_specs=[VMEM] * 3,
        out_specs=VMEM,
        name="pack",
    )(queries, new_kv, routes)
    if chips <= 4:
        pair = jnp.stack([packed, lax.ppermute(packed, "core", ((0, 1), (1, 0)))])
        parts = {0: pair}
        for k in SHIFTS:
            if k < chips:
                parts[k] = lax.ppermute(pair, "z", [(i, (i + k) % chips) for i in range(chips)])
        parts = [near(parts[k]) for k in range(chips)]
    else:
        parts = [sent(packed, WIDE)]
    per_unit = 2 if halves % 2 == 0 else 1
    units = halves // per_unit
    unit_width = per_unit * half_width
    gate_rows = far(jnp.swapaxes(gate_w, 1, 2).reshape(units, unit_width, width))
    up_rows = far(jnp.swapaxes(up_w, 1, 2).reshape(units, unit_width, width))
    down_rows = far(down_w.reshape(units, unit_width, width))
    early_count = EARLY if 2 * units >= sum(EARLY) else ()

    keys, extended, router_rows, gain, valid, own_rows, stream, mask = pl.pallas_call(
        stage_kernel,
        out_shape=[
            result((slots, BLK, HD), BF16),
            result((slots, BLK, 2 * HD), BF16),
            result((E, width), BF16),
            result((width,), F32),
            result((groups, slots, BLK), F32),
            result((heads * rows, HD), BF16),
            result((rows, feats), F32),
            result((heads * rows, all_rows), F32),
        ],
        in_specs=[SMEM] * 3 + [HBM] * 4 + [VMEM] * 2 + [ANY],
        out_specs=[VMEM] * 8,
        scratch_shapes=[pltpu.SemaphoreType.DMA((4,))],
        compiler_params=pltpu.CompilerParams(vmem_limit_bytes=16 * MIB),
        name="stage",
    )(
        far(page_table),
        far(lengths),
        far(parents.T),
        far(cache_keys[0]),
        far(cache_values[0]),
        far(router.T),
        far(norm_gain),
        far(queries),
        far(stream_in),
        packed,
    )
    early_shapes = [pltpu.VMEM((n, unit_width, width), BF16) for n in early_count]
    sums, chosen, *early = pl.pallas_call(
        functools.partial(attend_kernel, len(parts), early_count[0] if early_count else 0),
        out_shape=[
            result((all_rows, feats + LANES), BF16),
            result((all_rows, LANES), F32),
            *early_shapes[:1],
        ],
        in_specs=[VMEM] * (len(parts) + 5) + [HBM] * 2,
        out_specs=[VMEM] * (2 + len(early_shapes[:1])),
        scratch_shapes=[
            pltpu.VMEM((BEAMS * steps * heads, HD), BF16),
            pltpu.VMEM((BEAMS * steps * heads, slots * BLK), BF16),
            pltpu.VMEM((heads, all_rows, 2 * HD), F32),
            pltpu.VMEM((all_rows, payload), F32),
            pltpu.SemaphoreType.DMA((max(early_count[:1], default=1),)),
        ],
        compiler_params=pltpu.CompilerParams(vmem_limit_bytes=32 * MIB),
        name="attend",
    )(
        *parts, near(keys), near(extended), near(valid), near(own_rows), near(mask),
        gate_rows, up_rows,
    )
    arrived = sent(sums.reshape(wide_count, rows, feats + LANES), WIDE)
    residual, copies = pl.pallas_call(
        residual_kernel,
        out_shape=[
            result((rows, feats), BF16),
            result((kv_count * chips, rows, feats), BF16),
        ],
        in_specs=[VMEM] * 2,
        out_specs=[VMEM] * 2,
        compiler_params=pltpu.CompilerParams(vmem_limit_bytes=8 * MIB),
        name="residual",
    )(near(arrived), near(stream))

    own = sent(copies, ("kv", "z"))
    other = lax.ppermute(own, "core", ((0, 1), (1, 0)))
    half = all_rows // 2
    norm_own, share_own, *more = pl.pallas_call(
        functools.partial(fetch_kernel, *(early_count or (0, 0))),
        out_shape=[result((half, width), BF16), result((LANES, half), F32), *early_shapes[1:]],
        in_specs=[VMEM] * 4 + [HBM] * 2,
        out_specs=[VMEM] * (2 + len(early_shapes[1:])),
        scratch_shapes=[
            pltpu.VMEM((kv_count, half, feats), F32),
            pltpu.VMEM((half, LANES), F32),
            pltpu.SemaphoreType.DMA((max(early_count[1:], default=1),)),
        ],
        compiler_params=pltpu.CompilerParams(vmem_limit_bytes=16 * MIB),
        name="fetch",
    )(near(own), near(chosen), near(gain), near(router_rows), gate_rows, up_rows)
    early = early + more
    mine, theirs = pl.pallas_call(
        functools.partial(expert_kernel, per_unit, early_count),
        out_shape=[result((kv_count * chips, rows, feats), BF16)] * 2,
        in_specs=[VMEM] * 6 + [HBM] * 3 + [VMEM] * len(early),
        out_specs=[VMEM] * 2,
        scratch_shapes=[
            pltpu.VMEM((3 * units - sum(early_count), unit_width, width), BF16),
            pltpu.VMEM((kv_count, half, feats), F32),
            pltpu.VMEM((half, LANES), F32),
            pltpu.VMEM((half, width), BF16),
            pltpu.VMEM((LANES, half), F32),
            pltpu.VMEM((LANES, all_rows), F32),
            pltpu.VMEM((units, unit_width, all_rows), BF16),
            pltpu.VMEM((kv_count, all_rows, feats), F32),
            pltpu.SemaphoreType.DMA((3 * units,)),
        ],
        compiler_params=pltpu.CompilerParams(vmem_limit_bytes=46 * MIB),
        cost_estimate=pl.CostEstimate(
            flops=6 * all_rows * halves * half_width * width,
            bytes_accessed=6 * halves * half_width * width,
            transcendentals=0,
        ),
        name="experts",
    )(
        near(other),
        near(norm_own),
        near(share_own),
        near(chosen),
        near(gain),
        near(router_rows),
        gate_rows,
        up_rows,
        down_rows,
        *[pltpu.with_memory_space_constraint(block, pltpu.VMEM) for block in early],
    )
    swapped = lax.ppermute(theirs, "core", ((0, 1), (1, 0)))
    both = pl.pallas_call(
        add_kernel,
        out_shape=result(mine.shape, BF16),
        in_specs=[VMEM] * 2,
        out_specs=VMEM,
        name="add",
    )(near(mine), near(swapped))
    returned = sent(both, ("kv", "z"))
    return pl.pallas_call(
        finish_kernel,
        out_shape=jax.ShapeDtypeStruct(stream_in.shape, BF16),
        in_specs=[VMEM] * 2,
        out_specs=VMEM,
        name="finish",
    )(near(returned), near(residual))


def solution(mesh):
    kv_count, wide_count = mesh.devices.shape
    split = Mesh(mesh.devices.reshape(kv_count, wide_count // 2, 2), ("kv",) + WIDE)
    return jax.shard_map(
        local,
        mesh=split,
        in_specs=(
            P(WIDE, None, "kv"),
            P(WIDE, None, "kv"),
            P(WIDE, None, None, "kv"),
            P("kv", WIDE, None, None),
            P("kv", WIDE, None, None),
            P(),
            P(),
            P(),
            P(WIDE, None, None),
            P(),
            P(),
            P(WIDE, None, "kv"),
            P(WIDE, None, "kv"),
            P(WIDE, "kv", None),
        ),
        out_specs=P(WIDE, None, "kv"),
        check_vma=False,
    )
```

time: 70.7 us -> 67.7 us (0.958)
  blocking collectives: 24 us -> 32.9 us
  waiting for transfers between devices: 12.4 us -> 4.05 us
  starting transfers between devices: 9.92 us -> 7.05 us
    all_to_all x2 -> x0, waiting for transfers between devices: 9.79 us -> none  [sent(): return lax.all_to_all(block, axes, split_axis=0, concat_axis=0, tiled=True)]
    all_to_all x2 -> x0, starting transfers between devices: 9.69 us -> none  [sent(): return lax.all_to_all(block, axes, split_axis=0, concat_axis=0, tiled=True)]
    all_to_all x2 -> x3, blocking collectives: 24 us -> 32.9 us  [sent(): return lax.all_to_all(block, axes, split_axis=0, concat_axis=0, tiled=True)]
    ppermute x0 -> x4, starting transfers between devices: none -> 6.47 us  [the longest x3 5.95 us: local(): lax.ppermute(pair, 'z', [(i, (i + k) % chips) for i in range(chips)])]
    ppermute x0 -> x4, waiting for transfers between devices: none -> 3.02 us  [the longest x3 2.18 us: local(): lax.ppermute(pair, 'z', [(i, (i + k) % chips) for i in range(chips)])]
    ppermute x1, waiting for transfers between devices: 1.39 us -> 0.01 us  [local(): other = lax.ppermute(own, 'core', ((0, 1), (1, 0)))]
    pallas_call x4, Pallas kernels: 20.7 us -> 19.9 us  [the longest x1 14.7 us: local(): pl.pallas_call(functools.partial(expert_kernel, per_unit, early_count), o...]
  transfers between devices with their start and end apart: 4 -> 6, of which waited for: 4 -> 4; matrix products, arithmetic and copies ran while one was open for 0% -> 0% of each run, Pallas kernels for 5% -> 7%
where the time goes in v4:
time: 67.7 us; the launch traced here: 67.4 us
  blocking collectives  32.9 us (49%)
  Pallas kernels  23.3 us (34%)
  starting transfers between devices  7.05 us (10%)
  waiting for transfers between devices  4.05 us (6%)
    all_to_all x3, blocking collectives, sent(): return lax.all_to_all(block, axes, split_axis=0, concat_axis=0, tiled=True)  32.9 us
    pallas_call x1, Pallas kernels, local(): pl.pallas_call(functools.partial(expert_kernel, per_unit, early_count), o...  14.7 us
    ppermute x3, starting transfers between devices, local(): lax.ppermute(pair, 'z', [(i, (i + k) % chips) for i in range(chips)])  5.95 us
    pallas_call x1, Pallas kernels, local(): pl.pallas_call(stage_kernel, out_shape=[result((slots, BLK, HD), BF16), r...  2.51 us
    pallas_call x1, Pallas kernels, local(): pl.pallas_call(functools.partial(fetch_kernel, *(early_count or (0, 0))),...  2.19 us
    pallas_call x1, Pallas kernels, local(): pl.pallas_call(functools.partial(attend_kernel, len(parts), early_count[0...  2.19 us
    ppermute x3, waiting for transfers between devices, local(): lax.ppermute(pair, 'z', [(i, (i + k) % chips) for i in range(chips)])  2.18 us
  transfers between devices with their start and end apart: 6, of which 4 were waited for; matrix products, arithmetic and copies ran while one was open for 0% of the time, Pallas kernels for 7%

profile of v4, /device:TPU:0, one launch (start us, length us, event | category | flops | bytes accessed | tf_op | source)
XLA Modules:
  0.0 67.4 jit_solution(16409294062135342833)
XLA Ops:
  0.0 0.8 %pack.1.after_ref = bf16[8,1024]{1,0:T(8,128)(2,1)S(1)} custom-call(bf16[2,4,640]{2,1,0:T(4,128)(2,1)} %query_ref.3, bf16[2,4,2,128]{3,2,1,0:T(2,128)(2,1)} %new_ref.1, s32[2,4,6]{2,1,0:T(4,128)} %route_ref.1), custom_call_target="tpu_custom_call" | custom-call | tf_op jit(solution)/shard_map/pack/pallas_call | solution.py:415
  0.8 0.5 collective-permute-start
  1.3 0.8 %collective-permute-done = bf16[8,1024]{1,0:T(8,128)(2,1)S(1)} collective-permute-done((bf16[8,1024]{1,0:T(8,128)(2,1)S(1)}, bf16[8,1024]{1,0:T(8,128)(2,1)S(1)}, u32[]{:S(2)}, u32[]{:S(2)}) %collective-permute-start) | collective-permute-done | bytes 16416 | tf_op jit(solution)/shard_map/ppermute | solution.py:423
  2.2 4.9 %collective-permute-start.3 = (bf16[2,8,1024]{2,1,0:T(8,128)(2,1)S(1)}, bf16[2,8,1024]{2,1,0:T(8,128)(2,1)S(1)}, u32[]{:S(2)}, u32[]{:S(2)}) collective-permute-start(bf16[2,8,1024]{2,1,0:T(8,128)(2,1)S(1)} %pad_maximum_fusion.refs_0_), channel_id=1, source_target_pairs={{0,6},{2,0},{4,2},{6,4},{1,7},{3,1},{5,3},{7,5},{8,14},{10,8},{12,... | collective-permute-start | bytes 98312 | tf_op jit(solution)/shard_map/ppermute | solution.py:427
  7.1 0.0 collective-permute-start.2
  7.1 1.0 %collective-permute-start.1 = (bf16[2,8,1024]{2,1,0:T(8,128)(2,1)S(1)}, bf16[2,8,1024]{2,1,0:T(8,128)(2,1)S(1)}, u32[]{:S(2)}, u32[]{:S(2)}) collective-permute-start(bf16[2,8,1024]{2,1,0:T(8,128)(2,1)S(1)} %pad_maximum_fusion.refs_0_), channel_id=1, source_target_pairs={{0,2},{2,4},{4,6},{6,0},{1,3},{3,5},{5,7},{7,1},{8,10},{10,12},{12... | collective-permute-start | bytes 98312 | tf_op jit(solution)/shard_map/ppermute | solution.py:427
  8.1 2.5 %stage.1 = (bf16[16,128,128]{2,1,0:T(8,128)(2,1)S(1)}, bf16[16,128,256]{2,1,0:T(8,128)(2,1)S(1)}, bf16[64,2560]{1,0:T(8,128)(2,1)S(1)}, f32[2560]{0:T(1024)S(1)}...) custom-call(s32[2,32]{1,0:T(2,128)} %table_ref.1, ...), custom_call_target="tpu_custom_call" | custom-call | tf_op jit(solution)/shard_map/stage/pallas_call | solution.py:439
  10.6 0.0 collective-permute-done.3.refs_3_
  10.7 1.4 %collective-permute-done.2.refs_2_ = bf16[2,8,1024]{2,1,0:T(8,128)(2,1)S(1)} collective-permute-done((bf16[2,8,1024]{2,1,0:T(8,128)(2,1)S(1)}, bf16[2,8,1024]{2,1,0:T(8,128)(2,1)S(1)}, u32[]{:S(2)}, u32[]{:S(2)}) %collective-permute-start.2) | collective-permute-done | bytes 32800 | tf_op jit(solution)/shard_map/ppermute | solution.py:427
  12.1 0.7 %collective-permute-done.1.refs_1_ = bf16[2,8,1024]{2,1,0:T(8,128)(2,1)S(1)} collective-permute-done((bf16[2,8,1024]{2,1,0:T(8,128)(2,1)S(1)}, bf16[2,8,1024]{2,1,0:T(8,128)(2,1)S(1)}, u32[]{:S(2)}, u32[]{:S(2)}) %collective-permute-start.1) | collective-permute-done | bytes 32800 | tf_op jit(solution)/shard_map/ppermute | solution.py:427
  12.8 2.2 %attend.1 = (bf16[64,768]{1,0:T(8,128)(2,1)S(1)}, f32[64,128]{1,0:T(8,128)S(1)}, bf16[2,384,2560]{2,1,0:T(8,128)(2,1)S(1)}) custom-call(bf16[2,8,1024]{2,1,0:T(8,128)(2,1)S(1)} %pad_maximum_fusion.refs_0_, bf16[2,8,1024]{2,1,0:T(8,128)(2,1)S(1)} %collective-permute-done.1.refs_1_, bf16[2,8,1024]{2,1,0:T(8,128)(2,1)S(1)} %collective-permute-done.2.refs_2_, ...), custom_call_target="tpu_custom_call" | custom-call | tf_op jit(solution)/shard_map/attend/pallas_call | solution.py:469
  15.0 8.7 %all_to_all.15.sums_ref = bf16[8,8,768]{2,1,0:T(8,128)(2,1)S(1)} all-to-all(bf16[8,8,768]{2,1,0:T(8,128)(2,1)S(1)} %bitcast.15), channel_id=1, replica_groups=mesh['kv'=4,'z'=4,'core'=2] {'z','core'}, dimensions={0} | all-to-all | bytes 196608 | tf_op jit(solution)/shard_map/all_to_all | solution.py:53
  23.8 0.2 residual.1
  23.9 12.4 %all_to_all.16.pieces_ref = bf16[16,8,640]{2,1,0:T(8,128)(2,1)S(1)} all-to-all(bf16[16,8,640]{2,1,0:T(8,128)(2,1)S(1)} %get-tuple-element.30), channel_id=1, replica_groups=mesh['kv'=4,'z'=4,'core'=2] {'kv','z'}, dimensions={0} | all-to-all | bytes 327680 | tf_op jit(solution)/shard_map/all_to_all | solution.py:53
  36.4 0.0 collective-permute-start.4
  36.4 2.2 %fetch.1 = (bf16[32,2560]{1,0:T(8,128)(2,1)S(1)}, f32[128,32]{1,0:T(8,128)S(1)}, bf16[2,384,2560]{2,1,0:T(8,128)(2,1)S(1)}) custom-call(bf16[16,8,640]{2,1,0:T(8,128)(2,1)S(1)} %all_to_all.16.pieces_ref, f32[64,128]{1,0:T(8,128)S(1)} %get-tuple-element.31.chosen_ref, f32[2560]{0:T(1024)S(1)} %get-tuple-element.32.gain_ref, ...), custom_call_target="tpu_custom_call" | custom-call | tf_op jit(solution)/shard_map/fetch/pallas_call | solution.py:507
  38.6 0.0 collective-permute-done.4.pieces_ref
  38.6 14.7 %experts.1 = (bf16[16,8,640]{2,1,0:T(8,128)(2,1)S(1)}, bf16[16,8,640]{2,1,0:T(8,128)(2,1)S(1)}) custom-call(bf16[16,8,640]{2,1,0:T(8,128)(2,1)S(1)} %collective-permute-done.4.pieces_ref, bf16[32,2560]{1,0:T(8,128)(2,1)S(1)} %get-tuple-element.34.norm_own_ref, f32[128,32]{1,0:T(8,128)S(1)} %get-tuple-element.35.share_own_ref, ...), custom_call_target="tpu_custom_call" | custom-call | flops 3019898880 | bytes 47185920 | tf_op jit(solution)/shard_map/experts/pallas_call | solution.py:521
  53.3 0.6 collective-permute-start.5
  53.9 1.0 %collective-permute-done.5.right_ref = bf16[16,8,640]{2,1,0:T(8,128)(2,1)S(1)} collective-permute-done((bf16[16,8,640]{2,1,0:T(8,128)(2,1)S(1)}, bf16[16,8,640]{2,1,0:T(8,128)(2,1)S(1)}, u32[]{:S(2)}, u32[]{:S(2)}) %collective-permute-start.5) | collective-permute-done | bytes 163872 | tf_op jit(solution)/shard_map/ppermute | solution.py:556
  55.0 11.8 %all_to_all.17.parts_ref = bf16[16,8,640]{2,1,0:T(8,128)(2,1)S(1)} all-to-all(bf16[16,8,640]{2,1,0:T(8,128)(2,1)S(1)} %add.1), channel_id=1, replica_groups=mesh['kv'=4,'z'=4,'core'=2] {'kv','z'}, dimensions={0} | all-to-all | bytes 327680 | tf_op jit(solution)/shard_map/all_to_all | solution.py:53
  66.7 0.6 finish.1
  (2 shorter events, 0.0 us)
Async XLA Ops:
  0.8 1.4 %collective-permute-start = (bf16[8,1024]{1,0:T(8,128)(2,1)S(1)}, bf16[8,1024]{1,0:T(8,128)(2,1)S(1)}, u32[]{:S(2)}, u32[]{:S(2)}) collective-permute-start(bf16[8,1024]{1,0:T(8,128)(2,1)S(1)} %pack.1.after_ref), channel_id=1, source_target_pairs={{0,1},{1,0},{2,3},{3,2},{4,5},{5,4},{6,7},{7,6},{8,9},{9,8},{10,11... | collective-permute-start | bytes 49160 | tf_op jit(solution)/shard_map/ppermute | solution.py:423
  2.2 8.5 %collective-permute-start.3 = (bf16[2,8,1024]{2,1,0:T(8,128)(2,1)S(1)}, bf16[2,8,1024]{2,1,0:T(8,128)(2,1)S(1)}, u32[]{:S(2)}, u32[]{:S(2)}) collective-permute-start(bf16[2,8,1024]{2,1,0:T(8,128)(2,1)S(1)} %pad_maximum_fusion.refs_0_), channel_id=1, source_target_pairs={{0,6},{2,0},{4,2},{6,4},{1,7},{3,1},{5,3},{7,5},{8,14},{10,8},{12,... | collective-permute-start | bytes 98312 | tf_op jit(solution)/shard_map/ppermute | solution.py:427
  7.1 5.0 %collective-permute-start.2 = (bf16[2,8,1024]{2,1,0:T(8,128)(2,1)S(1)}, bf16[2,8,1024]{2,1,0:T(8,128)(2,1)S(1)}, u32[]{:S(2)}, u32[]{:S(2)}) collective-permute-start(bf16[2,8,1024]{2,1,0:T(8,128)(2,1)S(1)} %pad_maximum_fusion.refs_0_), channel_id=1, source_target_pairs={{0,4},{2,6},{4,0},{6,2},{1,5},{3,7},{5,1},{7,3},{8,12},{10,14},{12... | collective-permute-start | bytes 98312 | tf_op jit(solution)/shard_map/ppermute | solution.py:427
  7.1 5.7 %collective-permute-start.1 = (bf16[2,8,1024]{2,1,0:T(8,128)(2,1)S(1)}, bf16[2,8,1024]{2,1,0:T(8,128)(2,1)S(1)}, u32[]{:S(2)}, u32[]{:S(2)}) collective-permute-start(bf16[2,8,1024]{2,1,0:T(8,128)(2,1)S(1)} %pad_maximum_fusion.refs_0_), channel_id=1, source_target_pairs={{0,2},{2,4},{4,6},{6,0},{1,3},{3,5},{5,7},{7,1},{8,10},{10,12},{12... | collective-permute-start | bytes 98312 | tf_op jit(solution)/shard_map/ppermute | solution.py:427
  36.4 2.2 %collective-permute-start.4 = (bf16[16,8,640]{2,1,0:T(8,128)(2,1)S(1)}, bf16[16,8,640]{2,1,0:T(8,128)(2,1)S(1)}, u32[]{:S(2)}, u32[]{:S(2)}) collective-permute-start(bf16[16,8,640]{2,1,0:T(8,128)(2,1)S(1)} %all_to_all.16.pieces_ref), channel_id=1, source_target_pairs={{0,1},{1,0},{2,3},{3,2},{4,5},{5,4},{6,7},{7,6},{8,9},{9,8},{10,11... | collective-permute-start | bytes 491528 | tf_op jit(solution)/shard_map/ppermute | solution.py:505
  53.3 1.6 %collective-permute-start.5 = (bf16[16,8,640]{2,1,0:T(8,128)(2,1)S(1)}, bf16[16,8,640]{2,1,0:T(8,128)(2,1)S(1)}, u32[]{:S(2)}, u32[]{:S(2)}) collective-permute-start(bf16[16,8,640]{2,1,0:T(8,128)(2,1)S(1)} %get-tuple-element.39), channel_id=1, source_target_pairs={{0,1},{1,0},{2,3},{3,2},{4,5},{5,4},{6,7},{7,6},{8,9},{9,8},{10,11... | collective-permute-start | bytes 491528 | tf_op jit(solution)/shard_map/ppermute | solution.py:556

commit v5 on v4

--- a/solution.py
+++ b/solution.py
@@ -16,14 +16,13 @@
 LANES = 128
 MIB = 2**20
 AHEAD = 6
-EARLY = (2, 2)
+EARLY = (0, 0, 1, 3, 1)
 SHIFTS = (3, 1, 2)
 F32 = jnp.float32
 BF16 = jnp.bfloat16
 NT = (((1,), (1,)), ((), ()))
 TN = (((0,), (0,)), ((), ()))
 VMEM = pl.BlockSpec(memory_space=pltpu.VMEM)
-SMEM = pl.BlockSpec(memory_space=pltpu.SMEM)
 HBM = pl.BlockSpec(memory_space=pltpu.HBM)
 ANY = pl.BlockSpec(memory_space=pl.ANY)
 WIDE = ("z", "core")
@@ -41,6 +40,10 @@
 
 def far(array):
     return pltpu.with_memory_space_constraint(array, pltpu.HBM)
+
+
+def pinned(array):
+    return pltpu.with_memory_space_constraint(array, pltpu.VMEM)
 
 
 def result(shape, dtype):
@@ -81,12 +84,32 @@
             out_ref[w] = block
 
 
+def early_copies(skip, count, gate_hbm, up_hbm, early_ref, sems):
+    return [
+        pltpu.make_async_copy(
+            (gate_hbm, up_hbm)[(i + skip) % 2].at[(i + skip) // 2], early_ref.at[i], sems.at[i]
+        )
+        for i in range(count)
+    ]
+
+
 def stage_kernel(
-    table_ref, length_ref, parent_ref, key_hbm, value_hbm, router_hbm, gain_hbm, query_ref,
-    stream_ref, after_ref,
-    key_ref, extended_ref, router_ref, gain_ref, valid_ref, own_ref, own_stream_ref, mask_ref, sems,
+    skip, count, table_hbm, length_hbm, parent_hbm, key_hbm, value_hbm, router_hbm, gain_hbm,
+    gate_hbm, up_hbm, query_hbm, stream_hbm, after_ref,
+    key_ref, extended_ref, router_ref, gain_ref, valid_ref, own_ref, own_stream_ref, mask_ref, *refs,
 ):
     del after_ref
+    table_ref, length_ref, parent_ref, query_ref, stream_ref, sems = refs[-7:-1]
+    early = early_copies(skip, count, gate_hbm, up_hbm, refs[0], refs[-1])
+    first = [
+        pltpu.make_async_copy(table_hbm, table_ref, sems.at[4]),
+        pltpu.make_async_copy(length_hbm, length_ref, sems.at[5]),
+        pltpu.make_async_copy(parent_hbm, parent_ref, sems.at[6]),
+        pltpu.make_async_copy(query_hbm, query_ref, sems.at[7]),
+        pltpu.make_async_copy(stream_hbm, stream_ref, sems.at[8]),
+    ]
+    for copy in first:
+        copy.start()
     slots = key_ref.shape[0]
     groups, blocks = table_ref.shape
     copies = [
@@ -95,25 +118,31 @@
         pltpu.make_async_copy(router_hbm, router_ref, sems.at[2]),
         pltpu.make_async_copy(gain_hbm, gain_ref, sems.at[3]),
     ]
-    for copy in copies:
+    for copy in copies + early:
         copy.start()
     extended_ref[:, :, HD:] = jnp.ones((slots, BLK, HD), BF16)
     valid_ref[...] = jnp.zeros_like(valid_ref)
+    for copy in first:
+        copy.wait()
     first_slot = lax.axis_index(WIDE) * slots
     place = lax.broadcasted_iota(jnp.int32, (1, BLK), 1)
 
-    def look(i, carry):
-        group, block = i // blocks, i % blocks
-        slot = table_ref[group, block] - first_slot
-
-        @pl.when((slot >= 0) & (slot < slots))
-        def _():
-            limit = length_ref[group] - block * BLK
-            valid_ref[group, pl.ds(slot, 1), :] = jnp.where(place < limit, 1.0, 0.0)
-
+    def look_group(group, carry):
+        length = length_ref[group]
+
+        def look(block, limit):
+            slot = table_ref[group, block] - first_slot
+
+            @pl.when((slot >= 0) & (slot < slots))
+            def _():
+                valid_ref[group, pl.ds(slot, 1), :] = jnp.where(place < limit, 1.0, 0.0)
+
+            return limit - BLK
+
+        lax.fori_loop(0, blocks, look, length, unroll=4)
         return carry
 
-    lax.fori_loop(0, groups * blocks, look, 0)
+    lax.fori_loop(0, groups, look_group, 0, unroll=groups <= 2)
     step_tok, steps, feats = query_ref.shape
     rows = step_tok * steps
     heads = feats // HD
@@ -124,7 +153,7 @@
         [stream_ref[t].astype(F32) for t in range(step_tok)], axis=0
     )
     first_token = lax.axis_index(WIDE) * step_tok
-    row = lax.broadcasted_iota(jnp.int32, mask_ref.shape, 0) % rows
+    row = jnp.concatenate([lax.broadcasted_iota(jnp.int32, (rows, mask_ref.shape[1]), 0)] * heads, axis=0)
     column = lax.broadcasted_iota(jnp.int32, mask_ref.shape, 1)
     mask = jnp.zeros(mask_ref.shape, F32)
     for t in range(step_tok):
@@ -138,25 +167,56 @@
                 if j > 0:
                     ancestor = base + parent_ref[j - 1, ancestor]
     mask_ref[...] = mask
+    for copy in copies + early:
+        copy.wait()
+
+
+def with_denominators(numerators, denominators):
+    lanes = lax.broadcasted_iota(jnp.int32, (numerators[0].shape[0], LANES), 1)
+    heads = len(numerators)
+    last = jnp.zeros(lanes.shape, F32)
+    for h, denominator in enumerate(denominators):
+        high = denominator.astype(BF16).astype(F32)
+        last = jnp.where(lanes == h, high, last)
+        last = jnp.where(lanes == heads + h, denominator - high, last)
+    return jnp.concatenate(numerators + [last], axis=1).astype(BF16)
+
+
+def denominators_of(total, feats):
+    heads = feats // HD
+    return total[:, feats : feats + heads] + total[:, feats + heads : feats + 2 * heads]
+
+
+def bring_kernel(skip, count, after_ref, gate_hbm, up_hbm, early_ref, sems):
+    del after_ref
+    copies = early_copies(skip, count, gate_hbm, up_hbm, early_ref, sems)
+    for copy in copies:
+        copy.start()
     for copy in copies:
         copy.wait()
 
 
-def attend_kernel(part_count, early_count, *refs):
+def merge_kernel(held, left_ref, right_ref, *out_refs):
+    out_refs = out_refs[held:]
+    feats = left_ref.shape[2] - LANES
+    for k, ref in enumerate(out_refs):
+        total = left_ref[k].astype(F32) + right_ref[k].astype(F32)
+        dens = denominators_of(total, feats)
+        ref[...] = with_denominators(
+            [total[:, h * HD : (h + 1) * HD] for h in range(feats // HD)],
+            [dens[:, h : h + 1] for h in range(feats // HD)],
+        )
+
+
+def attend_kernel(part_count, skip, count, *refs):
     part_refs, refs = refs[:part_count], refs[part_count:]
     key_ref, extended_ref, valid_ref, own_ref, mask_ref, gate_hbm, up_hbm = refs[:7]
-    out_ref, chosen_ref = refs[7:9]
-    refs = refs[9:]
-    early_copies = []
-    if early_count:
-        early_ref, early_sem = refs[0], refs[-1]
-        refs = refs[1:]
-        early_copies = [
-            pltpu.make_async_copy((gate_hbm, up_hbm)[i % 2].at[i // 2], early_ref.at[i], early_sem.at[i])
-            for i in range(early_count)
-        ]
-    for copy in early_copies:
+    outs = 1 if part_count == 1 else 2
+    out_refs, chosen_ref, refs = refs[7 : 7 + outs], refs[7 + outs], refs[8 + outs :]
+    early = early_copies(skip, count, gate_hbm, up_hbm, refs[0], refs[-1])
+    for copy in early:
         copy.start()
+    refs = refs[1 if count else 0 :]
     query_ref, weight_ref, total_ref, rows_ref = refs[:4]
     if part_count == 1:
         for w in range(part_refs[0].shape[0]):
@@ -174,7 +234,7 @@
     slots = key_ref.shape[0]
     groups = valid_ref.shape[0]
     stacked = query_ref.shape[0]
-    feats = out_ref.shape[1] - LANES
+    feats = out_refs[0].shape[-1] - LANES
     heads = feats // HD
     span = stacked // heads
     scale = 1.0 / math.sqrt(HD)
@@ -211,22 +271,28 @@
     mine = pl.ds(pl.multiple_of(lax.axis_index(WIDE) * rows, rows), rows)
     for h in range(heads):
         total_ref[h, mine, :] += tail[h * rows : (h + 1) * rows, :]
-    lanes = lax.broadcasted_iota(jnp.int32, (span, LANES), 1)
-
-    def pack_group(g, carry):
-        rows = pl.ds(pl.multiple_of(g * span, span), span)
-        last = jnp.zeros((span, LANES), F32)
-        for h in range(heads):
-            piece = total_ref[h, rows, :]
-            out_ref[rows, h * HD : (h + 1) * HD] = piece[:, :HD].astype(BF16)
-            high = piece[:, HD:].astype(BF16).astype(F32)
-            last = jnp.where(lanes == h, high, last)
-            last = jnp.where(lanes == heads + h, piece[:, HD:] - high, last)
-        out_ref[rows, feats:] = last.astype(BF16)
-        return carry
-
-    lax.fori_loop(0, groups, pack_group, 0, unroll=groups <= 2)
-    for copy in early_copies:
+
+    if part_count == 1:
+
+        def pack_group(g, carry):
+            rows = pl.ds(pl.multiple_of(g * span, span), span)
+            out_refs[0][rows, :] = with_denominators(
+                [total_ref[h, rows, :HD] for h in range(heads)],
+                [total_ref[h, rows, HD:] for h in range(heads)],
+            )
+            return carry
+
+        lax.fori_loop(0, groups, pack_group, 0, unroll=groups <= 2)
+    else:
+        for k in range(part_count):
+            target = (chip + k) % part_count
+            for ref, side in zip(out_refs, (core, 1 - core), strict=True):
+                at = pl.ds(pl.multiple_of((target * 2 + side) * rows, rows), rows)
+                ref[k] = with_denominators(
+                    [total_ref[h, at, :HD] for h in range(heads)],
+                    [total_ref[h, at, HD:] for h in range(heads)],
+                )
+    for copy in early:
         copy.wait()
 
 
@@ -265,12 +331,7 @@
 
 def fetch_kernel(skip, count, pieces_ref, chosen_ref, gain_ref, router_ref, gate_hbm, up_hbm, *refs):
     norm_ref, share_ref = refs[:2]
-    copies = [
-        pltpu.make_async_copy(
-            (gate_hbm, up_hbm)[(i + skip) % 2].at[(i + skip) // 2], refs[2].at[i], refs[-1].at[i]
-        )
-        for i in range(count)
-    ]
+    copies = early_copies(skip, count, gate_hbm, up_hbm, refs[2], refs[-1])
     for copy in copies:
         copy.start()
     stack_ref, pick_ref = refs[-3:-1]
@@ -282,13 +343,19 @@
         copy.wait()
 
 
-def residual_kernel(sums_ref, stream_ref, out_ref, spread_ref):
+def residual_kernel(part_count, *refs):
+    part_refs, stream_ref = refs[:part_count], refs[part_count]
+    out_ref, spread_ref = refs[-2:]
     rows, feats = out_ref.shape
     heads = feats // HD
-    total = sums_ref[0].astype(F32)
-    for w in range(1, sums_ref.shape[0]):
-        total = total + sums_ref[w].astype(F32)
-    dens = total[:, feats : feats + heads] + total[:, feats + heads : feats + 2 * heads]
+    if part_count == 1:
+        blocks = [part_refs[0][w] for w in range(part_refs[0].shape[0])]
+    else:
+        blocks = [ref[...] for ref in part_refs]
+    total = blocks[0].astype(F32)
+    for block in blocks[1:]:
+        total = total + block.astype(F32)
+    dens = denominators_of(total, feats)
     parts = []
     for h in range(heads):
         at = slice(h * HD, (h + 1) * HD)
@@ -304,11 +371,11 @@
     per_unit, early_count, pieces_ref, norm_own_ref, share_own_ref, chosen_ref, gain_ref, router_ref,
     gate_hbm, up_hbm, down_hbm, *refs,
 ):
-    early_refs = refs[: len(early_count)]
+    early_refs = refs[:early_count]
     mine_ref, theirs_ref, slot_ref, stack_ref, pick_ref, norm_ref, half_ref, share_ref = refs[
-        len(early_count) : len(early_count) + 8
+        early_count : early_count + 8
     ]
-    hidden_ref, total_ref, sems = refs[len(early_count) + 8 :]
+    hidden_ref, total_ref, sems = refs[early_count + 8 :]
     kv_count, both, feats = total_ref.shape
     count = both // 2
     pieces, rows, _ = pieces_ref.shape
@@ -434,10 +501,13 @@
     gate_rows = far(jnp.swapaxes(gate_w, 1, 2).reshape(units, unit_width, width))
     up_rows = far(jnp.swapaxes(up_w, 1, 2).reshape(units, unit_width, width))
     down_rows = far(down_w.reshape(units, unit_width, width))
-    early_count = EARLY if 2 * units >= sum(EARLY) else ()
-
-    keys, extended, router_rows, gain, valid, own_rows, stream, mask = pl.pallas_call(
-        stage_kernel,
+    early_count = EARLY if 2 * units >= sum(EARLY) else (0,) * len(EARLY)
+    skips = [sum(early_count[:i]) for i in range(len(EARLY))]
+    shapes = [[pltpu.VMEM((n, unit_width, width), BF16)] if n else [] for n in early_count]
+    early_sems = [pltpu.SemaphoreType.DMA((max(n, 1),)) for n in early_count]
+
+    keys, extended, router_rows, gain, valid, own_rows, stream, mask, *early = pl.pallas_call(
+        functools.partial(stage_kernel, skips[0], early_count[0]),
         out_shape=[
             result((slots, BLK, HD), BF16),
             result((slots, BLK, 2 * HD), BF16),
@@ -447,10 +517,19 @@
             result((heads * rows, HD), BF16),
             result((rows, feats), F32),
             result((heads * rows, all_rows), F32),
+            *shapes[0],
         ],
-        in_specs=[SMEM] * 3 + [HBM] * 4 + [VMEM] * 2 + [ANY],
-        out_specs=[VMEM] * 8,
-        scratch_shapes=[pltpu.SemaphoreType.DMA((4,))],
+        in_specs=[HBM] * 11 + [ANY],
+        out_specs=[VMEM] * (8 + len(shapes[0])),
+        scratch_shapes=[
+            pltpu.SMEM(page_table.shape, jnp.int32),
+            pltpu.SMEM(lengths.shape, jnp.int32),
+            pltpu.SMEM(parents.shape[::-1], jnp.int32),
+            pltpu.VMEM(queries.shape, BF16),
+            pltpu.VMEM(stream_in.shape, BF16),
+            pltpu.SemaphoreType.DMA((9,)),
+            early_sems[0],
+        ],
         compiler_params=pltpu.CompilerParams(vmem_limit_bytes=16 * MIB),
         name="stage",
     )(
@@ -461,26 +540,31 @@
         far(cache_values[0]),
         far(router.T),
         far(norm_gain),
+        gate_rows,
+        up_rows,
         far(queries),
         far(stream_in),
         packed,
     )
-    early_shapes = [pltpu.VMEM((n, unit_width, width), BF16) for n in early_count]
-    sums, chosen, *early = pl.pallas_call(
-        functools.partial(attend_kernel, len(parts), early_count[0] if early_count else 0),
+    near_chips = chips <= 4
+    if near_chips:
+        sum_shapes = [result((chips, rows, feats + LANES), BF16)] * 2
+    else:
+        sum_shapes = [result((all_rows, feats + LANES), BF16)]
+    *sums, chosen = pl.pallas_call(
+        functools.partial(attend_kernel, len(parts), skips[1], early_count[1]),
         out_shape=[
-            result((all_rows, feats + LANES), BF16),
+            *sum_shapes,
             result((all_rows, LANES), F32),
-            *early_shapes[:1],
         ],
         in_specs=[VMEM] * (len(parts) + 5) + [HBM] * 2,
-        out_specs=[VMEM] * (2 + len(early_shapes[:1])),
+        out_specs=[VMEM] * (len(sum_shapes) + 1),
         scratch_shapes=[
             pltpu.VMEM((BEAMS * steps * heads, HD), BF16),
             pltpu.VMEM((BEAMS * steps * heads, slots * BLK), BF16),
             pltpu.VMEM((heads, all_rows, 2 * HD), F32),
             pltpu.VMEM((all_rows, payload), F32),
-            pltpu.SemaphoreType.DMA((max(early_count[:1], default=1),)),
+            early_sems[1],
         ],
         compiler_params=pltpu.CompilerParams(vmem_limit_bytes=32 * MIB),
         name="attend",
@@ -488,38 +572,78 @@
         *parts, near(keys), near(extended), near(valid), near(own_rows), near(mask),
         gate_rows, up_rows,
     )
-    arrived = sent(sums.reshape(wide_count, rows, feats + LANES), WIDE)
+
+    def bring(i, after):
+        if not early_count[i]:
+            return []
+        return [
+            pl.pallas_call(
+                functools.partial(bring_kernel, skips[i], early_count[i]),
+                out_shape=shapes[i],
+                in_specs=[ANY, HBM, HBM],
+                out_specs=[VMEM],
+                scratch_shapes=[early_sems[i]],
+                compiler_params=pltpu.CompilerParams(vmem_limit_bytes=MIB),
+                name="bring",
+            )(after, gate_rows, up_rows)[0]
+        ]
+
+    if near_chips:
+        kept, passed = sums
+        passed = lax.ppermute(passed, "core", ((0, 1), (1, 0)))
+        brought = [pinned(block) for block in bring(2, kept)]
+        early = early + brought
+        merged = pl.pallas_call(
+            functools.partial(merge_kernel, len(brought)),
+            out_shape=[result((rows, feats + LANES), BF16)] * chips,
+            in_specs=[VMEM] * 2 + [ANY] * len(brought),
+            out_specs=[VMEM] * chips,
+            compiler_params=pltpu.CompilerParams(vmem_limit_bytes=4 * MIB),
+            name="merge",
+        )(near(kept), near(passed), *brought)
+        arrived = [near(merged[0])]
+        for k in SHIFTS:
+            if k < chips:
+                pairs = [(i, (i + k) % chips) for i in range(chips)]
+                arrived.append(near(lax.ppermute(merged[k], "z", pairs)))
+        brought = [pinned(block) for block in bring(3, merged[0])]
+        early = early + brought
+    else:
+        brought = []
+        arrived = [near(sent(sums[0].reshape(wide_count, rows, feats + LANES), WIDE))]
     residual, copies = pl.pallas_call(
-        residual_kernel,
+        functools.partial(residual_kernel, len(arrived)),
         out_shape=[
             result((rows, feats), BF16),
             result((kv_count * chips, rows, feats), BF16),
         ],
-        in_specs=[VMEM] * 2,
+        in_specs=[VMEM] * (len(arrived) + 1) + [ANY] * len(brought),
         out_specs=[VMEM] * 2,
         compiler_params=pltpu.CompilerParams(vmem_limit_bytes=8 * MIB),
         name="residual",
-    )(near(arrived), near(stream))
+    )(*arrived, near(stream), *brought)
 
     own = sent(copies, ("kv", "z"))
     other = lax.ppermute(own, "core", ((0, 1), (1, 0)))
     half = all_rows // 2
+    waiting = (3 * units - sum(early_count)) * unit_width * width * 2
+    expert_room = waiting + 20 * all_rows * width + 4 * MIB
     norm_own, share_own, *more = pl.pallas_call(
-        functools.partial(fetch_kernel, *(early_count or (0, 0))),
-        out_shape=[result((half, width), BF16), result((LANES, half), F32), *early_shapes[1:]],
+        functools.partial(fetch_kernel, skips[4], early_count[4]),
+        out_shape=[result((half, width), BF16), result((LANES, half), F32), *shapes[4]],
         in_specs=[VMEM] * 4 + [HBM] * 2,
-        out_specs=[VMEM] * (2 + len(early_shapes[1:])),
+        out_specs=[VMEM] * (2 + len(shapes[4])),
         scratch_shapes=[
             pltpu.VMEM((kv_count, half, feats), F32),
             pltpu.VMEM((half, LANES), F32),
-            pltpu.SemaphoreType.DMA((max(early_count[1:], default=1),)),
+            early_sems[4],
         ],
         compiler_params=pltpu.CompilerParams(vmem_limit_bytes=16 * MIB),
         name="fetch",
     )(near(own), near(chosen), near(gain), near(router_rows), gate_rows, up_rows)
     early = early + more
     mine, theirs = pl.pallas_call(
-        functools.partial(expert_kernel, per_unit, early_count),
+        functools.partial(expert_kernel, per_unit, len(early)),
         out_shape=[result((kv_count * chips, rows, feats), BF16)] * 2,
         in_specs=[VMEM] * 6 + [HBM] * 3 + [VMEM] * len(early),
         out_specs=[VMEM] * 2,
@@ -534,7 +658,7 @@
             pltpu.VMEM((kv_count, all_rows, feats), F32),
             pltpu.SemaphoreType.DMA((3 * units,)),
         ],
-        compiler_params=pltpu.CompilerParams(vmem_limit_bytes=46 * MIB),
+        compiler_params=pltpu.CompilerParams(vmem_limit_bytes=expert_room),
         cost_estimate=pl.CostEstimate(
             flops=6 * all_rows * halves * half_width * width,
             bytes_accessed=6 * halves * half_width * width,
@@ -551,7 +675,7 @@
         gate_rows,
         up_rows,
         down_rows,
-        *[pltpu.with_memory_space_constraint(block, pltpu.VMEM) for block in early],
+        *[pinned(block) for block in early],
     )
     swapped = lax.ppermute(theirs, "core", ((0, 1), (1, 0)))
     both = pl.pallas_call(

time: 67.7 us -> 66.5 us (0.982)
  blocking collectives: 32.9 us -> 25.1 us
  starting transfers between devices: 7.05 us -> 10.3 us
  Pallas kernels: 23.3 us -> 25 us
  waiting for transfers between devices: 4.05 us -> 5.6 us
    all_to_all x3 -> x2, blocking collectives: 32.9 us -> 25.1 us  [sent(): return lax.all_to_all(block, axes, split_axis=0, concat_axis=0, tiled=True)]
    ppermute x0 -> x4, starting transfers between devices: none -> 3.28 us  [the longest x3 3.21 us: local(): arrived.append(near(lax.ppermute(merged[k], 'z', pairs)))]
    pallas_call x5 -> x8, Pallas kernels: 21.8 us -> 23.5 us  [the longest x1 14.2 us: local(): pl.pallas_call(functools.partial(expert_kernel, per_unit, len(early)), ou...]
    ppermute x3, waiting for transfers between devices: 2.18 us -> 3.04 us  [local(): lax.ppermute(pair, 'z', [(i, (i + k) % chips) for i in range(chips)])]
    ppermute x0 -> x4, waiting for transfers between devices: none -> 0.69 us  [the longest x3 0.69 us: local(): arrived.append(near(lax.ppermute(merged[k], 'z', pairs)))]
  transfers between devices with their start and end apart: 6 -> 10, of which waited for: 4 -> 6; matrix products, arithmetic and copies ran while one was open for 0% -> 0% of each run, Pallas kernels for 7% -> 11%
where the time goes in v5:
time: 66.5 us; the launch traced here: 66.2 us
  blocking collectives  25.1 us (38%)
  Pallas kernels  25 us (38%)
  starting transfers between devices  10.3 us (15%)
  waiting for transfers between devices  5.6 us (8%)
    all_to_all x2, blocking collectives, sent(): return lax.all_to_all(block, axes, split_axis=0, concat_axis=0, tiled=True)  25.1 us
    pallas_call x1, Pallas kernels, local(): pl.pallas_call(functools.partial(expert_kernel, per_unit, len(early)), ou...  14.2 us
    ppermute x3, starting transfers between devices, local(): lax.ppermute(pair, 'z', [(i, (i + k) % chips) for i in range(chips)])  5.95 us
    pallas_call x2, Pallas kernels, bring(): pl.pallas_call(functools.partial(bring_kernel, skips[i], early_count[i]),...  4.31 us
    ppermute x3, starting transfers between devices, local(): arrived.append(near(lax.ppermute(merged[k], 'z', pairs)))  3.21 us
    ppermute x3, waiting for transfers between devices, local(): lax.ppermute(pair, 'z', [(i, (i + k) % chips) for i in range(chips)])  3.04 us
    pallas_call x1, Pallas kernels, local(): pl.pallas_call(functools.partial(stage_kernel, skips[0], early_count[0]),...  1.64 us
    pallas_call x1, Pallas kernels, local(): pl.pallas_call(functools.partial(fetch_kernel, skips[4], early_count[4]),...  1.56 us
  transfers between devices with their start and end apart: 10, of which 6 were waited for; matrix products, arithmetic and copies ran while one was open for 0% of the time, Pallas kernels for 11%

profile of v5, /device:TPU:0, one launch (start us, length us, event | category | flops | bytes accessed | tf_op | source)
XLA Modules:
  0.0 66.2 jit_solution(10587071297416120744)
XLA Ops:
  0.0 0.8 %pack.1.after_ref = bf16[8,1024]{1,0:T(8,128)(2,1)S(1)} custom-call(bf16[2,4,640]{2,1,0:T(4,128)(2,1)} %query_hbm.1, bf16[2,4,2,128]{3,2,1,0:T(2,128)(2,1)} %new_ref.1, s32[2,4,6]{2,1,0:T(4,128)} %route_ref.1), custom_call_target="tpu_custom_call" | custom-call | tf_op jit(solution)/shard_map/pack/pallas_call | solution.py:482
  0.8 0.5 collective-permute-start
  1.3 0.8 %collective-permute-done = bf16[8,1024]{1,0:T(8,128)(2,1)S(1)} collective-permute-done((bf16[8,1024]{1,0:T(8,128)(2,1)S(1)}, bf16[8,1024]{1,0:T(8,128)(2,1)S(1)}, u32[]{:S(2)}, u32[]{:S(2)}) %collective-permute-start) | collective-permute-done | bytes 16416 | tf_op jit(solution)/shard_map/ppermute | solution.py:490
  2.2 4.9 %collective-permute-start.3 = (bf16[2,8,1024]{2,1,0:T(8,128)(2,1)S(1)}, bf16[2,8,1024]{2,1,0:T(8,128)(2,1)S(1)}, u32[]{:S(2)}, u32[]{:S(2)}) collective-permute-start(bf16[2,8,1024]{2,1,0:T(8,128)(2,1)S(1)} %pad_maximum_fusion.refs_0_), channel_id=1, source_target_pairs={{0,6},{2,0},{4,2},{6,4},{1,7},{3,1},{5,3},{7,5},{8,14},{10,8},{12,... | collective-permute-start | bytes 98312 | tf_op jit(solution)/shard_map/ppermute | solution.py:494
  7.1 0.0 collective-permute-start.2
  7.1 1.0 %collective-permute-start.1 = (bf16[2,8,1024]{2,1,0:T(8,128)(2,1)S(1)}, bf16[2,8,1024]{2,1,0:T(8,128)(2,1)S(1)}, u32[]{:S(2)}, u32[]{:S(2)}) collective-permute-start(bf16[2,8,1024]{2,1,0:T(8,128)(2,1)S(1)} %pad_maximum_fusion.refs_0_), channel_id=1, source_target_pairs={{0,2},{2,4},{4,6},{6,0},{1,3},{3,5},{5,7},{7,1},{8,10},{10,12},{12... | collective-permute-start | bytes 98312 | tf_op jit(solution)/shard_map/ppermute | solution.py:494
  8.1 1.6 %stage.1 = (bf16[16,128,128]{2,1,0:T(8,128)(2,1)S(1)}, bf16[16,128,256]{2,1,0:T(8,128)(2,1)S(1)}, bf16[64,2560]{1,0:T(8,128)(2,1)S(1)}, f32[2560]{0:T(1024)S(1)}...) custom-call(s32[2,32]{1,0:T(2,128)} %table_hbm.1, ...), custom_call_target="tpu_custom_call" | custom-call | tf_op jit(solution)/shard_map/stage/pallas_call | solution.py:509
  9.8 0.0 collective-permute-done.3.refs_3_
  9.8 2.3 %collective-permute-done.2.refs_2_ = bf16[2,8,1024]{2,1,0:T(8,128)(2,1)S(1)} collective-permute-done((bf16[2,8,1024]{2,1,0:T(8,128)(2,1)S(1)}, bf16[2,8,1024]{2,1,0:T(8,128)(2,1)S(1)}, u32[]{:S(2)}, u32[]{:S(2)}) %collective-permute-start.2) | collective-permute-done | bytes 32800 | tf_op jit(solution)/shard_map/ppermute | solution.py:494
  12.1 0.7 %collective-permute-done.1.refs_1_ = bf16[2,8,1024]{2,1,0:T(8,128)(2,1)S(1)} collective-permute-done((bf16[2,8,1024]{2,1,0:T(8,128)(2,1)S(1)}, bf16[2,8,1024]{2,1,0:T(8,128)(2,1)S(1)}, u32[]{:S(2)}, u32[]{:S(2)}) %collective-permute-start.1) | collective-permute-done | bytes 32800 | tf_op jit(solution)/shard_map/ppermute | solution.py:494
  12.8 1.4 %attend.1 = (bf16[4,8,768]{2,1,0:T(8,128)(2,1)S(1)}, bf16[4,8,768]{2,1,0:T(8,128)(2,1)S(1)}, f32[64,128]{1,0:T(8,128)S(1)}) custom-call(bf16[2,8,1024]{2,1,0:T(8,128)(2,1)S(1)} %pad_maximum_fusion.refs_0_, bf16[2,8,1024]{2,1,0:T(8,128)(2,1)S(1)} %collective-permute-done.1.refs_1_, bf16[2,8,1024]{2,1,0:T(8,128)(2,1)S(1)} %collective-permute-done.2.refs_2_, ...), custom_call_target="tpu_custom_call" | custom-call | tf_op jit(solution)/shard_map/attend/pallas_call | solution.py:554
  14.3 0.1 collective-permute-start.4
  14.4 1.6 %bring.2.out_refs_0_.refs_0_ = bf16[1,384,2560]{2,1,0:T(8,128)(2,1)S(1)} custom-call(bf16[4,8,768]{2,1,0:T(8,128)(2,1)S(1)} %get-tuple-element.32.after_ref.left_ref, bf16[8,384,2560]{2,1,0:T(8,128)(2,1)} %bitcast.16, bf16[8,384,2560]{2,1,0:T(8,128)(2,1)} %bitcast.22), custom_call_target="tpu_custom_call" | custom-call | tf_op jit(solution)/shard_map/bring/pallas_call | solution.py:580
  15.9 0.0 collective-permute-done.4.right_ref
  15.9 0.2 merge.1
  16.1 0.7 collective-permute-start.5
  16.8 1.4 %collective-permute-start.6 = (bf16[8,768]{1,0:T(8,128)(2,1)S(1)}, bf16[8,768]{1,0:T(8,128)(2,1)S(1)}, u32[]{:S(2)}, u32[]{:S(2)}) collective-permute-start(bf16[8,768]{1,0:T(8,128)(2,1)S(1)} %get-tuple-element.36), channel_id=1, source_target_pairs={{0,2},{2,4},{4,6},{6,0},{1,3},{3,5},{5,7},{7,1},{8,10},{10,12},{12... | collective-permute-start | bytes 36872 | tf_op jit(solution)/shard_map/ppermute | solution.py:608
  18.2 1.1 %collective-permute-start.7 = (bf16[8,768]{1,0:T(8,128)(2,1)S(1)}, bf16[8,768]{1,0:T(8,128)(2,1)S(1)}, u32[]{:S(2)}, u32[]{:S(2)}) collective-permute-start(bf16[8,768]{1,0:T(8,128)(2,1)S(1)} %get-tuple-element.37), channel_id=1, source_target_pairs={{0,4},{2,6},{4,0},{6,2},{1,5},{3,7},{5,1},{7,3},{8,12},{10,14},{12... | collective-permute-start | bytes 36872 | tf_op jit(solution)/shard_map/ppermute | solution.py:608
  19.3 2.8 %bring.3.refs_5_.refs_1_ = bf16[3,384,2560]{2,1,0:T(8,128)(2,1)S(1)} custom-call(bf16[8,768]{1,0:T(8,128)(2,1)S(1)} %get-tuple-element.34.after_ref.refs_0_, bf16[8,384,2560]{2,1,0:T(8,128)(2,1)} %bitcast.17, bf16[8,384,2560]{2,1,0:T(8,128)(2,1)} %bitcast.23), custom_call_target="tpu_custom_call" | custom-call | tf_op jit(solution)/shard_map/bring/pallas_call | solution.py:580
  22.1 0.0 collective-permute-done.5.refs_1_
  22.1 0.2 collective-permute-done.6.refs_2_
  22.3 0.5 collective-permute-done.7.refs_3_
  22.8 0.2 residual.1
  23.0 13.2 %all_to_all.10.pieces_ref = bf16[16,8,640]{2,1,0:T(8,128)(2,1)S(1)} all-to-all(bf16[16,8,640]{2,1,0:T(8,128)(2,1)S(1)} %get-tuple-element.39), channel_id=1, replica_groups=mesh['kv'=4,'z'=4,'core'=2] {'kv','z'}, dimensions={0} | all-to-all | bytes 327680 | tf_op jit(solution)/shard_map/all_to_all | solution.py:56
  36.1 0.0 collective-permute-start.8
  36.1 1.6 %fetch.1 = (bf16[32,2560]{1,0:T(8,128)(2,1)S(1)}, f32[128,32]{1,0:T(8,128)S(1)}, bf16[1,384,2560]{2,1,0:T(8,128)(2,1)S(1)}) custom-call(bf16[16,8,640]{2,1,0:T(8,128)(2,1)S(1)} %all_to_all.10.pieces_ref, f32[64,128]{1,0:T(8,128)S(1)} %get-tuple-element.40.chosen_ref, f32[2560]{0:T(1024)S(1)} %get-tuple-element.41.gain_ref, ...), custom_call_target="tpu_custom_call" | custom-call | tf_op jit(solution)/shard_map/fetch/pallas_call | solution.py:631
  37.7 0.0 collective-permute-done.8.pieces_ref
  37.7 14.2 %experts.1 = (bf16[16,8,640]{2,1,0:T(8,128)(2,1)S(1)}, bf16[16,8,640]{2,1,0:T(8,128)(2,1)S(1)}) custom-call(bf16[16,8,640]{2,1,0:T(8,128)(2,1)S(1)} %collective-permute-done.8.pieces_ref, bf16[32,2560]{1,0:T(8,128)(2,1)S(1)} %get-tuple-element.43.norm_own_ref, f32[128,32]{1,0:T(8,128)S(1)} %get-tuple-element.44.share_own_ref, ...), custom_call_target="tpu_custom_call" | custom-call | flops 3019898880 | bytes 47185920 | tf_op jit(solution)/shard_map/experts/pallas_call | solution.py:645
  51.9 0.6 collective-permute-start.9
  52.5 1.0 %collective-permute-done.9.right_ref = bf16[16,8,640]{2,1,0:T(8,128)(2,1)S(1)} collective-permute-done((bf16[16,8,640]{2,1,0:T(8,128)(2,1)S(1)}, bf16[16,8,640]{2,1,0:T(8,128)(2,1)S(1)}, u32[]{:S(2)}, u32[]{:S(2)}) %collective-permute-start.9) | collective-permute-done | bytes 163872 | tf_op jit(solution)/shard_map/ppermute | solution.py:680
  53.6 12.0 %all_to_all.11.parts_ref = bf16[16,8,640]{2,1,0:T(8,128)(2,1)S(1)} all-to-all(bf16[16,8,640]{2,1,0:T(8,128)(2,1)S(1)} %add.1), channel_id=1, replica_groups=mesh['kv'=4,'z'=4,'core'=2] {'kv','z'}, dimensions={0} | all-to-all | bytes 327680 | tf_op jit(solution)/shard_map/all_to_all | solution.py:56
  65.5 0.6 finish.1
  (2 shorter events, 0.0 us)
Async XLA Ops:
  0.8 1.4 %collective-permute-start = (bf16[8,1024]{1,0:T(8,128)(2,1)S(1)}, bf16[8,1024]{1,0:T(8,128)(2,1)S(1)}, u32[]{:S(2)}, u32[]{:S(2)}) collective-permute-start(bf16[8,1024]{1,0:T(8,128)(2,1)S(1)} %pack.1.after_ref), channel_id=1, source_target_pairs={{0,1},{1,0},{2,3},{3,2},{4,5},{5,4},{6,7},{7,6},{8,9},{9,8},{10,11... | collective-permute-start | bytes 49160 | tf_op jit(solution)/shard_map/ppermute | solution.py:490
  2.2 7.6 %collective-permute-start.3 = (bf16[2,8,1024]{2,1,0:T(8,128)(2,1)S(1)}, bf16[2,8,1024]{2,1,0:T(8,128)(2,1)S(1)}, u32[]{:S(2)}, u32[]{:S(2)}) collective-permute-start(bf16[2,8,1024]{2,1,0:T(8,128)(2,1)S(1)} %pad_maximum_fusion.refs_0_), channel_id=1, source_target_pairs={{0,6},{2,0},{4,2},{6,4},{1,7},{3,1},{5,3},{7,5},{8,14},{10,8},{12,... | collective-permute-start | bytes 98312 | tf_op jit(solution)/shard_map/ppermute | solution.py:494
  7.1 5.0 %collective-permute-start.2 = (bf16[2,8,1024]{2,1,0:T(8,128)(2,1)S(1)}, bf16[2,8,1024]{2,1,0:T(8,128)(2,1)S(1)}, u32[]{:S(2)}, u32[]{:S(2)}) collective-permute-start(bf16[2,8,1024]{2,1,0:T(8,128)(2,1)S(1)} %pad_maximum_fusion.refs_0_), channel_id=1, source_target_pairs={{0,4},{2,6},{4,0},{6,2},{1,5},{3,7},{5,1},{7,3},{8,12},{10,14},{12... | collective-permute-start | bytes 98312 | tf_op jit(solution)/shard_map/ppermute | solution.py:494
  7.1 5.7 %collective-permute-start.1 = (bf16[2,8,1024]{2,1,0:T(8,128)(2,1)S(1)}, bf16[2,8,1024]{2,1,0:T(8,128)(2,1)S(1)}, u32[]{:S(2)}, u32[]{:S(2)}) collective-permute-start(bf16[2,8,1024]{2,1,0:T(8,128)(2,1)S(1)} %pad_maximum_fusion.refs_0_), channel_id=1, source_target_pairs={{0,2},{2,4},{4,6},{6,0},{1,3},{3,5},{5,7},{7,1},{8,10},{10,12},{12... | collective-permute-start | bytes 98312 | tf_op jit(solution)/shard_map/ppermute | solution.py:494
  14.3 1.6 %collective-permute-start.4 = (bf16[4,8,768]{2,1,0:T(8,128)(2,1)S(1)}, bf16[4,8,768]{2,1,0:T(8,128)(2,1)S(1)}, u32[]{:S(2)}, u32[]{:S(2)}) collective-permute-start(bf16[4,8,768]{2,1,0:T(8,128)(2,1)S(1)} %get-tuple-element.33), channel_id=1, source_target_pairs={{0,1},{1,0},{2,3},{3,2},{4,5},{5,4},{6,7},{7,6},{8,9},{9,8},{10,11... | collective-permute-start | bytes 147464 | tf_op jit(solution)/shard_map/ppermute | solution.py:593
  16.1 6.0 %collective-permute-start.5 = (bf16[8,768]{1,0:T(8,128)(2,1)S(1)}, bf16[8,768]{1,0:T(8,128)(2,1)S(1)}, u32[]{:S(2)}, u32[]{:S(2)}) collective-permute-start(bf16[8,768]{1,0:T(8,128)(2,1)S(1)} %get-tuple-element.35), channel_id=1, source_target_pairs={{0,6},{2,0},{4,2},{6,4},{1,7},{3,1},{5,3},{7,5},{8,14},{10,8},{12,... | collective-permute-start | bytes 36872 | tf_op jit(solution)/shard_map/ppermute | solution.py:608
  16.8 5.5 %collective-permute-start.6 = (bf16[8,768]{1,0:T(8,128)(2,1)S(1)}, bf16[8,768]{1,0:T(8,128)(2,1)S(1)}, u32[]{:S(2)}, u32[]{:S(2)}) collective-permute-start(bf16[8,768]{1,0:T(8,128)(2,1)S(1)} %get-tuple-element.36), channel_id=1, source_target_pairs={{0,2},{2,4},{4,6},{6,0},{1,3},{3,5},{5,7},{7,1},{8,10},{10,12},{12... | collective-permute-start | bytes 36872 | tf_op jit(solution)/shard_map/ppermute | solution.py:608
  18.2 4.6 %collective-permute-start.7 = (bf16[8,768]{1,0:T(8,128)(2,1)S(1)}, bf16[8,768]{1,0:T(8,128)(2,1)S(1)}, u32[]{:S(2)}, u32[]{:S(2)}) collective-permute-start(bf16[8,768]{1,0:T(8,128)(2,1)S(1)} %get-tuple-element.37), channel_id=1, source_target_pairs={{0,4},{2,6},{4,0},{6,2},{1,5},{3,7},{5,1},{7,3},{8,12},{10,14},{12... | collective-permute-start | bytes 36872 | tf_op jit(solution)/shard_map/ppermute | solution.py:608
  36.1 1.6 %collective-permute-start.8 = (bf16[16,8,640]{2,1,0:T(8,128)(2,1)S(1)}, bf16[16,8,640]{2,1,0:T(8,128)(2,1)S(1)}, u32[]{:S(2)}, u32[]{:S(2)}) collective-permute-start(bf16[16,8,640]{2,1,0:T(8,128)(2,1)S(1)} %all_to_all.10.pieces_ref), channel_id=1, source_target_pairs={{0,1},{1,0},{2,3},{3,2},{4,5},{5,4},{6,7},{7,6},{8,9},{9,8},{10,11... | collective-permute-start | bytes 491528 | tf_op jit(solution)/shard_map/ppermute | solution.py:627
  51.9 1.6 %collective-permute-start.9 = (bf16[16,8,640]{2,1,0:T(8,128)(2,1)S(1)}, bf16[16,8,640]{2,1,0:T(8,128)(2,1)S(1)}, u32[]{:S(2)}, u32[]{:S(2)}) collective-permute-start(bf16[16,8,640]{2,1,0:T(8,128)(2,1)S(1)} %get-tuple-element.47), channel_id=1, source_target_pairs={{0,1},{1,0},{2,3},{3,2},{4,5},{5,4},{6,7},{7,6},{8,9},{9,8},{10,11... | collective-permute-start | bytes 491528 | tf_op jit(solution)/shard_map/ppermute | solution.py:680

commit v6 on v5

--- a/solution.py
+++ b/solution.py
@@ -16,8 +16,8 @@
 LANES = 128
 MIB = 2**20
 AHEAD = 6
-EARLY = (0, 0, 1, 3, 1)
-SHIFTS = (3, 1, 2)
+EARLY = (0, 0, 0, 5, 1)
+SHIFTS = (3, 2, 1)
 F32 = jnp.float32
 BF16 = jnp.bfloat16
 NT = (((1,), (1,)), ((), ()))

time: 66.5 us -> 65.9 us (level)
  Pallas kernels: 25 us -> 24.1 us
    ppermute x1, waiting for transfers between devices: 0.01 us -> 1.22 us  [local(): passed = lax.ppermute(passed, 'core', ((0, 1), (1, 0)))]
    ppermute x3, waiting for transfers between devices: 0.69 us -> 0.01 us  [local(): arrived.append(near(lax.ppermute(merged[k], 'z', pairs)))]
    pallas_call x2 -> x1, Pallas kernels: 4.31 us -> 3.91 us  [bring(): pl.pallas_call(functools.partial(bring_kernel, skips[i], early_count[i]),...]
  transfers between devices with their start and end apart: 10 -> 10, of which waited for: 6 -> 5; matrix products, arithmetic and copies ran while one was open for 0% -> 0% of each run, Pallas kernels for 11% -> 11%
where the time goes in v6:
time: 65.9 us; the launch traced here: 65.6 us
  blocking collectives  24.9 us (38%)
  Pallas kernels  24.1 us (37%)
  starting transfers between devices  10.3 us (16%)
  waiting for transfers between devices  6.16 us (9%)
    all_to_all x2, blocking collectives, sent(): return lax.all_to_all(block, axes, split_axis=0, concat_axis=0, tiled=True)  24.9 us
    pallas_call x1, Pallas kernels, local(): pl.pallas_call(functools.partial(expert_kernel, per_unit, len(early)), ou...  13.7 us
    ppermute x3, starting transfers between devices, local(): lax.ppermute(pair, 'z', [(i, (i + k) % chips) for i in range(chips)])  5.95 us
    pallas_call x1, Pallas kernels, bring(): pl.pallas_call(functools.partial(bring_kernel, skips[i], early_count[i]),...  3.91 us
    ppermute x3, starting transfers between devices, local(): arrived.append(near(lax.ppermute(merged[k], 'z', pairs)))  3.2 us
    ppermute x3, waiting for transfers between devices, local(): lax.ppermute(pair, 'z', [(i, (i + k) % chips) for i in range(chips)])  3.06 us
    pallas_call x1, Pallas kernels, local(): pl.pallas_call(functools.partial(stage_kernel, skips[0], early_count[0]),...  1.62 us
    pallas_call x1, Pallas kernels, local(): pl.pallas_call(functools.partial(fetch_kernel, skips[4], early_count[4]),...  1.56 us
  transfers between devices with their start and end apart: 10, of which 5 were waited for; matrix products, arithmetic and copies ran while one was open for 0% of the time, Pallas kernels for 11%

profile of v6, /device:TPU:0, one launch (start us, length us, event | category | flops | bytes accessed | tf_op | source)
XLA Modules:
  0.0 65.6 jit_solution(4197369440982306566)
XLA Ops:
  0.0 0.8 %pack.1.after_ref = bf16[8,1024]{1,0:T(8,128)(2,1)S(1)} custom-call(bf16[2,4,640]{2,1,0:T(4,128)(2,1)} %query_hbm.1, bf16[2,4,2,128]{3,2,1,0:T(2,128)(2,1)} %new_ref.1, s32[2,4,6]{2,1,0:T(4,128)} %route_ref.1), custom_call_target="tpu_custom_call" | custom-call | tf_op jit(solution)/shard_map/pack/pallas_call | solution.py:482
  0.8 0.5 collective-permute-start
  1.3 0.8 %collective-permute-done = bf16[8,1024]{1,0:T(8,128)(2,1)S(1)} collective-permute-done((bf16[8,1024]{1,0:T(8,128)(2,1)S(1)}, bf16[8,1024]{1,0:T(8,128)(2,1)S(1)}, u32[]{:S(2)}, u32[]{:S(2)}) %collective-permute-start) | collective-permute-done | bytes 16416 | tf_op jit(solution)/shard_map/ppermute | solution.py:490
  2.2 4.9 %collective-permute-start.3 = (bf16[2,8,1024]{2,1,0:T(8,128)(2,1)S(1)}, bf16[2,8,1024]{2,1,0:T(8,128)(2,1)S(1)}, u32[]{:S(2)}, u32[]{:S(2)}) collective-permute-start(bf16[2,8,1024]{2,1,0:T(8,128)(2,1)S(1)} %pad_maximum_fusion.refs_0_), channel_id=1, source_target_pairs={{0,6},{2,0},{4,2},{6,4},{1,7},{3,1},{5,3},{7,5},{8,14},{10,8},{12,... | collective-permute-start | bytes 98312 | tf_op jit(solution)/shard_map/ppermute | solution.py:494
  7.1 0.0 collective-permute-start.2
  7.1 1.0 %collective-permute-start.1 = (bf16[2,8,1024]{2,1,0:T(8,128)(2,1)S(1)}, bf16[2,8,1024]{2,1,0:T(8,128)(2,1)S(1)}, u32[]{:S(2)}, u32[]{:S(2)}) collective-permute-start(bf16[2,8,1024]{2,1,0:T(8,128)(2,1)S(1)} %pad_maximum_fusion.refs_0_), channel_id=1, source_target_pairs={{0,2},{2,4},{4,6},{6,0},{1,3},{3,5},{5,7},{7,1},{8,10},{10,12},{12... | collective-permute-start | bytes 98312 | tf_op jit(solution)/shard_map/ppermute | solution.py:494
  8.1 1.6 %stage.1 = (bf16[16,128,128]{2,1,0:T(8,128)(2,1)S(1)}, bf16[16,128,256]{2,1,0:T(8,128)(2,1)S(1)}, bf16[64,2560]{1,0:T(8,128)(2,1)S(1)}, f32[2560]{0:T(1024)S(1)}...) custom-call(s32[2,32]{1,0:T(2,128)} %table_hbm.1, ...), custom_call_target="tpu_custom_call" | custom-call | tf_op jit(solution)/shard_map/stage/pallas_call | solution.py:509
  9.8 0.0 collective-permute-done.3.refs_3_
  9.8 2.3 %collective-permute-done.2.refs_2_ = bf16[2,8,1024]{2,1,0:T(8,128)(2,1)S(1)} collective-permute-done((bf16[2,8,1024]{2,1,0:T(8,128)(2,1)S(1)}, bf16[2,8,1024]{2,1,0:T(8,128)(2,1)S(1)}, u32[]{:S(2)}, u32[]{:S(2)}) %collective-permute-start.2) | collective-permute-done | bytes 32800 | tf_op jit(solution)/shard_map/ppermute | solution.py:494
  12.1 0.7 %collective-permute-done.1.refs_1_ = bf16[2,8,1024]{2,1,0:T(8,128)(2,1)S(1)} collective-permute-done((bf16[2,8,1024]{2,1,0:T(8,128)(2,1)S(1)}, bf16[2,8,1024]{2,1,0:T(8,128)(2,1)S(1)}, u32[]{:S(2)}, u32[]{:S(2)}) %collective-permute-start.1) | collective-permute-done | bytes 32800 | tf_op jit(solution)/shard_map/ppermute | solution.py:494
  12.8 1.4 %attend.1 = (bf16[4,8,768]{2,1,0:T(8,128)(2,1)S(1)}, bf16[4,8,768]{2,1,0:T(8,128)(2,1)S(1)}, f32[64,128]{1,0:T(8,128)S(1)}) custom-call(bf16[2,8,1024]{2,1,0:T(8,128)(2,1)S(1)} %pad_maximum_fusion.refs_0_, bf16[2,8,1024]{2,1,0:T(8,128)(2,1)S(1)} %collective-permute-done.1.refs_1_, bf16[2,8,1024]{2,1,0:T(8,128)(2,1)S(1)} %collective-permute-done.2.refs_2_, ...), custom_call_target="tpu_custom_call" | custom-call | tf_op jit(solution)/shard_map/attend/pallas_call | solution.py:554
  14.3 0.1 collective-permute-start.4
  14.4 1.2 %collective-permute-done.4.right_ref = bf16[4,8,768]{2,1,0:T(8,128)(2,1)S(1)} collective-permute-done((bf16[4,8,768]{2,1,0:T(8,128)(2,1)S(1)}, bf16[4,8,768]{2,1,0:T(8,128)(2,1)S(1)}, u32[]{:S(2)}, u32[]{:S(2)}) %collective-permute-start.4) | collective-permute-done | bytes 49184 | tf_op jit(solution)/shard_map/ppermute | solution.py:593
  15.6 0.2 merge.1
  15.8 0.6 collective-permute-start.5
  16.4 0.6 collective-permute-start.6
  17.0 1.9 %collective-permute-start.7 = (bf16[8,768]{1,0:T(8,128)(2,1)S(1)}, bf16[8,768]{1,0:T(8,128)(2,1)S(1)}, u32[]{:S(2)}, u32[]{:S(2)}) collective-permute-start(bf16[8,768]{1,0:T(8,128)(2,1)S(1)} %get-tuple-element.37), channel_id=1, source_target_pairs={{0,2},{2,4},{4,6},{6,0},{1,3},{3,5},{5,7},{7,1},{8,10},{10,12},{12... | collective-permute-start | bytes 36872 | tf_op jit(solution)/shard_map/ppermute | solution.py:608
  19.0 3.9 %bring.1.refs_5_.refs_0_ = bf16[5,384,2560]{2,1,0:T(8,128)(2,1)S(1)} custom-call(bf16[8,768]{1,0:T(8,128)(2,1)S(1)} %get-tuple-element.34.after_ref.refs_0_, bf16[8,384,2560]{2,1,0:T(8,128)(2,1)} %bitcast.16, bf16[8,384,2560]{2,1,0:T(8,128)(2,1)} %bitcast.21), custom_call_target="tpu_custom_call" | custom-call | tf_op jit(solution)/shard_map/bring/pallas_call | solution.py:580
  22.9 0.0 collective-permute-done.5.refs_1_
  22.9 0.0 collective-permute-done.6.refs_2_
  22.9 0.0 collective-permute-done.7.refs_3_
  22.9 0.2 residual.1
  23.1 13.2 %all_to_all.10.pieces_ref = bf16[16,8,640]{2,1,0:T(8,128)(2,1)S(1)} all-to-all(bf16[16,8,640]{2,1,0:T(8,128)(2,1)S(1)} %get-tuple-element.39), channel_id=1, replica_groups=mesh['kv'=4,'z'=4,'core'=2] {'kv','z'}, dimensions={0} | all-to-all | bytes 327680 | tf_op jit(solution)/shard_map/all_to_all | solution.py:56
  36.3 0.0 collective-permute-start.8
  36.3 1.6 %fetch.1 = (bf16[32,2560]{1,0:T(8,128)(2,1)S(1)}, f32[128,32]{1,0:T(8,128)S(1)}, bf16[1,384,2560]{2,1,0:T(8,128)(2,1)S(1)}) custom-call(bf16[16,8,640]{2,1,0:T(8,128)(2,1)S(1)} %all_to_all.10.pieces_ref, f32[64,128]{1,0:T(8,128)S(1)} %get-tuple-element.40.chosen_ref, f32[2560]{0:T(1024)S(1)} %get-tuple-element.41.gain_ref, ...), custom_call_target="tpu_custom_call" | custom-call | tf_op jit(solution)/shard_map/fetch/pallas_call | solution.py:631
  37.8 0.0 collective-permute-done.8.pieces_ref
  37.8 13.7 %experts.1 = (bf16[16,8,640]{2,1,0:T(8,128)(2,1)S(1)}, bf16[16,8,640]{2,1,0:T(8,128)(2,1)S(1)}) custom-call(bf16[16,8,640]{2,1,0:T(8,128)(2,1)S(1)} %collective-permute-done.8.pieces_ref, bf16[32,2560]{1,0:T(8,128)(2,1)S(1)} %get-tuple-element.43.norm_own_ref, f32[128,32]{1,0:T(8,128)S(1)} %get-tuple-element.44.share_own_ref, ...), custom_call_target="tpu_custom_call" | custom-call | flops 3019898880 | bytes 47185920 | tf_op jit(solution)/shard_map/experts/pallas_call | solution.py:645
  51.5 0.6 collective-permute-start.9
  52.1 1.0 %collective-permute-done.9.right_ref = bf16[16,8,640]{2,1,0:T(8,128)(2,1)S(1)} collective-permute-done((bf16[16,8,640]{2,1,0:T(8,128)(2,1)S(1)}, bf16[16,8,640]{2,1,0:T(8,128)(2,1)S(1)}, u32[]{:S(2)}, u32[]{:S(2)}) %collective-permute-start.9) | collective-permute-done | bytes 163872 | tf_op jit(solution)/shard_map/ppermute | solution.py:680
  53.2 11.8 %all_to_all.11.parts_ref = bf16[16,8,640]{2,1,0:T(8,128)(2,1)S(1)} all-to-all(bf16[16,8,640]{2,1,0:T(8,128)(2,1)S(1)} %add.1), channel_id=1, replica_groups=mesh['kv'=4,'z'=4,'core'=2] {'kv','z'}, dimensions={0} | all-to-all | bytes 327680 | tf_op jit(solution)/shard_map/all_to_all | solution.py:56
  64.9 0.6 finish.1
  (2 shorter events, 0.1 us)
Async XLA Ops:
  0.8 1.4 %collective-permute-start = (bf16[8,1024]{1,0:T(8,128)(2,1)S(1)}, bf16[8,1024]{1,0:T(8,128)(2,1)S(1)}, u32[]{:S(2)}, u32[]{:S(2)}) collective-permute-start(bf16[8,1024]{1,0:T(8,128)(2,1)S(1)} %pack.1.after_ref), channel_id=1, source_target_pairs={{0,1},{1,0},{2,3},{3,2},{4,5},{5,4},{6,7},{7,6},{8,9},{9,8},{10,11... | collective-permute-start | bytes 49160 | tf_op jit(solution)/shard_map/ppermute | solution.py:490
  2.2 7.6 %collective-permute-start.3 = (bf16[2,8,1024]{2,1,0:T(8,128)(2,1)S(1)}, bf16[2,8,1024]{2,1,0:T(8,128)(2,1)S(1)}, u32[]{:S(2)}, u32[]{:S(2)}) collective-permute-start(bf16[2,8,1024]{2,1,0:T(8,128)(2,1)S(1)} %pad_maximum_fusion.refs_0_), channel_id=1, source_target_pairs={{0,6},{2,0},{4,2},{6,4},{1,7},{3,1},{5,3},{7,5},{8,14},{10,8},{12,... | collective-permute-start | bytes 98312 | tf_op jit(solution)/shard_map/ppermute | solution.py:494
  7.1 5.0 %collective-permute-start.2 = (bf16[2,8,1024]{2,1,0:T(8,128)(2,1)S(1)}, bf16[2,8,1024]{2,1,0:T(8,128)(2,1)S(1)}, u32[]{:S(2)}, u32[]{:S(2)}) collective-permute-start(bf16[2,8,1024]{2,1,0:T(8,128)(2,1)S(1)} %pad_maximum_fusion.refs_0_), channel_id=1, source_target_pairs={{0,4},{2,6},{4,0},{6,2},{1,5},{3,7},{5,1},{7,3},{8,12},{10,14},{12... | collective-permute-start | bytes 98312 | tf_op jit(solution)/shard_map/ppermute | solution.py:494
  7.1 5.7 %collective-permute-start.1 = (bf16[2,8,1024]{2,1,0:T(8,128)(2,1)S(1)}, bf16[2,8,1024]{2,1,0:T(8,128)(2,1)S(1)}, u32[]{:S(2)}, u32[]{:S(2)}) collective-permute-start(bf16[2,8,1024]{2,1,0:T(8,128)(2,1)S(1)} %pad_maximum_fusion.refs_0_), channel_id=1, source_target_pairs={{0,2},{2,4},{4,6},{6,0},{1,3},{3,5},{5,7},{7,1},{8,10},{10,12},{12... | collective-permute-start | bytes 98312 | tf_op jit(solution)/shard_map/ppermute | solution.py:494
  14.3 1.3 %collective-permute-start.4 = (bf16[4,8,768]{2,1,0:T(8,128)(2,1)S(1)}, bf16[4,8,768]{2,1,0:T(8,128)(2,1)S(1)}, u32[]{:S(2)}, u32[]{:S(2)}) collective-permute-start(bf16[4,8,768]{2,1,0:T(8,128)(2,1)S(1)} %get-tuple-element.33), channel_id=1, source_target_pairs={{0,1},{1,0},{2,3},{3,2},{4,5},{5,4},{6,7},{7,6},{8,9},{9,8},{10,11... | collective-permute-start | bytes 147464 | tf_op jit(solution)/shard_map/ppermute | solution.py:593
  15.8 7.1 %collective-permute-start.5 = (bf16[8,768]{1,0:T(8,128)(2,1)S(1)}, bf16[8,768]{1,0:T(8,128)(2,1)S(1)}, u32[]{:S(2)}, u32[]{:S(2)}) collective-permute-start(bf16[8,768]{1,0:T(8,128)(2,1)S(1)} %get-tuple-element.35), channel_id=1, source_target_pairs={{0,6},{2,0},{4,2},{6,4},{1,7},{3,1},{5,3},{7,5},{8,14},{10,8},{12,... | collective-permute-start | bytes 36872 | tf_op jit(solution)/shard_map/ppermute | solution.py:608
  16.4 6.5 %collective-permute-start.6 = (bf16[8,768]{1,0:T(8,128)(2,1)S(1)}, bf16[8,768]{1,0:T(8,128)(2,1)S(1)}, u32[]{:S(2)}, u32[]{:S(2)}) collective-permute-start(bf16[8,768]{1,0:T(8,128)(2,1)S(1)} %get-tuple-element.36), channel_id=1, source_target_pairs={{0,4},{2,6},{4,0},{6,2},{1,5},{3,7},{5,1},{7,3},{8,12},{10,14},{12... | collective-permute-start | bytes 36872 | tf_op jit(solution)/shard_map/ppermute | solution.py:608
  17.0 5.9 %collective-permute-start.7 = (bf16[8,768]{1,0:T(8,128)(2,1)S(1)}, bf16[8,768]{1,0:T(8,128)(2,1)S(1)}, u32[]{:S(2)}, u32[]{:S(2)}) collective-permute-start(bf16[8,768]{1,0:T(8,128)(2,1)S(1)} %get-tuple-element.37), channel_id=1, source_target_pairs={{0,2},{2,4},{4,6},{6,0},{1,3},{3,5},{5,7},{7,1},{8,10},{10,12},{12... | collective-permute-start | bytes 36872 | tf_op jit(solution)/shard_map/ppermute | solution.py:608
  36.3 1.6 %collective-permute-start.8 = (bf16[16,8,640]{2,1,0:T(8,128)(2,1)S(1)}, bf16[16,8,640]{2,1,0:T(8,128)(2,1)S(1)}, u32[]{:S(2)}, u32[]{:S(2)}) collective-permute-start(bf16[16,8,640]{2,1,0:T(8,128)(2,1)S(1)} %all_to_all.10.pieces_ref), channel_id=1, source_target_pairs={{0,1},{1,0},{2,3},{3,2},{4,5},{5,4},{6,7},{7,6},{8,9},{9,8},{10,11... | collective-permute-start | bytes 491528 | tf_op jit(solution)/shard_map/ppermute | solution.py:627
  51.5 1.6 %collective-permute-start.9 = (bf16[16,8,640]{2,1,0:T(8,128)(2,1)S(1)}, bf16[16,8,640]{2,1,0:T(8,128)(2,1)S(1)}, u32[]{:S(2)}, u32[]{:S(2)}) collective-permute-start(bf16[16,8,640]{2,1,0:T(8,128)(2,1)S(1)} %get-tuple-element.47), channel_id=1, source_target_pairs={{0,1},{1,0},{2,3},{3,2},{4,5},{5,4},{6,7},{7,6},{8,9},{9,8},{10,11... | collective-permute-start | bytes 491528 | tf_op jit(solution)/shard_map/ppermute | solution.py:680

commit v7 on v6

--- a/solution.py
+++ b/solution.py
@@ -95,18 +95,16 @@
 
 def stage_kernel(
     skip, count, table_hbm, length_hbm, parent_hbm, key_hbm, value_hbm, router_hbm, gain_hbm,
-    gate_hbm, up_hbm, query_hbm, stream_hbm, after_ref,
+    gate_hbm, up_hbm, query_ref, stream_ref, after_ref,
     key_ref, extended_ref, router_ref, gain_ref, valid_ref, own_ref, own_stream_ref, mask_ref, *refs,
 ):
     del after_ref
-    table_ref, length_ref, parent_ref, query_ref, stream_ref, sems = refs[-7:-1]
+    table_ref, length_ref, parent_ref, sems = refs[-5:-1]
     early = early_copies(skip, count, gate_hbm, up_hbm, refs[0], refs[-1])
     first = [
         pltpu.make_async_copy(table_hbm, table_ref, sems.at[4]),
         pltpu.make_async_copy(length_hbm, length_ref, sems.at[5]),
         pltpu.make_async_copy(parent_hbm, parent_ref, sems.at[6]),
-        pltpu.make_async_copy(query_hbm, query_ref, sems.at[7]),
-        pltpu.make_async_copy(stream_hbm, stream_ref, sems.at[8]),
     ]
     for copy in first:
         copy.start()
@@ -519,15 +517,13 @@
             result((heads * rows, all_rows), F32),
             *shapes[0],
         ],
-        in_specs=[HBM] * 11 + [ANY],
+        in_specs=[HBM] * 9 + [VMEM] * 2 + [ANY],
         out_specs=[VMEM] * (8 + len(shapes[0])),
         scratch_shapes=[
             pltpu.SMEM(page_table.shape, jnp.int32),
             pltpu.SMEM(lengths.shape, jnp.int32),
             pltpu.SMEM(parents.shape[::-1], jnp.int32),
-            pltpu.VMEM(queries.shape, BF16),
-            pltpu.VMEM(stream_in.shape, BF16),
-            pltpu.SemaphoreType.DMA((9,)),
+            pltpu.SemaphoreType.DMA((7,)),
             early_sems[0],
         ],
         compiler_params=pltpu.CompilerParams(vmem_limit_bytes=16 * MIB),

time: 65.9 us -> 66.2 us (level)
  Pallas kernels: 24.1 us -> 24.8 us
  waiting for transfers between devices: 6.16 us -> 5.49 us
    pallas_call x1, Pallas kernels: 1.62 us -> 2.32 us  [local(): pl.pallas_call(functools.partial(stage_kernel, skips[0], early_count[0]),...]
    ppermute x3, waiting for transfers between devices: 3.06 us -> 2.36 us  [local(): lax.ppermute(pair, 'z', [(i, (i + k) % chips) for i in range(chips)])]
  transfers between devices with their start and end apart: 10 -> 10, of which waited for: 5 -> 5; matrix products, arithmetic and copies ran while one was open for 0% -> 0% of each run, Pallas kernels for 11% -> 12%
where the time goes in v7:
time: 66.2 us; the launch traced here: 65.8 us
  blocking collectives  25.1 us (38%)
  Pallas kernels  24.8 us (37%)
  starting transfers between devices  10.3 us (16%)
  waiting for transfers between devices  5.49 us (8%)
    all_to_all x2, blocking collectives, sent(): return lax.all_to_all(block, axes, split_axis=0, concat_axis=0, tiled=True)  25.1 us
    pallas_call x1, Pallas kernels, local(): pl.pallas_call(functools.partial(expert_kernel, per_unit, len(early)), ou...  13.7 us
    ppermute x3, starting transfers between devices, local(): lax.ppermute(pair, 'z', [(i, (i + k) % chips) for i in range(chips)])  5.95 us
    pallas_call x1, Pallas kernels, bring(): pl.pallas_call(functools.partial(bring_kernel, skips[i], early_count[i]),...  3.91 us
    ppermute x3, starting transfers between devices, local(): arrived.append(near(lax.ppermute(merged[k], 'z', pairs)))  3.2 us
    ppermute x3, waiting for transfers between devices, local(): lax.ppermute(pair, 'z', [(i, (i + k) % chips) for i in range(chips)])  2.36 us
    pallas_call x1, Pallas kernels, local(): pl.pallas_call(functools.partial(stage_kernel, skips[0], early_count[0]),...  2.32 us
    pallas_call x1, Pallas kernels, local(): pl.pallas_call(functools.partial(fetch_kernel, skips[4], early_count[4]),...  1.56 us
  transfers between devices with their start and end apart: 10, of which 5 were waited for; matrix products, arithmetic and copies ran while one was open for 0% of the time, Pallas kernels for 12%

profile of v7, /device:TPU:0, one launch (start us, length us, event | category | flops | bytes accessed | tf_op | source)
XLA Modules:
  0.0 65.8 jit_solution(6830310708083032401)
XLA Ops:
  0.0 0.8 %pack.1.after_ref = bf16[8,1024]{1,0:T(8,128)(2,1)S(1)} custom-call(bf16[2,4,640]{2,1,0:T(4,128)(2,1)} %query_ref.3, bf16[2,4,2,128]{3,2,1,0:T(2,128)(2,1)} %new_ref.1, s32[2,4,6]{2,1,0:T(4,128)} %route_ref.1), custom_call_target="tpu_custom_call" | custom-call | tf_op jit(solution)/shard_map/pack/pallas_call | solution.py:480
  0.8 0.5 collective-permute-start
  1.3 0.8 %collective-permute-done = bf16[8,1024]{1,0:T(8,128)(2,1)S(1)} collective-permute-done((bf16[8,1024]{1,0:T(8,128)(2,1)S(1)}, bf16[8,1024]{1,0:T(8,128)(2,1)S(1)}, u32[]{:S(2)}, u32[]{:S(2)}) %collective-permute-start) | collective-permute-done | bytes 16416 | tf_op jit(solution)/shard_map/ppermute | solution.py:488
  2.2 4.9 %collective-permute-start.3 = (bf16[2,8,1024]{2,1,0:T(8,128)(2,1)S(1)}, bf16[2,8,1024]{2,1,0:T(8,128)(2,1)S(1)}, u32[]{:S(2)}, u32[]{:S(2)}) collective-permute-start(bf16[2,8,1024]{2,1,0:T(8,128)(2,1)S(1)} %pad_maximum_fusion.refs_0_), channel_id=1, source_target_pairs={{0,6},{2,0},{4,2},{6,4},{1,7},{3,1},{5,3},{7,5},{8,14},{10,8},{12,... | collective-permute-start | bytes 98312 | tf_op jit(solution)/shard_map/ppermute | solution.py:492
  7.1 0.0 collective-permute-start.2
  7.1 1.0 %collective-permute-start.1 = (bf16[2,8,1024]{2,1,0:T(8,128)(2,1)S(1)}, bf16[2,8,1024]{2,1,0:T(8,128)(2,1)S(1)}, u32[]{:S(2)}, u32[]{:S(2)}) collective-permute-start(bf16[2,8,1024]{2,1,0:T(8,128)(2,1)S(1)} %pad_maximum_fusion.refs_0_), channel_id=1, source_target_pairs={{0,2},{2,4},{4,6},{6,0},{1,3},{3,5},{5,7},{7,1},{8,10},{10,12},{12... | collective-permute-start | bytes 98312 | tf_op jit(solution)/shard_map/ppermute | solution.py:492
  8.1 2.3 %stage.1 = (bf16[16,128,128]{2,1,0:T(8,128)(2,1)S(1)}, bf16[16,128,256]{2,1,0:T(8,128)(2,1)S(1)}, bf16[64,2560]{1,0:T(8,128)(2,1)S(1)}, f32[2560]{0:T(1024)S(1)}...) custom-call(s32[2,32]{1,0:T(2,128)} %table_hbm.1, ...), custom_call_target="tpu_custom_call" | custom-call | tf_op jit(solution)/shard_map/stage/pallas_call | solution.py:507
  10.5 0.0 collective-permute-done.3.refs_3_
  10.5 1.6 %collective-permute-done.2.refs_2_ = bf16[2,8,1024]{2,1,0:T(8,128)(2,1)S(1)} collective-permute-done((bf16[2,8,1024]{2,1,0:T(8,128)(2,1)S(1)}, bf16[2,8,1024]{2,1,0:T(8,128)(2,1)S(1)}, u32[]{:S(2)}, u32[]{:S(2)}) %collective-permute-start.2) | collective-permute-done | bytes 32800 | tf_op jit(solution)/shard_map/ppermute | solution.py:492
  12.1 0.7 %collective-permute-done.1.refs_1_ = bf16[2,8,1024]{2,1,0:T(8,128)(2,1)S(1)} collective-permute-done((bf16[2,8,1024]{2,1,0:T(8,128)(2,1)S(1)}, bf16[2,8,1024]{2,1,0:T(8,128)(2,1)S(1)}, u32[]{:S(2)}, u32[]{:S(2)}) %collective-permute-start.1) | collective-permute-done | bytes 32800 | tf_op jit(solution)/shard_map/ppermute | solution.py:492
  12.8 1.4 %attend.1 = (bf16[4,8,768]{2,1,0:T(8,128)(2,1)S(1)}, bf16[4,8,768]{2,1,0:T(8,128)(2,1)S(1)}, f32[64,128]{1,0:T(8,128)S(1)}) custom-call(bf16[2,8,1024]{2,1,0:T(8,128)(2,1)S(1)} %pad_maximum_fusion.refs_0_, bf16[2,8,1024]{2,1,0:T(8,128)(2,1)S(1)} %collective-permute-done.1.refs_1_, bf16[2,8,1024]{2,1,0:T(8,128)(2,1)S(1)} %collective-permute-done.2.refs_2_, ...), custom_call_target="tpu_custom_call" | custom-call | tf_op jit(solution)/shard_map/attend/pallas_call | solution.py:550
  14.3 0.1 collective-permute-start.4
  14.4 1.2 %collective-permute-done.4.right_ref = bf16[4,8,768]{2,1,0:T(8,128)(2,1)S(1)} collective-permute-done((bf16[4,8,768]{2,1,0:T(8,128)(2,1)S(1)}, bf16[4,8,768]{2,1,0:T(8,128)(2,1)S(1)}, u32[]{:S(2)}, u32[]{:S(2)}) %collective-permute-start.4) | collective-permute-done | bytes 49184 | tf_op jit(solution)/shard_map/ppermute | solution.py:589
  15.6 0.2 merge.1
  15.8 0.6 collective-permute-start.5
  16.4 1.0 %collective-permute-start.6 = (bf16[8,768]{1,0:T(8,128)(2,1)S(1)}, bf16[8,768]{1,0:T(8,128)(2,1)S(1)}, u32[]{:S(2)}, u32[]{:S(2)}) collective-permute-start(bf16[8,768]{1,0:T(8,128)(2,1)S(1)} %get-tuple-element.36), channel_id=1, source_target_pairs={{0,4},{2,6},{4,0},{6,2},{1,5},{3,7},{5,1},{7,3},{8,12},{10,14},{12... | collective-permute-start | bytes 36872 | tf_op jit(solution)/shard_map/ppermute | solution.py:604
  17.4 1.5 %collective-permute-start.7 = (bf16[8,768]{1,0:T(8,128)(2,1)S(1)}, bf16[8,768]{1,0:T(8,128)(2,1)S(1)}, u32[]{:S(2)}, u32[]{:S(2)}) collective-permute-start(bf16[8,768]{1,0:T(8,128)(2,1)S(1)} %get-tuple-element.37), channel_id=1, source_target_pairs={{0,2},{2,4},{4,6},{6,0},{1,3},{3,5},{5,7},{7,1},{8,10},{10,12},{12... | collective-permute-start | bytes 36872 | tf_op jit(solution)/shard_map/ppermute | solution.py:604
  19.0 3.9 %bring.1.refs_5_.refs_0_ = bf16[5,384,2560]{2,1,0:T(8,128)(2,1)S(1)} custom-call(bf16[8,768]{1,0:T(8,128)(2,1)S(1)} %get-tuple-element.34.after_ref.refs_0_, bf16[8,384,2560]{2,1,0:T(8,128)(2,1)} %bitcast.16, bf16[8,384,2560]{2,1,0:T(8,128)(2,1)} %bitcast.21), custom_call_target="tpu_custom_call" | custom-call | tf_op jit(solution)/shard_map/bring/pallas_call | solution.py:576
  22.9 0.0 collective-permute-done.5.refs_1_
  22.9 0.0 collective-permute-done.6.refs_2_
  22.9 0.0 collective-permute-done.7.refs_3_
  22.9 0.2 residual.1
  23.1 13.3 %all_to_all.10.pieces_ref = bf16[16,8,640]{2,1,0:T(8,128)(2,1)S(1)} all-to-all(bf16[16,8,640]{2,1,0:T(8,128)(2,1)S(1)} %get-tuple-element.39), channel_id=1, replica_groups=mesh['kv'=4,'z'=4,'core'=2] {'kv','z'}, dimensions={0} | all-to-all | bytes 327680 | tf_op jit(solution)/shard_map/all_to_all | solution.py:56
  36.4 0.0 collective-permute-start.8
  36.4 1.6 %fetch.1 = (bf16[32,2560]{1,0:T(8,128)(2,1)S(1)}, f32[128,32]{1,0:T(8,128)S(1)}, bf16[1,384,2560]{2,1,0:T(8,128)(2,1)S(1)}) custom-call(bf16[16,8,640]{2,1,0:T(8,128)(2,1)S(1)} %all_to_all.10.pieces_ref, f32[64,128]{1,0:T(8,128)S(1)} %get-tuple-element.40.chosen_ref, f32[2560]{0:T(1024)S(1)} %get-tuple-element.41.gain_ref, ...), custom_call_target="tpu_custom_call" | custom-call | tf_op jit(solution)/shard_map/fetch/pallas_call | solution.py:627
  38.0 0.0 collective-permute-done.8.pieces_ref
  38.0 13.7 %experts.1 = (bf16[16,8,640]{2,1,0:T(8,128)(2,1)S(1)}, bf16[16,8,640]{2,1,0:T(8,128)(2,1)S(1)}) custom-call(bf16[16,8,640]{2,1,0:T(8,128)(2,1)S(1)} %collective-permute-done.8.pieces_ref, bf16[32,2560]{1,0:T(8,128)(2,1)S(1)} %get-tuple-element.43.norm_own_ref, f32[128,32]{1,0:T(8,128)S(1)} %get-tuple-element.44.share_own_ref, ...), custom_call_target="tpu_custom_call" | custom-call | flops 3019898880 | bytes 47185920 | tf_op jit(solution)/shard_map/experts/pallas_call | solution.py:641
  51.7 0.6 collective-permute-start.9
  52.3 1.0 %collective-permute-done.9.right_ref = bf16[16,8,640]{2,1,0:T(8,128)(2,1)S(1)} collective-permute-done((bf16[16,8,640]{2,1,0:T(8,128)(2,1)S(1)}, bf16[16,8,640]{2,1,0:T(8,128)(2,1)S(1)}, u32[]{:S(2)}, u32[]{:S(2)}) %collective-permute-start.9) | collective-permute-done | bytes 163872 | tf_op jit(solution)/shard_map/ppermute | solution.py:676
  53.4 11.8 %all_to_all.11.parts_ref = bf16[16,8,640]{2,1,0:T(8,128)(2,1)S(1)} all-to-all(bf16[16,8,640]{2,1,0:T(8,128)(2,1)S(1)} %add.1), channel_id=1, replica_groups=mesh['kv'=4,'z'=4,'core'=2] {'kv','z'}, dimensions={0} | all-to-all | bytes 327680 | tf_op jit(solution)/shard_map/all_to_all | solution.py:56
  65.1 0.6 finish.1
  (2 shorter events, 0.1 us)
Async XLA Ops:
  0.8 1.4 %collective-permute-start = (bf16[8,1024]{1,0:T(8,128)(2,1)S(1)}, bf16[8,1024]{1,0:T(8,128)(2,1)S(1)}, u32[]{:S(2)}, u32[]{:S(2)}) collective-permute-start(bf16[8,1024]{1,0:T(8,128)(2,1)S(1)} %pack.1.after_ref), channel_id=1, source_target_pairs={{0,1},{1,0},{2,3},{3,2},{4,5},{5,4},{6,7},{7,6},{8,9},{9,8},{10,11... | collective-permute-start | bytes 49160 | tf_op jit(solution)/shard_map/ppermute | solution.py:488
  2.2 8.3 %collective-permute-start.3 = (bf16[2,8,1024]{2,1,0:T(8,128)(2,1)S(1)}, bf16[2,8,1024]{2,1,0:T(8,128)(2,1)S(1)}, u32[]{:S(2)}, u32[]{:S(2)}) collective-permute-start(bf16[2,8,1024]{2,1,0:T(8,128)(2,1)S(1)} %pad_maximum_fusion.refs_0_), channel_id=1, source_target_pairs={{0,6},{2,0},{4,2},{6,4},{1,7},{3,1},{5,3},{7,5},{8,14},{10,8},{12,... | collective-permute-start | bytes 98312 | tf_op jit(solution)/shard_map/ppermute | solution.py:492
  7.1 5.0 %collective-permute-start.2 = (bf16[2,8,1024]{2,1,0:T(8,128)(2,1)S(1)}, bf16[2,8,1024]{2,1,0:T(8,128)(2,1)S(1)}, u32[]{:S(2)}, u32[]{:S(2)}) collective-permute-start(bf16[2,8,1024]{2,1,0:T(8,128)(2,1)S(1)} %pad_maximum_fusion.refs_0_), channel_id=1, source_target_pairs={{0,4},{2,6},{4,0},{6,2},{1,5},{3,7},{5,1},{7,3},{8,12},{10,14},{12... | collective-permute-start | bytes 98312 | tf_op jit(solution)/shard_map/ppermute | solution.py:492
  7.1 5.7 %collective-permute-start.1 = (bf16[2,8,1024]{2,1,0:T(8,128)(2,1)S(1)}, bf16[2,8,1024]{2,1,0:T(8,128)(2,1)S(1)}, u32[]{:S(2)}, u32[]{:S(2)}) collective-permute-start(bf16[2,8,1024]{2,1,0:T(8,128)(2,1)S(1)} %pad_maximum_fusion.refs_0_), channel_id=1, source_target_pairs={{0,2},{2,4},{4,6},{6,0},{1,3},{3,5},{5,7},{7,1},{8,10},{10,12},{12... | collective-permute-start | bytes 98312 | tf_op jit(solution)/shard_map/ppermute | solution.py:492
  14.3 1.3 %collective-permute-start.4 = (bf16[4,8,768]{2,1,0:T(8,128)(2,1)S(1)}, bf16[4,8,768]{2,1,0:T(8,128)(2,1)S(1)}, u32[]{:S(2)}, u32[]{:S(2)}) collective-permute-start(bf16[4,8,768]{2,1,0:T(8,128)(2,1)S(1)} %get-tuple-element.33), channel_id=1, source_target_pairs={{0,1},{1,0},{2,3},{3,2},{4,5},{5,4},{6,7},{7,6},{8,9},{9,8},{10,11... | collective-permute-start | bytes 147464 | tf_op jit(solution)/shard_map/ppermute | solution.py:589
  15.8 7.1 %collective-permute-start.5 = (bf16[8,768]{1,0:T(8,128)(2,1)S(1)}, bf16[8,768]{1,0:T(8,128)(2,1)S(1)}, u32[]{:S(2)}, u32[]{:S(2)}) collective-permute-start(bf16[8,768]{1,0:T(8,128)(2,1)S(1)} %get-tuple-element.35), channel_id=1, source_target_pairs={{0,6},{2,0},{4,2},{6,4},{1,7},{3,1},{5,3},{7,5},{8,14},{10,8},{12,... | collective-permute-start | bytes 36872 | tf_op jit(solution)/shard_map/ppermute | solution.py:604
  16.4 6.5 %collective-permute-start.6 = (bf16[8,768]{1,0:T(8,128)(2,1)S(1)}, bf16[8,768]{1,0:T(8,128)(2,1)S(1)}, u32[]{:S(2)}, u32[]{:S(2)}) collective-permute-start(bf16[8,768]{1,0:T(8,128)(2,1)S(1)} %get-tuple-element.36), channel_id=1, source_target_pairs={{0,4},{2,6},{4,0},{6,2},{1,5},{3,7},{5,1},{7,3},{8,12},{10,14},{12... | collective-permute-start | bytes 36872 | tf_op jit(solution)/shard_map/ppermute | solution.py:604
  17.4 5.5 %collective-permute-start.7 = (bf16[8,768]{1,0:T(8,128)(2,1)S(1)}, bf16[8,768]{1,0:T(8,128)(2,1)S(1)}, u32[]{:S(2)}, u32[]{:S(2)}) collective-permute-start(bf16[8,768]{1,0:T(8,128)(2,1)S(1)} %get-tuple-element.37), channel_id=1, source_target_pairs={{0,2},{2,4},{4,6},{6,0},{1,3},{3,5},{5,7},{7,1},{8,10},{10,12},{12... | collective-permute-start | bytes 36872 | tf_op jit(solution)/shard_map/ppermute | solution.py:604
  36.4 1.6 %collective-permute-start.8 = (bf16[16,8,640]{2,1,0:T(8,128)(2,1)S(1)}, bf16[16,8,640]{2,1,0:T(8,128)(2,1)S(1)}, u32[]{:S(2)}, u32[]{:S(2)}) collective-permute-start(bf16[16,8,640]{2,1,0:T(8,128)(2,1)S(1)} %all_to_all.10.pieces_ref), channel_id=1, source_target_pairs={{0,1},{1,0},{2,3},{3,2},{4,5},{5,4},{6,7},{7,6},{8,9},{9,8},{10,11... | collective-permute-start | bytes 491528 | tf_op jit(solution)/shard_map/ppermute | solution.py:623
  51.7 1.6 %collective-permute-start.9 = (bf16[16,8,640]{2,1,0:T(8,128)(2,1)S(1)}, bf16[16,8,640]{2,1,0:T(8,128)(2,1)S(1)}, u32[]{:S(2)}, u32[]{:S(2)}) collective-permute-start(bf16[16,8,640]{2,1,0:T(8,128)(2,1)S(1)} %get-tuple-element.47), channel_id=1, source_target_pairs={{0,1},{1,0},{2,3},{3,2},{4,5},{5,4},{6,7},{7,6},{8,9},{9,8},{10,11... | collective-permute-start | bytes 491528 | tf_op jit(solution)/shard_map/ppermute | solution.py:676
